TPU v7x, 512 devices: a whole 4x4x16 slice. The times are simulated.
512 devices in a mesh: blk: 128 (over z, y, core), kv: 4 (over x).
Axes of the slice: x: 4, y: 4, z: 16, core: 2. Of those that a mesh axis runs over, the one named last changes fastest.
Arguments:
- queries: bfloat16 [2048, 64, 128], P('blk', 'kv'), may hold values from -9 to 9
- prefix_keys: bfloat16 [128, 1024, 8, 128], P('blk', None, 'kv'), may hold values from -6 to 6
- prefix_values: bfloat16 [128, 1024, 8, 128], P('blk', None, 'kv'), may hold values from -6 to 6
- suffix_keys: bfloat16 [2048, 128, 8, 128], P('blk', None, 'kv'), may hold values from -6 to 6
- suffix_values: bfloat16 [2048, 128, 8, 128], P('blk', None, 'kv'), may hold values from -6 to 6
- out_weight: bfloat16 [8192, 8192], P('kv', 'blk'), may hold values from -0.25 to 0.25
- prefix_lists: int32 [2048, 8], P('blk'), may hold values from 0 to 127, all different within a row; in each aligned block of 16 rows (0 to 15, 16 to 31, ...) at most 2 rows name the same one
- suffix_lengths: int32 [2048], P('blk'), may hold values from 1 to 128, 163840 in all
- block_place: int32 [128], replicated, may hold values from 0 to 127, each once
Outputs:
- layer_out: bfloat16 [2048, 8192], P(None, ('blk', 'kv'))
Inputs may be any that keep to these rules, and one draw needn't show every extreme that they name: `prefix_lists`: each row names 8 different blocks. Among the rows of one device no block is named more than 2 times, and in some device some block is named exactly 2 times. `suffix_lengths`: the largest is exactly 128. `block_place`: each stored position appears once.
All inputs are finite; a program needn't handle non-finite values. No bound on the sum of `suffix_lengths` on one device may be relied on, other than what follows from the above.
Results may differ from a plain program's by a relative error of at most 0.0058.
Values may be sent and summed in bfloat16 or wider, within the bound.
No kernel may reach another device: no remote copies, remote signals or barrier semaphores. Data moves between devices by JAX's collectives and lax.ppermute only.
A program may use at most 64 MiB of HBM per device.

v0:
```python
import jax
import jax.numpy as jnp
from jax import lax
from jax.sharding import PartitionSpec as P


def block_partials(arrived, block_keys, block_values):
    sources, items, q_heads, head_dim = arrived.shape
    kv_heads = block_keys.shape[1]
    group_size = q_heads // kv_heads
    grouped = arrived.reshape(sources * items, kv_heads, group_size, head_dim)
    mixed_list = []
    lse_list = []
    for head in range(kv_heads):
        scores = jnp.einsum(
            "rgd,ld->rgl", grouped[:, head], block_keys[:, head], preferred_element_type=jnp.float32
        ) * head_dim ** (-0.5)
        row_top = jnp.max(scores, axis=-1)
        exponent = jnp.exp(scores - row_top[..., None])
        row_total = jnp.sum(exponent, axis=-1)
        weights = exponent.astype(jnp.bfloat16)
        mixed_out = (
            jnp.einsum(
                "rgl,ld->rgd", weights, block_values[:, head], preferred_element_type=jnp.float32
            )
            / row_total[..., None]
        )
        mixed_list.append(mixed_out.astype(jnp.bfloat16))
        lse_list.append(row_top + jnp.log(row_total))
    mixed_all = jnp.stack(mixed_list, axis=1).reshape(sources, items, q_heads, head_dim)
    lse_all = jnp.stack(lse_list, axis=1).reshape(sources, items, q_heads)
    return (mixed_all, lse_all)


def return_partials(partials):
    return (
        lax.all_to_all(
            partials[0].astype(jnp.float32), "blk", split_axis=0, concat_axis=0, tiled=True
        ).astype(jnp.bfloat16),
        lax.all_to_all(partials[1], "blk", split_axis=0, concat_axis=0, tiled=True),
    )


def own_partials(queries, own_keys, own_values, lengths):
    req_rows, q_heads, head_dim = queries.shape
    kv_heads = own_keys.shape[2]
    grouped = queries.reshape(req_rows, kv_heads, q_heads // kv_heads, head_dim)
    scores = jnp.einsum(
        "rhgd,rlhd->rhgl", grouped, own_keys, preferred_element_type=jnp.float32
    ) * head_dim ** (-0.5)
    visible = jnp.arange(own_keys.shape[1])[None, None, None, :] < lengths[:, None, None, None]
    scores = jnp.where(visible, scores, jnp.float32(-1e30))
    row_top = jnp.max(scores, axis=-1)
    exponent = jnp.exp(scores - row_top[..., None])
    row_total = jnp.sum(exponent, axis=-1)
    weights = exponent.astype(jnp.bfloat16)
    mixed_out = (
        jnp.einsum("rhgl,rlhd->rhgd", weights, own_values, preferred_element_type=jnp.float32)
        / row_total[..., None]
    )
    return (
        mixed_out.reshape(req_rows, q_heads, head_dim),
        (row_top + jnp.log(row_total)).reshape(req_rows, q_heads),
    )


def on_device(
    queries,
    prefix_keys,
    prefix_values,
    suffix_keys,
    suffix_values,
    out_weight,
    prefix_lists,
    suffix_lengths,
    block_place,
):
    owners = lax.axis_size("blk")
    req_rows, q_heads, head_dim = queries.shape
    listing = prefix_lists.shape[1]
    capacity = min(req_rows, max(2, 2 * req_rows * listing // owners))
    pair_count = req_rows * listing
    earlier = (jnp.arange(pair_count)[:, None] > jnp.arange(pair_count)[None, :]).astype(
        jnp.float32
    )
    placed = (block_place[:, None] == jnp.arange(owners)[None, :]).astype(jnp.float32)
    listed = prefix_lists.reshape(pair_count)
    named_hot = (listed[:, None] == jnp.arange(owners)[None, :]).astype(jnp.float32)
    dest_hot = jnp.dot(named_hot, placed, precision=lax.Precision.HIGHEST)
    before = jnp.dot(earlier, dest_hot, precision=lax.Precision.HIGHEST)
    slot_rank = jnp.sum(before * dest_hot, axis=1)
    slot_hot = (slot_rank[:, None] == jnp.arange(capacity)[None, :]).astype(jnp.float32)
    select = (dest_hot[:, :, None] * slot_hot[:, None, :]).reshape(pair_count, owners * capacity)
    select_half = select.astype(jnp.bfloat16)
    block_keys = prefix_keys[0]
    block_values = prefix_values[0]
    pair_queries = jnp.repeat(queries.reshape(req_rows, q_heads * head_dim), listing, axis=0)
    outgoing = jnp.einsum(
        "ps,px->sx", select_half, pair_queries, preferred_element_type=jnp.float32
    )
    outgoing = outgoing.astype(jnp.bfloat16).reshape(owners, capacity, q_heads, head_dim)
    back_mixed, back_lse = return_partials(
        block_partials(
            lax.all_to_all(outgoing, "blk", split_axis=0, concat_axis=0, tiled=True),
            block_keys,
            block_values,
        )
    )
    pair_mixed = jnp.einsum(
        "ps,sx->px",
        select_half,
        back_mixed.reshape(owners * capacity, q_heads * head_dim),
        preferred_element_type=jnp.float32,
    )
    pair_mixed = pair_mixed.reshape(req_rows, listing, q_heads, head_dim)
    pair_lse = jnp.dot(
        select, back_lse.reshape(owners * capacity, q_heads), precision=lax.Precision.HIGHEST
    ).reshape(req_rows, listing, q_heads)
    own_out, own_lse = own_partials(queries, suffix_keys, suffix_values, suffix_lengths)
    every_out = jnp.concatenate([pair_mixed, own_out[:, None]], axis=1)
    every_lse = jnp.concatenate([pair_lse, own_lse[:, None]], axis=1)
    joint_top = jnp.max(every_lse, axis=1)
    scaled = jnp.exp(every_lse - joint_top[:, None])
    joined = jnp.sum(scaled[..., None] * every_out, axis=1) / jnp.sum(scaled, axis=1)[..., None]
    attended = joined.astype(jnp.bfloat16).reshape(req_rows, q_heads * head_dim)
    partial_terms = jnp.dot(
        lax.all_gather(attended, "blk", axis=0, tiled=True),
        out_weight,
        preferred_element_type=jnp.float32,
    )
    return lax.psum_scatter(partial_terms, "kv", scatter_dimension=1, tiled=True).astype(
        jnp.bfloat16
    )


def solution(mesh):
    placed = (
        P("blk", "kv", None),
        P("blk", None, "kv", None),
        P("blk", None, "kv", None),
        P("blk", None, "kv", None),
        P("blk", None, "kv", None),
        P("kv", "blk"),
        P("blk", None),
        P("blk"),
        P(),
    )
    return jax.shard_map(
        on_device, mesh=mesh, in_specs=placed, out_specs=P(None, ("blk", "kv")), check_vma=False
    )
```

profile of v0, /device:TPU:1, one launch (start us, length us, event | category | flops | bytes accessed | tf_op | source)
XLA Modules:
  0.0 369.2 jit_solution(4274681151658845572)
XLA Ops:
  10.1 1.2 copy.78
  11.3 20.6 %all-to-all-start = ((bf16[128,2,16,128]{3,2,1,0:T(8,128)(2,1)}), bf16[128,2,16,128]{3,2,1,0:T(8,128)(2,1)S(1)}, u32[]{:S(2)}, u32[]{:S(2)}) async-start(bf16[128,2,16,128]{3,2,1,0:T(8,128)(2,1)} %bitcast.38), calls=%async_computation | async-start | bytes 2097152 | tf_op jit(solution)/shard_map/all_to_all | solution.py:104
  34.1 49.6 %all-to-all-done = bf16[128,2,16,128]{3,2,1,0:T(8,128)(2,1)S(1)} async-done(((bf16[128,2,16,128]{3,2,1,0:T(8,128)(2,1)}), bf16[128,2,16,128]{3,2,1,0:T(8,128)(2,1)S(1)}, u32[]{:S(2)}, u32[]{:S(2)}) %all-to-all-start) | async-done | bytes 1048608 | tf_op jit(solution)/shard_map/all_to_all | solution.py:104
  84.7 1.3 multiply_reduce_fusion
  86.1 1.3 multiply_reduce_fusion.1
  87.4 1.8 fusion.3
  89.2 1.8 fusion.29
  91.0 1.8 fusion.1
  92.8 1.8 fusion.24
  95.7 10.2 %all-to-all-start.1 = ((f32[128,2,16]{2,1,0:T(2,128)}), f32[128,2,16]{2,1,0:T(2,128)S(1)}, u32[]{:S(2)}, u32[]{:S(2)}) async-start(f32[128,2,16]{2,1,0:T(2,128)} %reshape.222), calls=%async_computation.1 | async-start | bytes 262144 | tf_op jit(solution)/shard_map/all_to_all | solution.py:40
  106.0 2.2 copy.68
  108.2 13.7 %all-to-all-done.1 = f32[128,2,16]{2,1,0:T(2,128)S(1)} async-done(((f32[128,2,16]{2,1,0:T(2,128)}), f32[128,2,16]{2,1,0:T(2,128)S(1)}, u32[]{:S(2)}, u32[]{:S(2)}) %all-to-all-start.1) | async-done | bytes 16416 | tf_op jit(solution)/shard_map/all_to_all | solution.py:40
  121.9 7.7 %all-to-all-start.2 = ((bf16[128,2,16,128]{3,2,1,0:T(8,128)(2,1)}), bf16[128,2,16,128]{3,2,1,0:T(8,128)(2,1)}, u32[]{:S(2)}, u32[]{:S(2)}) async-start(bf16[128,2,16,128]{3,2,1,0:T(8,128)(2,1)} %copy.68), calls=%async_computation.2 | async-start | bytes 2097152 | tf_op jit(solution)/shard_map/all_to_all | solution.py:37
  129.6 2.2 convert_element_type.82
  134.3 2.3 convolution_divide_fusion
  136.6 3.5 fusion.52
  140.4 40.6 %all-to-all-done.2 = bf16[128,2,16,128]{3,2,1,0:T(8,128)(2,1)} async-done(((bf16[128,2,16,128]{3,2,1,0:T(8,128)(2,1)}), bf16[128,2,16,128]{3,2,1,0:T(8,128)(2,1)}, u32[]{:S(2)}, u32[]{:S(2)}) %all-to-all-start.2) | async-done | bytes 1048608 | tf_op jit(solution)/shard_map/all_to_all | solution.py:37
  181.1 1.5 copy.98
  183.1 3.5 fusion.18
  186.6 1.7 fusion.12
  189.2 142.5 %all-gather.2.cloned.1.call-done = bf16[2048,2048]{1,0:T(8,128)(2,1)} async-done(((bf16[16,2048]{1,0:T(8,128)(2,1)}), bf16[2048,2048]{1,0:T(8,128)(2,1)}) %all-gather.2.cloned.1.call-update) | async-done | bytes 8388624 | tf_op jit(solution)/shard_map/all_gather | solution.py:127
  331.7 6.9 %fusion.53 = f32[2048,64]{0,1:T(8,128)} fusion(bf16[2048,2048]{1,0:T(8,128)(2,1)} %all-gather.2.cloned.1.call-done, bf16[2048,64]{0,1:T(8,128)(2,1)} %param.14), kind=kOutput, calls=%fused_computation.79 | convolution fusion | flops 536870912 | bytes 9175040 | tf_op jit(solution)/shard_map/dot_general | solution.py:126
  338.7 22.2 %reduce-scatter.2.cloned.1.call-done = f32[2048,16]{0,1:T(8,128)} async-done(((f32[2048,64]{0,1:T(8,128)}), f32[2048,16]{0,1:T(8,128)}) %reduce-scatter.2.cloned.1.call-update) | async-done | bytes 131088 | tf_op jit(solution)/shard_map/reduce_scatter | solution.py:131
  360.8 1.5 convert_element_type.93
  (42 shorter events, 12.1 us)
Async XLA Ops:
  6.5 126.5 %copy-start = (bf16[16,128,2,128]{3,2,1,0:T(2,128)(2,1)S(1)}, bf16[16,128,2,128]{3,2,1,0:T(2,128)(2,1)}, u32[]{:S(2)}) copy-start(bf16[16,128,2,128]{3,2,1,0:T(2,128)(2,1)} %param.12) | copy-start | bytes 3145732
  11.3 72.4 %all-to-all-start = ((bf16[128,2,16,128]{3,2,1,0:T(8,128)(2,1)}), bf16[128,2,16,128]{3,2,1,0:T(8,128)(2,1)S(1)}, u32[]{:S(2)}, u32[]{:S(2)}) async-start(bf16[128,2,16,128]{3,2,1,0:T(8,128)(2,1)} %bitcast.38), calls=%async_computation | async-start | bytes 2097152 | tf_op jit(solution)/shard_map/all_to_all | solution.py:104
  94.5 38.4 %copy-start.2 = (s32[16]{0:T(128)S(1)}, s32[16]{0:T(128)}, u32[]{:S(2)}) copy-start(s32[16]{0:T(128)} %param.16) | copy-start | bytes 196
  94.6 38.5 %copy-start.1 = (bf16[16,16,128]{2,1,0:T(8,128)(2,1)S(1)}, bf16[16,16,128]{2,1,0:T(8,128)(2,1)}, u32[]{:S(2)}) copy-start(bf16[16,16,128]{2,1,0:T(8,128)(2,1)} %param.9) | copy-start | bytes 196612
  95.7 26.2 %all-to-all-start.1 = ((f32[128,2,16]{2,1,0:T(2,128)}), f32[128,2,16]{2,1,0:T(2,128)S(1)}, u32[]{:S(2)}, u32[]{:S(2)}) async-start(f32[128,2,16]{2,1,0:T(2,128)} %reshape.222), calls=%async_computation.1 | async-start | bytes 262144 | tf_op jit(solution)/shard_map/all_to_all | solution.py:40
  121.9 59.2 %all-to-all-start.2 = ((bf16[128,2,16,128]{3,2,1,0:T(8,128)(2,1)}), bf16[128,2,16,128]{3,2,1,0:T(8,128)(2,1)}, u32[]{:S(2)}, u32[]{:S(2)}) async-start(bf16[128,2,16,128]{3,2,1,0:T(8,128)(2,1)} %copy.68), calls=%async_computation.2 | async-start | bytes 2097152 | tf_op jit(solution)/shard_map/all_to_all | solution.py:37
  129.6 202.2 %all-gather.2.cloned.1.call-start = ((), (), s32[]{:S(2)}) async-start(), calls=%async_computation.4 | async-start | bytes 8454144 | tf_op jit(solution)/shard_map/all_gather | solution.py:127
  189.2 171.6 %reduce-scatter.2.cloned.1.call-start = ((), (), s32[]{:S(2)}) async-start(), calls=%async_computation.5 | async-start | bytes 655360 | tf_op jit(solution)/shard_map/reduce_scatter | solution.py:131
Sparse Core Ops, SparseCore 0:
  189.3 142.3 all-gather.1
  338.8 22.0 reduce-scatter.1
where the time goes:
time: 371 us; the launch traced here: 369 us
  waiting for transfers between devices  269 us (73%)
  starting transfers between devices  38.5 us (10%)
  matrix products  24.8 us (7%)
  local copies, waits for them, and re-layouts  16 us (4%)
  between operations  13.6 us (4%)
  other arithmetic  7.58 us (2%)
    all_gather x1, waiting for transfers between devices, on_device(): lax.all_gather(attended, 'blk', axis=0, tiled=True)  143 us
    all_to_all x1, waiting for transfers between devices, on_device(): lax.all_to_all(outgoing, 'blk', split_axis=0, concat_axis=0, tiled=True)  49.6 us
    all_to_all x1, waiting for transfers between devices, return_partials(): lax.all_to_all(partials[0].astype(jnp.float32), 'blk', split_axis=0, conc...  40.6 us
    reduce_scatter x1, waiting for transfers between devices, on_device(): lax.psum_scatter(partial_terms, 'kv', scatter_dimension=1, tiled=True)  22.2 us
    all_to_all x1, starting transfers between devices, on_device(): lax.all_to_all(outgoing, 'blk', split_axis=0, concat_axis=0, tiled=True)  20.6 us
    all_to_all x1, waiting for transfers between devices, return_partials(): lax.all_to_all(partials[1], 'blk', split_axis=0, concat_axis=0, tiled=True)  13.7 us
    all_to_all x1, starting transfers between devices, return_partials(): lax.all_to_all(partials[1], 'blk', split_axis=0, concat_axis=0, tiled=True)  10.2 us
    all_to_all x1, starting transfers between devices, return_partials(): lax.all_to_all(partials[0].astype(jnp.float32), 'blk', split_axis=0, conc...  7.66 us
  transfers between devices with their start and end apart: 5, of which 5 were waited for; matrix products, arithmetic and copies ran while one was open for 4% of the time, Pallas kernels for 0%

commit v1 on v0

v1 whole, which is shorter than its diff:
```python
import jax
import jax.numpy as jnp
from jax import lax
from jax.experimental import pallas as pl
from jax.experimental.pallas import tpu as pltpu
from jax.sharding import Mesh, PartitionSpec as P

ZS, YS, CS, XS = 16, 4, 2, 4
PLANE = YS * CS
ROWS = 16
HEADS = 16
HD = 128
WIDE = HEADS * HD
PACK = WIDE + 128
POOL = ZS * ROWS
SLOTS = POOL
CAP = SLOTS // PLANE
TOKENS = 1024
FAR = -1e30
SCALE = HD ** -0.5
LOG2E = 1.4426950408889634
PARAMS = pltpu.CompilerParams(vmem_limit_bytes=40 * 1024 * 1024)


def lanes(shape):
    return lax.broadcasted_iota(jnp.int32, shape, len(shape) - 1)


def split_parts(value):
    high = value.astype(jnp.bfloat16).astype(jnp.float32)
    rest = value - high
    middle = rest.astype(jnp.bfloat16).astype(jnp.float32)
    low = (rest - middle).astype(jnp.bfloat16).astype(jnp.float32)
    return high + pltpu.roll(middle, 16, 1) + pltpu.roll(low, 32, 1)


def join_parts(packed):
    whole = packed + pltpu.roll(packed, 112, 1) + pltpu.roll(packed, 96, 1)
    return jnp.where(lanes(whole.shape) < HEADS, whole, 0.0)


def dispatch_kernel(logical_ref, pool_ref, out_ref, select_ref):
    listed = pool_ref[:, WIDE:].astype(jnp.float32)
    logical = logical_ref[0:1, :]
    hot = jnp.zeros((POOL, 128), jnp.float32)
    for item in range(8):
        hot = jnp.where(listed[:, item : item + 1] == logical, 1.0, hot)
    hot = hot.astype(jnp.bfloat16)
    row = lax.broadcasted_iota(jnp.int32, (POOL, POOL), 0)
    column = lax.broadcasted_iota(jnp.int32, (POOL, POOL), 1)
    earlier = jnp.where(row > column, 1.0, 0.0).astype(jnp.bfloat16)
    rank = jnp.dot(earlier, hot, preferred_element_type=jnp.float32).astype(jnp.bfloat16)
    owner = lax.broadcasted_iota(jnp.int32, (128, SLOTS), 0)
    slot = lax.broadcasted_iota(jnp.int32, (128, SLOTS), 1)
    spread = jnp.where(slot // CAP == owner, 1.0, 0.0).astype(jnp.bfloat16)
    hot_at = jnp.dot(hot, spread, preferred_element_type=jnp.float32)
    rank_at = jnp.dot(rank, spread, preferred_element_type=jnp.float32)
    wanted = (lanes((POOL, SLOTS)) % CAP).astype(jnp.float32)
    select = jnp.where((hot_at > 0.5) & (rank_at == wanted), 1.0, 0.0).astype(jnp.bfloat16)
    select_ref[...] = select
    out_ref[...] = lax.dot_general(
        select, pool_ref[:, :WIDE], (((0,), (0,)), ((), ())), preferred_element_type=jnp.float32
    ).astype(jnp.bfloat16)


def attend_kernel(q_ref, k_ref, v_ref, out_ref):
    logs = jnp.zeros((SLOTS, 128), jnp.float32)
    lane = lanes((SLOTS, 128))
    for head in range(HEADS):
        group = slice((head // 8) * HD, (head // 8 + 1) * HD)
        at = slice(head * HD, (head + 1) * HD)
        scores = lax.dot_general(
            q_ref[:, at], k_ref[:, group], (((1,), (1,)), ((), ())), preferred_element_type=jnp.float32
        )
        top = jnp.max(scores, axis=1, keepdims=True)
        grown = jnp.exp2((scores - top) * (SCALE * LOG2E))
        total = jnp.sum(grown, axis=1, keepdims=True)
        mixed = jnp.dot(
            grown.astype(jnp.bfloat16), v_ref[:, group], preferred_element_type=jnp.float32
        )
        out_ref[:, at] = (mixed / total).astype(jnp.bfloat16)
        logs = jnp.where(lane == head, top * SCALE + jnp.log(total), logs)
    flags = jnp.where((lane >= 48) & (lane < 64), 1.0, 0.0)
    out_ref[:, WIDE:] = (split_parts(logs) + flags).astype(jnp.bfloat16)


STAY, NEXT, BACK, NEXT2, BACK2 = (0, 4, 8, 12), (1, 5, 9, 13), (15, 3, 7, 11), (2, 6), (14, 10)


def gather_kernel(place_ref, back_ref, select_ref, *refs):
    outs, joined_ref = refs[:-1], refs[-1]
    select = select_ref[...]
    packed = back_ref[:, WIDE:]
    lane = lanes((POOL, 128))
    slot = lanes((POOL, SLOTS))
    tops = []
    hots = []
    for block in range(PLANE):
        part = jnp.where(slot // CAP == block, select, jnp.zeros_like(select))
        found = jnp.dot(part, packed, preferred_element_type=jnp.float32)
        hot = pltpu.roll(found, 80, 1)
        hot = (hot > 0.5) & (lane < HEADS)
        tops.append(jnp.where(hot, join_parts(found), FAR))
        hots.append(hot)
    top = tops[0]
    for other in tops[1:]:
        top = jnp.maximum(top, other)
    total = jnp.zeros((POOL, 128), jnp.float32)
    for log, hot in zip(tops, hots):
        total = total + jnp.where(hot, jnp.exp(log - top), 0.0)
    whole = jnp.where(lane < HEADS, top + jnp.log(jnp.maximum(total, 1.0)), 0.0)
    whole_parts = split_parts(whole).astype(jnp.bfloat16)
    at_slot = lax.dot_general(
        select, whole_parts, (((0,), (0,)), ((), ())), preferred_element_type=jnp.float32
    )
    weight = jnp.exp(join_parts(packed.astype(jnp.float32)) - join_parts(at_slot))
    for head in range(HEADS):
        at = slice(head * HD, (head + 1) * HD)
        scaled = weight[:, head : head + 1] * back_ref[:, at].astype(jnp.float32)
        high = scaled.astype(jnp.bfloat16)
        low = (scaled - high.astype(jnp.float32)).astype(jnp.bfloat16)
        joined_ref[:, at] = (
            jnp.dot(select, high, preferred_element_type=jnp.float32)
            + jnp.dot(select, low, preferred_element_type=jnp.float32)
        ).astype(jnp.bfloat16)
    joined_ref[:, WIDE:] = whole_parts
    place = place_ref[0]
    for out_ref, distances in zip(outs, (STAY, NEXT, BACK, NEXT2, BACK2)):
        for index, distance in enumerate(distances):
            block = lax.rem(place + distance, ZS)
            start = pl.multiple_of(block * ROWS, ROWS)
            out_ref[index * ROWS : (index + 1) * ROWS, :] = joined_ref[pl.ds(start, ROWS), :]


def merge(terms):
    top = terms[0][1]
    for _, log in terms[1:]:
        top = jnp.maximum(top, log)
    lane = lanes((ROWS, 128))
    weights = [jnp.exp(log - top) for _, log in terms]
    total = weights[0]
    for weight in weights[1:]:
        total = total + weight
    columns = []
    for head in range(HEADS):
        at = slice(head * HD, (head + 1) * HD)
        row = None
        for (rows, _), weight in zip(terms, weights):
            term = weight[:, head : head + 1] * rows(at)
            row = term if row is None else row + term
        columns.append(row / total[:, head : head + 1])
    return columns, jnp.where(lane < HEADS, top + jnp.log(total), 0.0)


def packed_term(ref, index):
    rows = slice(index * ROWS, (index + 1) * ROWS)
    return (
        lambda at: ref[rows, at].astype(jnp.float32),
        join_parts(ref[rows, WIDE:].astype(jnp.float32)),
    )


def middle_kernel(stay_ref, next_ref, back_ref, next2_ref, back2_ref, *outs):
    for quarter, out_ref in enumerate(outs):
        terms = [packed_term(stay_ref, quarter), packed_term(next_ref, quarter), packed_term(back_ref, quarter)]
        if quarter < 2:
            terms.append(packed_term(next2_ref, quarter))
        if quarter in (0, 3):
            terms.append(packed_term(back2_ref, 0 if quarter == 0 else 1))
        columns, log = merge(terms)
        for head in range(HEADS):
            out_ref[:, head * HD : (head + 1) * HD] = columns[head].astype(jnp.bfloat16)
        out_ref[:, WIDE:] = split_parts(log).astype(jnp.bfloat16)


def final_kernel(a_ref, b_ref, c_ref, d_ref, own_ref, own_log_ref, out_ref):
    terms = [packed_term(ref, 0) for ref in (a_ref, b_ref, c_ref, d_ref)]
    terms.append((lambda at: own_ref[:, at], own_log_ref[...]))
    columns, _ = merge(terms)
    for head in range(HEADS):
        out_ref[:, head * HD : (head + 1) * HD] = columns[head].astype(jnp.bfloat16)


def own_partials(queries, own_keys, own_values, lengths):
    req_rows, q_heads, head_dim = queries.shape
    kv_heads = own_keys.shape[2]
    grouped = queries.reshape(req_rows, kv_heads, q_heads // kv_heads, head_dim)
    scores = jnp.einsum(
        "rhgd,rlhd->rhgl", grouped, own_keys, preferred_element_type=jnp.float32
    ) * head_dim ** (-0.5)
    visible = jnp.arange(own_keys.shape[1])[None, None, None, :] < lengths[:, None, None, None]
    scores = jnp.where(visible, scores, jnp.float32(-1e30))
    row_top = jnp.max(scores, axis=-1)
    exponent = jnp.exp(scores - row_top[..., None])
    row_total = jnp.sum(exponent, axis=-1)
    weights = exponent.astype(jnp.bfloat16)
    mixed_out = (
        jnp.einsum("rhgl,rlhd->rhgd", weights, own_values, preferred_element_type=jnp.float32)
        / row_total[..., None]
    )
    return (
        mixed_out.reshape(req_rows, q_heads * head_dim),
        (row_top + jnp.log(row_total)).reshape(req_rows, q_heads),
    )


def packed(rows):
    return jax.ShapeDtypeStruct((rows, PACK), jnp.bfloat16)


def shifted(value, distance):
    return lax.ppermute(value, "z", [(place, (place + distance) % ZS) for place in range(ZS)])


def on_device(
    queries,
    prefix_keys,
    prefix_values,
    suffix_keys,
    suffix_values,
    out_weight,
    prefix_lists,
    suffix_lengths,
    block_place,
):
    place = lax.axis_index("z")
    flat_queries = queries.reshape(ROWS, WIDE)
    listed = jnp.pad(prefix_lists.astype(jnp.bfloat16), ((0, 0), (0, 120)))
    pool = lax.all_gather(
        jnp.concatenate([flat_queries, listed], axis=1), "z", axis=0, tiled=True
    )

    stored = place * PLANE + jnp.arange(128)
    here = (block_place[None, :] == stored[:, None]) & (jnp.arange(128) < PLANE)[:, None]
    logical = jnp.sum(jnp.where(here, jnp.arange(128)[None, :], 0), axis=1)
    logical = jnp.where(jnp.arange(128) < PLANE, logical, -1).astype(jnp.float32)

    outgoing, select = pl.pallas_call(
        dispatch_kernel,
        out_shape=(
            jax.ShapeDtypeStruct((SLOTS, WIDE), jnp.bfloat16),
            jax.ShapeDtypeStruct((POOL, SLOTS), jnp.bfloat16),
        ),
        compiler_params=PARAMS,
        name="dispatch",
    )(jnp.broadcast_to(logical[None], (8, 128)), pool)

    turned, pool_seen = lax.optimization_barrier((out_weight.T, pool))
    plane_weight = lax.all_gather(turned, ("y", "c"), axis=0, tiled=True)

    arrived = lax.all_to_all(outgoing, ("y", "c"), split_axis=0, concat_axis=0, tiled=True)
    partials = pl.pallas_call(
        attend_kernel, out_shape=packed(SLOTS), compiler_params=PARAMS, name="attend"
    )(
        arrived,
        prefix_keys.reshape(TOKENS, 2 * HD),
        prefix_values.reshape(TOKENS, 2 * HD),
    )
    back = lax.all_to_all(partials, ("y", "c"), split_axis=0, concat_axis=0, tiled=True)
    stay, near, rear, near2, rear2 = pl.pallas_call(
        gather_kernel,
        in_specs=[
            pl.BlockSpec(memory_space=pltpu.SMEM),
            pl.BlockSpec(memory_space=pltpu.VMEM),
            pl.BlockSpec(memory_space=pltpu.VMEM),
        ],
        out_shape=(packed(64), packed(64), packed(64), packed(32), packed(32)),
        scratch_shapes=[pltpu.VMEM((POOL, PACK), jnp.bfloat16)],
        compiler_params=PARAMS,
        name="gather",
    )(place.reshape(1).astype(jnp.int32), back, select)
    near, rear = shifted(near, 1), shifted(rear, -1)
    near2, rear2 = shifted(near2, 2), shifted(rear2, -2)
    kept, plus4, plus8, minus4 = pl.pallas_call(
        middle_kernel,
        out_shape=(packed(ROWS),) * 4,
        compiler_params=PARAMS,
        name="middle",
    )(stay, near, rear, near2, rear2)
    plus4, minus4, plus8 = shifted(plus4, 4), shifted(minus4, -4), shifted(plus8, 8)

    own_out, own_log = own_partials(queries, suffix_keys, suffix_values, suffix_lengths)
    attended = pl.pallas_call(
        final_kernel,
        out_shape=jax.ShapeDtypeStruct((ROWS, WIDE), jnp.bfloat16),
        compiler_params=PARAMS,
        name="final",
    )(kept, plus4, plus8, minus4, own_out, jnp.pad(own_log, ((0, 0), (0, 112))))

    rows = lax.all_gather(attended, "z", axis=0, tiled=True)
    terms = lax.dot_general(
        plane_weight, rows, (((1,), (1,)), ((), ())), preferred_element_type=jnp.float32
    )
    terms = lax.all_to_all(
        terms.reshape(PLANE * XS, 16, POOL),
        ("y", "c", "kv"),
        split_axis=0,
        concat_axis=0,
        tiled=True,
    )
    summed = jnp.sum(terms.reshape(PLANE, XS, 16, ZS, ROWS), axis=1).astype(jnp.bfloat16)
    return summed.transpose(2, 0, 3, 1).reshape(ZS * PLANE * ROWS, 16)


def solution(mesh):
    blk = ("z", "y", "c")
    fine = Mesh(mesh.devices.reshape(ZS, YS, CS, XS), blk + ("kv",))
    placed = (
        P(blk, "kv", None),
        P(blk, None, "kv", None),
        P(blk, None, "kv", None),
        P(blk, None, "kv", None),
        P(blk, None, "kv", None),
        P("kv", blk),
        P(blk, None),
        P(blk),
        P(),
    )
    return jax.shard_map(
        on_device, mesh=fine, in_specs=placed, out_specs=P(None, blk + ("kv",)), check_vma=False
    )
```

time: 371 us -> 299 us (0.81)
  waiting for transfers between devices: 269 us -> 171 us
  blocking collectives: 0 us -> 28.2 us
  matrix products: 24.8 us -> 5.63 us
  Pallas kernels: 0 us -> 17 us
  starting transfers between devices: 38.5 us -> 48.1 us
  local copies, waits for them, and re-layouts: 16 us -> 8.98 us
    all_to_all x3 -> x2, waiting for transfers between devices: 104 us -> 31.5 us  [the longest x1 17.1 us: on_device(): lax.all_to_all(outgoing, ('y', 'c'), split_axis=0, concat_axis=0, tiled=T...]
    ppermute x0 -> x7, starting transfers between devices: none -> 28.3 us  [shifted(): lax.ppermute(value, 'z', [(place, (place + distance) % ZS) for place in r...]
    all_to_all x0 -> x1, blocking collectives: none -> 28.2 us  [on_device(): lax.all_to_all(terms.reshape(PLANE * XS, 16, POOL), ('y', 'c', 'kv'), spl...]
    reduce_scatter x1 -> x0, waiting for transfers between devices: 22.2 us -> none  [on_device(): lax.psum_scatter(partial_terms, 'kv', scatter_dimension=1, tiled=True)]
    dot_general x10 -> x1, matrix products: 21.8 us -> 2.59 us  [on_device(): lax.dot_general(plane_weight, rows, (((1,), (1,)), ((), ())), preferred_e...]
    all_to_all x3 -> x2, starting transfers between devices: 38.4 us -> 19.8 us  [the longest x1 14.5 us: on_device(): lax.all_to_all(outgoing, ('y', 'c'), split_axis=0, concat_axis=0, tiled=T...]
    all_gather x1 -> x3, waiting for transfers between devices: 143 us -> 125 us  [the longest x1 67.6 us: on_device(): lax.all_gather(jnp.concatenate([flat_queries, listed], axis=1), 'z', axis...]
    pallas_call x0 -> x5, Pallas kernels: none -> 17 us  [the longest x1 9.22 us: on_device(): pl.pallas_call(attend_kernel, out_shape=packed(SLOTS), compiler_params=PA...]
  transfers between devices with their start and end apart: 5 -> 12, of which waited for: 5 -> 8; matrix products, arithmetic and copies ran while one was open for 4% -> 2% of each run, Pallas kernels for 0% -> 6%
where the time goes in v1:
time: 299 us; the launch traced here: 298 us
  waiting for transfers between devices  171 us (57%)
  starting transfers between devices  48.1 us (16%)
  blocking collectives  28.2 us (9%)
  Pallas kernels  17 us (6%)
  between operations  13.3 us (4%)
  local copies, waits for them, and re-layouts  8.98 us (3%)
  other arithmetic  5.87 us (2%)
  matrix products  5.63 us (2%)
    all_gather x1, waiting for transfers between devices, on_device(): lax.all_gather(jnp.concatenate([flat_queries, listed], axis=1), 'z', axis...  67.6 us
    all_gather x1, waiting for transfers between devices, on_device(): rows = lax.all_gather(attended, 'z', axis=0, tiled=True)  57.3 us
    ppermute x7, starting transfers between devices, shifted(): lax.ppermute(value, 'z', [(place, (place + distance) % ZS) for place in r...  28.3 us
    all_to_all x1, blocking collectives, on_device(): lax.all_to_all(terms.reshape(PLANE * XS, 16, POOL), ('y', 'c', 'kv'), spl...  28.2 us
    all_to_all x1, waiting for transfers between devices, on_device(): lax.all_to_all(outgoing, ('y', 'c'), split_axis=0, concat_axis=0, tiled=T...  17.1 us
    all_to_all x1, starting transfers between devices, on_device(): lax.all_to_all(outgoing, ('y', 'c'), split_axis=0, concat_axis=0, tiled=T...  14.5 us
    ppermute x7, waiting for transfers between devices, shifted(): lax.ppermute(value, 'z', [(place, (place + distance) % ZS) for place in r...  14.5 us
    all_to_all x1, waiting for transfers between devices, on_device(): lax.all_to_all(partials, ('y', 'c'), split_axis=0, concat_axis=0, tiled=T...  14.4 us
  transfers between devices with their start and end apart: 12, of which 8 were waited for; matrix products, arithmetic and copies ran while one was open for 2% of the time, Pallas kernels for 6%

profile of v1, /device:TPU:1, one launch (start us, length us, event | category | flops | bytes accessed | tf_op | source)
XLA Modules:
  0.0 297.9 jit_solution(14337118739005880711)
XLA Ops:
  9.0 67.6 %all-gather.4.cloned.1.call-done.pool_ref = bf16[256,2176]{1,0:T(8,128)(2,1)} async-done(((bf16[16,2176]{1,0:T(8,128)(2,1)}), bf16[256,2176]{1,0:T(8,128)(2,1)}) %all-gather.4.cloned.1.call-update) | async-done | bytes 1114128 | tf_op jit(solution)/shard_map/all_gather | solution.py:229
  78.7 2.0 dispatch.1
  80.7 14.5 %all-to-all-start = ((bf16[8,32,2048]{2,1,0:T(8,128)(2,1)}), bf16[8,32,2048]{2,1,0:T(8,128)(2,1)S(1)}, u32[]{:S(2)}, u32[]{:S(2)}) async-start(bf16[8,32,2048]{2,1,0:T(8,128)(2,1)} %bitcast.2), calls=%async_computation | async-start | bytes 2097152 | tf_op jit(solution)/shard_map/all_to_all | solution.py:251
  96.6 17.1 %all-to-all-done = bf16[8,32,2048]{2,1,0:T(8,128)(2,1)S(1)} async-done(((bf16[8,32,2048]{2,1,0:T(8,128)(2,1)}), bf16[8,32,2048]{2,1,0:T(8,128)(2,1)S(1)}, u32[]{:S(2)}, u32[]{:S(2)}) %all-to-all-start) | async-done | bytes 1048608 | tf_op jit(solution)/shard_map/all_to_all | solution.py:251
  113.8 9.2 %attend.1 = bf16[256,2176]{1,0:T(8,128)(2,1)} custom-call(bf16[256,2048]{1,0:T(8,128)(2,1)S(1)} %bitcast.41, bf16[1024,256]{1,0:T(8,128)(2,1)S(1)} %get-tuple-element.32.k_ref, bf16[1024,256]{1,0:T(8,128)(2,1)S(1)} %get-tuple-element.31.v_ref), custom_call_target="tpu_custom_call" | custom-call | tf_op jit(solution)/shard_map/attend/pallas_call | solution.py:252
  123.0 5.3 %all-to-all-start.1 = ((bf16[8,32,2176]{2,1,0:T(8,128)(2,1)}), bf16[8,32,2176]{2,1,0:T(8,128)(2,1)S(1)}, u32[]{:S(2)}, u32[]{:S(2)}) async-start(bf16[8,32,2176]{2,1,0:T(8,128)(2,1)} %bitcast.4), calls=%async_computation.1 | async-start | bytes 2228224 | tf_op jit(solution)/shard_map/all_to_all | solution.py:259
  129.7 14.4 %all-to-all-done.1 = bf16[8,32,2176]{2,1,0:T(8,128)(2,1)S(1)} async-done(((bf16[8,32,2176]{2,1,0:T(8,128)(2,1)}), bf16[8,32,2176]{2,1,0:T(8,128)(2,1)S(1)}, u32[]{:S(2)}, u32[]{:S(2)}) %all-to-all-start.1) | async-done | bytes 1114144 | tf_op jit(solution)/shard_map/all_to_all | solution.py:259
  144.1 3.1 %gather.1 = (bf16[64,2176]{1,0:T(8,128)(2,1)S(1)}, bf16[64,2176]{1,0:T(8,128)(2,1)S(1)}, bf16[64,2176]{1,0:T(8,128)(2,1)S(1)}, bf16[32,2176]{1,0:T(8,128)(2,1)S(1)}, bf16[32,2176]{1,0:T(8,128)(2,1)S(1)}) custom-call(s32[1]{0:T(128)} %bitcast.1.place_ref, bf16[256,2176]{1,0:T(8,128)(2,1)S(1)} %bitcast.40, bf16[256,256]{1,0:T(8,128)(2,1)S(1)} %get-tuple-element.19.select_ref), custom_call_target="tpu_custom_call" | custom-call | tf_op jit(solution)/shard_map/gather/pallas_call | solution.py:260
  147.2 3.0 %collective-permute-start = (bf16[64,2176]{1,0:T(8,128)(2,1)S(1)}, bf16[64,2176]{1,0:T(8,128)(2,1)S(1)}, u32[]{:S(2)}, u32[]{:S(2)}) collective-permute-start(bf16[64,2176]{1,0:T(8,128)(2,1)S(1)} %get-tuple-element.21), channel_id=1, source_target_pairs={{0,32},{32,64},{64,96},{96,128},{128,160},{160,192},{192,224},{224... | collective-permute-start | bytes 835592 | tf_op jit(solution)/shard_map/ppermute | solution.py:212
  150.2 3.5 %collective-permute-start.1 = (bf16[64,2176]{1,0:T(8,128)(2,1)S(1)}, bf16[64,2176]{1,0:T(8,128)(2,1)S(1)}, u32[]{:S(2)}, u32[]{:S(2)}) collective-permute-start(bf16[64,2176]{1,0:T(8,128)(2,1)S(1)} %get-tuple-element.22), channel_id=1, source_target_pairs={{0,480},{32,0},{64,32},{96,64},{128,96},{160,128},{192,160},{224,1... | collective-permute-start | bytes 835592 | tf_op jit(solution)/shard_map/ppermute | solution.py:212
  155.5 1.9 collective-permute-start.2
  157.4 5.5 %collective-permute-start.3 = (bf16[32,2176]{1,0:T(8,128)(2,1)S(1)}, bf16[32,2176]{1,0:T(8,128)(2,1)S(1)}, u32[]{:S(2)}, u32[]{:S(2)}) collective-permute-start(bf16[32,2176]{1,0:T(8,128)(2,1)S(1)} %get-tuple-element.24), channel_id=1, source_target_pairs={{0,448},{32,480},{64,0},{96,32},{128,64},{160,96},{192,128},{224,1... | collective-permute-start | bytes 417800 | tf_op jit(solution)/shard_map/ppermute | solution.py:212
  162.9 1.7 convolution_divide_fusion
  164.6 2.7 collective-permute-done.2.next2_ref
  169.4 3.5 %collective-permute-start.4 = (bf16[16,2176]{1,0:T(8,128)(2,1)S(1)}, bf16[16,2176]{1,0:T(8,128)(2,1)S(1)}, u32[]{:S(2)}, u32[]{:S(2)}) collective-permute-start(bf16[16,2176]{1,0:T(8,128)(2,1)S(1)} %get-tuple-element.26), channel_id=1, source_target_pairs={{0,128},{32,160},{64,192},{96,224},{128,256},{160,288},{192,320},{... | collective-permute-start | bytes 208904 | tf_op jit(solution)/shard_map/ppermute | solution.py:212
  172.9 9.0 %collective-permute-start.5 = (bf16[16,2176]{1,0:T(8,128)(2,1)S(1)}, bf16[16,2176]{1,0:T(8,128)(2,1)S(1)}, u32[]{:S(2)}, u32[]{:S(2)}) collective-permute-start(bf16[16,2176]{1,0:T(8,128)(2,1)S(1)} %get-tuple-element.27), channel_id=1, source_target_pairs={{0,256},{32,288},{64,320},{96,352},{128,384},{160,416},{192,448},{... | collective-permute-start | bytes 208904 | tf_op jit(solution)/shard_map/ppermute | solution.py:212
  181.9 1.9 collective-permute-start.6
  184.0 2.8 collective-permute-done.5.c_ref
  186.8 8.5 %collective-permute-done.6.d_ref = bf16[16,2176]{1,0:T(8,128)(2,1)S(1)} collective-permute-done((bf16[16,2176]{1,0:T(8,128)(2,1)S(1)}, bf16[16,2176]{1,0:T(8,128)(2,1)S(1)}, u32[]{:S(2)}, u32[]{:S(2)}) %collective-permute-start.6) | collective-permute-done | bytes 69664 | tf_op jit(solution)/shard_map/ppermute | solution.py:212
  196.3 57.3 %all-gather.8.cloned.1.call-done = bf16[256,2048]{1,0:T(8,128)(2,1)} async-done(((bf16[16,2048]{1,0:T(8,128)(2,1)}), bf16[256,2048]{1,0:T(8,128)(2,1)}) %all-gather.8.cloned.1.call-update) | async-done | bytes 1048592 | tf_op jit(solution)/shard_map/all_gather | solution.py:290
  253.6 2.6 fusion.11
  256.2 28.2 %all_to_all.27 = f32[32,16,256]{2,1,0:T(8,128)S(1)} all-to-all(f32[32,16,256]{2,1,0:T(8,128)S(1)} %bitcast.44), channel_id=1, replica_groups=mesh['z'=16,'y'=4,'c'=2,'kv'=4] {'y','c','kv'}, dimensions={0} | all-to-all | bytes 1048576 | tf_op jit(solution)/shard_map/all_to_all | solution.py:294
  284.4 2.6 reshape.83
  287.0 2.7 reduce_sum.29
  (42 shorter events, 14.2 us)
Async XLA Ops:
  6.5 121.8 %copy-start = (bf16[16,128,2,128]{3,2,1,0:T(2,128)(2,1)S(1)}, bf16[16,128,2,128]{3,2,1,0:T(2,128)(2,1)}, u32[]{:S(2)}) copy-start(bf16[16,128,2,128]{3,2,1,0:T(2,128)(2,1)} %param.12) | copy-start | bytes 3145732
  6.5 70.0 %all-gather.4.cloned.1.call-start = ((), (), s32[]{:S(2)}) async-start(), calls=%async_computation.3 | async-start | bytes 1183744 | tf_op jit(solution)/shard_map/all_gather | solution.py:229
  8.9 187.4 %all-gather.6.cloned.1.call-start = ((), (), s32[]{:S(2)}) async-start(), calls=%async_computation.4 | async-start | bytes 2359296 | tf_op jit(solution)/shard_map/all_gather | solution.py:249
  77.5 1.2 copy-start.1
  80.7 33.0 %all-to-all-start = ((bf16[8,32,2048]{2,1,0:T(8,128)(2,1)}), bf16[8,32,2048]{2,1,0:T(8,128)(2,1)S(1)}, u32[]{:S(2)}, u32[]{:S(2)}) async-start(bf16[8,32,2048]{2,1,0:T(8,128)(2,1)} %bitcast.2), calls=%async_computation | async-start | bytes 2097152 | tf_op jit(solution)/shard_map/all_to_all | solution.py:251
  113.8 14.5 %copy-start.3 = (s32[16]{0:T(128)S(1)}, s32[16]{0:T(128)}, u32[]{:S(2)}) copy-start(s32[16]{0:T(128)} %param.16) | copy-start | bytes 196
  113.8 14.6 %copy-start.2 = (bf16[16,16,128]{2,1,0:T(8,128)(2,1)S(1)}, bf16[16,16,128]{2,1,0:T(8,128)(2,1)}, u32[]{:S(2)}) copy-start(bf16[16,16,128]{2,1,0:T(8,128)(2,1)} %param.9) | copy-start | bytes 196612
  123.0 21.1 %all-to-all-start.1 = ((bf16[8,32,2176]{2,1,0:T(8,128)(2,1)}), bf16[8,32,2176]{2,1,0:T(8,128)(2,1)S(1)}, u32[]{:S(2)}, u32[]{:S(2)}) async-start(bf16[8,32,2176]{2,1,0:T(8,128)(2,1)} %bitcast.4), calls=%async_computation.1 | async-start | bytes 2228224 | tf_op jit(solution)/shard_map/all_to_all | solution.py:259
  128.3 125.3 %all-gather.8.cloned.1.call-start = ((), (), s32[]{:S(2)}) async-start(), calls=%async_computation.5 | async-start | bytes 1114112 | tf_op jit(solution)/shard_map/all_gather | solution.py:290
  147.2 20.6 %collective-permute-start = (bf16[64,2176]{1,0:T(8,128)(2,1)S(1)}, bf16[64,2176]{1,0:T(8,128)(2,1)S(1)}, u32[]{:S(2)}, u32[]{:S(2)}) collective-permute-start(bf16[64,2176]{1,0:T(8,128)(2,1)S(1)} %get-tuple-element.21), channel_id=1, source_target_pairs={{0,32},{32,64},{64,96},{96,128},{128,160},{160,192},{192,224},{224... | collective-permute-start | bytes 835592 | tf_op jit(solution)/shard_map/ppermute | solution.py:212
  150.2 17.6 %collective-permute-start.1 = (bf16[64,2176]{1,0:T(8,128)(2,1)S(1)}, bf16[64,2176]{1,0:T(8,128)(2,1)S(1)}, u32[]{:S(2)}, u32[]{:S(2)}) collective-permute-start(bf16[64,2176]{1,0:T(8,128)(2,1)S(1)} %get-tuple-element.22), channel_id=1, source_target_pairs={{0,480},{32,0},{64,32},{96,64},{128,96},{160,128},{192,160},{224,1... | collective-permute-start | bytes 835592 | tf_op jit(solution)/shard_map/ppermute | solution.py:212
  155.5 11.8 %collective-permute-start.2 = (bf16[32,2176]{1,0:T(8,128)(2,1)S(1)}, bf16[32,2176]{1,0:T(8,128)(2,1)S(1)}, u32[]{:S(2)}, u32[]{:S(2)}) collective-permute-start(bf16[32,2176]{1,0:T(8,128)(2,1)S(1)} %get-tuple-element.23), channel_id=1, source_target_pairs={{0,64},{32,96},{64,128},{96,160},{128,192},{160,224},{192,256},{22... | collective-permute-start | bytes 417800 | tf_op jit(solution)/shard_map/ppermute | solution.py:212
  157.4 10.4 %collective-permute-start.3 = (bf16[32,2176]{1,0:T(8,128)(2,1)S(1)}, bf16[32,2176]{1,0:T(8,128)(2,1)S(1)}, u32[]{:S(2)}, u32[]{:S(2)}) collective-permute-start(bf16[32,2176]{1,0:T(8,128)(2,1)S(1)} %get-tuple-element.24), channel_id=1, source_target_pairs={{0,448},{32,480},{64,0},{96,32},{128,64},{160,96},{192,128},{224,1... | collective-permute-start | bytes 417800 | tf_op jit(solution)/shard_map/ppermute | solution.py:212
  169.4 14.6 %collective-permute-start.4 = (bf16[16,2176]{1,0:T(8,128)(2,1)S(1)}, bf16[16,2176]{1,0:T(8,128)(2,1)S(1)}, u32[]{:S(2)}, u32[]{:S(2)}) collective-permute-start(bf16[16,2176]{1,0:T(8,128)(2,1)S(1)} %get-tuple-element.26), channel_id=1, source_target_pairs={{0,128},{32,160},{64,192},{96,224},{128,256},{160,288},{192,320},{... | collective-permute-start | bytes 208904 | tf_op jit(solution)/shard_map/ppermute | solution.py:212
  172.9 13.9 %collective-permute-start.5 = (bf16[16,2176]{1,0:T(8,128)(2,1)S(1)}, bf16[16,2176]{1,0:T(8,128)(2,1)S(1)}, u32[]{:S(2)}, u32[]{:S(2)}) collective-permute-start(bf16[16,2176]{1,0:T(8,128)(2,1)S(1)} %get-tuple-element.27), channel_id=1, source_target_pairs={{0,256},{32,288},{64,320},{96,352},{128,384},{160,416},{192,448},{... | collective-permute-start | bytes 208904 | tf_op jit(solution)/shard_map/ppermute | solution.py:212
  181.9 13.3 %collective-permute-start.6 = (bf16[16,2176]{1,0:T(8,128)(2,1)S(1)}, bf16[16,2176]{1,0:T(8,128)(2,1)S(1)}, u32[]{:S(2)}, u32[]{:S(2)}) collective-permute-start(bf16[16,2176]{1,0:T(8,128)(2,1)S(1)} %get-tuple-element.28), channel_id=1, source_target_pairs={{0,384},{32,416},{64,448},{96,480},{128,0},{160,32},{192,64},{224,... | collective-permute-start | bytes 208904 | tf_op jit(solution)/shard_map/ppermute | solution.py:212
Sparse Core Ops, SparseCore 0:
  9.4 67.0 all-gather.3
  78.7 42.2 all-gather.5
  196.4 57.1 all-gather.7

commit v2 on v1

v2 whole, which is shorter than its diff:
```python
import jax
import jax.numpy as jnp
from jax import lax
from jax.experimental import pallas as pl
from jax.experimental.pallas import tpu as pltpu
from jax.sharding import Mesh, PartitionSpec as P

ZH, ZP, ZQ, YS, CS, XS = 4, 2, 2, 4, 2, 4
QUAD = ZP * ZQ * YS * CS
GROUP = ZP * YS * CS
ROWS = 16
HEADS = 16
HD = 128
WIDE = HEADS * HD
PACK = WIDE + 128
POOL = ZH * ROWS
CAP = 2 * ZH
SLOTS = QUAD * CAP
TOKENS = 1024
FAR = -1e30
SCALE = HD ** -0.5
LOG2E = 1.4426950408889634
PARAMS = pltpu.CompilerParams(vmem_limit_bytes=40 * 1024 * 1024)


def lanes(shape):
    return lax.broadcasted_iota(jnp.int32, shape, len(shape) - 1)


def split_parts(value):
    high = value.astype(jnp.bfloat16).astype(jnp.float32)
    rest = value - high
    middle = rest.astype(jnp.bfloat16).astype(jnp.float32)
    low = (rest - middle).astype(jnp.bfloat16).astype(jnp.float32)
    return high + pltpu.roll(middle, 16, 1) + pltpu.roll(low, 32, 1)


def join_parts(packed):
    whole = packed + pltpu.roll(packed, 112, 1) + pltpu.roll(packed, 96, 1)
    return jnp.where(lanes(whole.shape) < HEADS, whole, 0.0)


def dispatch_kernel(logical_ref, pool_ref, out_ref, select_ref):
    listed = pool_ref[:, WIDE:].astype(jnp.float32)
    logical = logical_ref[0:1, :]
    hot = jnp.zeros((POOL, 128), jnp.float32)
    for item in range(8):
        hot = jnp.where(listed[:, item : item + 1] == logical, 1.0, hot)
    hot = hot.astype(jnp.bfloat16)
    row = lax.broadcasted_iota(jnp.int32, (POOL, POOL), 0)
    column = lax.broadcasted_iota(jnp.int32, (POOL, POOL), 1)
    earlier = jnp.where(row > column, 1.0, 0.0).astype(jnp.bfloat16)
    rank = jnp.dot(earlier, hot, preferred_element_type=jnp.float32).astype(jnp.bfloat16)
    owner = lax.broadcasted_iota(jnp.int32, (128, SLOTS), 0)
    slot = lax.broadcasted_iota(jnp.int32, (128, SLOTS), 1)
    spread = jnp.where(slot // CAP == owner, 1.0, 0.0).astype(jnp.bfloat16)
    hot_at = jnp.dot(hot, spread, preferred_element_type=jnp.float32)
    rank_at = jnp.dot(rank, spread, preferred_element_type=jnp.float32)
    wanted = (lanes((POOL, SLOTS)) % CAP).astype(jnp.float32)
    select = jnp.where((hot_at > 0.5) & (rank_at == wanted), 1.0, 0.0)
    select_ref[...] = select
    out_ref[...] = lax.dot_general(
        select.astype(jnp.bfloat16),
        pool_ref[:, :WIDE],
        (((0,), (0,)), ((), ())),
        preferred_element_type=jnp.float32,
    ).astype(jnp.bfloat16)


def attend_kernel(q_ref, k_ref, v_ref, weight_ref, out_ref):
    logs = jnp.zeros((SLOTS, 128), jnp.float32)
    lane = lanes((SLOTS, 128))
    for head in range(HEADS):
        group = slice((head // 8) * HD, (head // 8 + 1) * HD)
        at = slice(head * HD, (head + 1) * HD)
        scores = lax.dot_general(
            q_ref[:, at], k_ref[:, group], (((1,), (1,)), ((), ())), preferred_element_type=jnp.float32
        )
        top = jnp.max(scores, axis=1, keepdims=True)
        grown = jnp.exp2((scores - top) * (SCALE * LOG2E))
        total = jnp.sum(grown, axis=1, keepdims=True)
        mixed = jnp.dot(
            grown.astype(jnp.bfloat16), v_ref[:, group], preferred_element_type=jnp.float32
        )
        out_ref[:, at] = (mixed / total).astype(jnp.bfloat16)
        logs = jnp.where(lane == head, top * SCALE + jnp.log(total), logs)
    out_ref[:, WIDE:] = split_parts(logs).astype(jnp.bfloat16)


def gather_kernel(back_ref, select_ref, joined_ref):
    chosen = select_ref[...] > 0.5
    slot_logs = join_parts(back_ref[:, WIDE:].astype(jnp.float32)).T
    lane = lanes((POOL, 128))
    logs = jnp.zeros((POOL, 128), jnp.float32)
    for head in range(HEADS):
        at = slice(head * HD, (head + 1) * HD)
        log = jnp.where(chosen, slot_logs[head : head + 1, :], FAR)
        top = jnp.max(log, axis=1, keepdims=True)
        grown = jnp.where(chosen, jnp.exp(log - top), 0.0)
        total = jnp.maximum(jnp.sum(grown, axis=1, keepdims=True), 0.5)
        weight = grown / total
        high = weight.astype(jnp.bfloat16)
        low = (weight - high.astype(jnp.float32)).astype(jnp.bfloat16)
        mixed = jnp.dot(high, back_ref[:, at], preferred_element_type=jnp.float32)
        mixed = mixed + jnp.dot(low, back_ref[:, at], preferred_element_type=jnp.float32)
        joined_ref[:, at] = mixed.astype(jnp.bfloat16)
        logs = jnp.where(lane == head, top + jnp.log(total), logs)
    joined_ref[:, WIDE:] = split_parts(logs).astype(jnp.bfloat16)


def merge(terms):
    top = terms[0][1]
    for _, log in terms[1:]:
        top = jnp.maximum(top, log)
    lane = lanes((ROWS, 128))
    weights = [jnp.exp(log - top) for _, log in terms]
    total = weights[0]
    for weight in weights[1:]:
        total = total + weight
    columns = []
    for head in range(HEADS):
        at = slice(head * HD, (head + 1) * HD)
        row = None
        for (rows, _), weight in zip(terms, weights):
            term = weight[:, head : head + 1] * rows(at)
            row = term if row is None else row + term
        columns.append(row / total[:, head : head + 1])
    return columns, jnp.where(lane < HEADS, top + jnp.log(total), 0.0)


def packed_term(ref, index):
    rows = slice(index * ROWS, (index + 1) * ROWS)
    return (
        lambda at: ref[rows, at].astype(jnp.float32),
        join_parts(ref[rows, WIDE:].astype(jnp.float32)),
    )


def final_kernel(far_ref, own_ref, own_log_ref, out_ref):
    terms = [packed_term(far_ref, index) for index in range(ZH)]
    terms.append((lambda at: own_ref[:, at], own_log_ref[...]))
    columns, _ = merge(terms)
    for head in range(HEADS):
        out_ref[:, head * HD : (head + 1) * HD] = columns[head].astype(jnp.bfloat16)


def project_kernel(rows_ref, weight_ref, out_ref):
    terms = lax.dot_general(
        weight_ref[...], rows_ref[...], (((1,), (1,)), ((), ())), preferred_element_type=jnp.float32
    )
    owners = out_ref.shape[1]
    for owner in range(owners):
        for part in range(XS):
            first = (owner * XS + part) * 16
            out_ref[part, owner] = terms[first : first + 16, :]


def sum_kernel(place_ref, terms_ref, out_ref):
    place = place_ref[0]
    for owner in range(YS * CS):
        for half in range(ZP):
            index = owner * ZP + half
            term = terms_ref[0, index]
            for part in range(1, XS):
                term = term + terms_ref[part, index]
            side = place if half == 0 else 1 - place
            out_ref[side * (YS * CS) + owner] = term.astype(jnp.bfloat16)


def settle_kernel(place_ref, parts_ref, out_ref):
    place = place_ref[0]
    for group in range(GROUP):
        side, owner = divmod(group, YS * CS)
        turned = parts_ref[group].astype(jnp.float32).T.astype(jnp.bfloat16)
        for half in range(ZQ):
            near = place if half == 0 else 1 - place
            for far in range(ZH):
                start = ((far * ZP + side) * ZQ + near) * YS * CS + owner
                first = (half * ZH + far) * ROWS
                out_ref[pl.ds(pl.multiple_of(start * ROWS, ROWS), ROWS), :] = turned[
                    first : first + ROWS, :
                ]


def own_partials(queries, own_keys, own_values, lengths):
    req_rows, q_heads, head_dim = queries.shape
    kv_heads = own_keys.shape[2]
    grouped = queries.reshape(req_rows, kv_heads, q_heads // kv_heads, head_dim)
    scores = jnp.einsum(
        "rhgd,rlhd->rhgl", grouped, own_keys, preferred_element_type=jnp.float32
    ) * head_dim ** (-0.5)
    visible = jnp.arange(own_keys.shape[1])[None, None, None, :] < lengths[:, None, None, None]
    scores = jnp.where(visible, scores, jnp.float32(-1e30))
    row_top = jnp.max(scores, axis=-1)
    exponent = jnp.exp(scores - row_top[..., None])
    row_total = jnp.sum(exponent, axis=-1)
    weights = exponent.astype(jnp.bfloat16)
    mixed_out = (
        jnp.einsum("rhgl,rlhd->rhgd", weights, own_values, preferred_element_type=jnp.float32)
        / row_total[..., None]
    )
    return (
        mixed_out.reshape(req_rows, q_heads * head_dim),
        (row_top + jnp.log(row_total)).reshape(req_rows, q_heads),
    )


def packed(rows):
    return jax.ShapeDtypeStruct((rows, PACK), jnp.bfloat16)


def spread_along(value, axis, count):
    copies = jnp.broadcast_to(value[None], (count,) + value.shape)
    everyone = lax.all_to_all(copies, axis, split_axis=0, concat_axis=0, tiled=True)
    return everyone.reshape((count * value.shape[0],) + value.shape[1:])


def on_device(
    queries,
    prefix_keys,
    prefix_values,
    suffix_keys,
    suffix_values,
    out_weight,
    prefix_lists,
    suffix_lengths,
    block_place,
):
    quad = ("zp", "zq", "y", "c")
    swap = [(0, 1), (1, 0)]
    flat_queries = queries.reshape(ROWS, WIDE)
    listed = jnp.pad(prefix_lists.astype(jnp.bfloat16), ((0, 0), (0, 120)))
    pool = spread_along(jnp.concatenate([flat_queries, listed], axis=1), "zh", ZH)

    turned = out_weight.T
    turned = jnp.concatenate([turned, lax.ppermute(turned, "zp", swap)], axis=0)
    near_weight = lax.all_gather(turned, ("y", "c"), axis=0, tiled=True)

    lane = jnp.arange(128)
    stored = lax.axis_index("zh") * QUAD + lane
    here = (block_place[None, :] == stored[:, None]) & (lane < QUAD)[:, None]
    logical = jnp.sum(jnp.where(here, lane[None, :], 0), axis=1)
    logical = jnp.where(lane < QUAD, logical, -1).astype(jnp.float32)

    outgoing, select = pl.pallas_call(
        dispatch_kernel,
        out_shape=(
            jax.ShapeDtypeStruct((SLOTS, WIDE), jnp.bfloat16),
            jax.ShapeDtypeStruct((POOL, SLOTS), jnp.float32),
        ),
        compiler_params=PARAMS,
        name="dispatch",
    )(jnp.broadcast_to(logical[None], (8, 128)), pool)
    arrived = lax.all_to_all(outgoing, quad, split_axis=0, concat_axis=0, tiled=True)
    partials = pl.pallas_call(
        attend_kernel,
        in_specs=[pl.BlockSpec(memory_space=pltpu.VMEM)] * 3 + [pl.BlockSpec(memory_space=pl.ANY)],
        out_shape=packed(SLOTS),
        compiler_params=PARAMS,
        name="attend",
    )(
        arrived,
        prefix_keys.reshape(TOKENS, 2 * HD),
        prefix_values.reshape(TOKENS, 2 * HD),
        near_weight,
    )
    back = lax.all_to_all(partials, quad, split_axis=0, concat_axis=0, tiled=True)
    joined = pl.pallas_call(
        gather_kernel, out_shape=packed(POOL), compiler_params=PARAMS, name="gather"
    )(back, select)
    far = lax.all_to_all(joined, "zh", split_axis=0, concat_axis=0, tiled=True)

    own_out, own_log = own_partials(queries, suffix_keys, suffix_values, suffix_lengths)
    attended = pl.pallas_call(
        final_kernel,
        out_shape=jax.ShapeDtypeStruct((ROWS, WIDE), jnp.bfloat16),
        compiler_params=PARAMS,
        name="final",
    )(far, own_out, jnp.pad(own_log, ((0, 0), (0, 112))))

    rows = spread_along(attended, "zh", ZH)
    rows = jnp.concatenate([rows, lax.ppermute(rows, "zq", swap)], axis=0)
    steps = 4
    terms = pl.pallas_call(
        project_kernel,
        grid=(steps,),
        in_specs=[
            pl.BlockSpec((ZQ * POOL, WIDE), lambda step: (0, 0)),
            pl.BlockSpec((GROUP * 64 // steps, WIDE), lambda step: (step, 0)),
        ],
        out_specs=pl.BlockSpec((XS, GROUP // steps, 16, ZQ * POOL), lambda step: (0, step, 0, 0)),
        out_shape=jax.ShapeDtypeStruct((XS, GROUP, 16, ZQ * POOL), jnp.float32),
        compiler_params=PARAMS,
        name="project",
    )(rows, near_weight)
    terms = lax.all_to_all(terms, "kv", split_axis=0, concat_axis=0, tiled=True)
    one = [pl.BlockSpec(memory_space=pltpu.SMEM), pl.BlockSpec(memory_space=pltpu.VMEM)]
    parts = pl.pallas_call(
        sum_kernel,
        in_specs=one,
        out_shape=jax.ShapeDtypeStruct((GROUP, 16, ZQ * POOL), jnp.bfloat16),
        compiler_params=PARAMS,
        name="sum",
    )(lax.axis_index("zp").reshape(1).astype(jnp.int32), terms)
    parts = lax.all_to_all(parts, ("zp", "y", "c"), split_axis=0, concat_axis=0, tiled=True)
    return pl.pallas_call(
        settle_kernel,
        in_specs=one,
        out_shape=jax.ShapeDtypeStruct((ZH * QUAD * ROWS, 16), jnp.bfloat16),
        compiler_params=PARAMS,
        name="settle",
    )(lax.axis_index("zq").reshape(1).astype(jnp.int32), parts)


def solution(mesh):
    blk = ("zh", "zp", "zq", "y", "c")
    fine = Mesh(mesh.devices.reshape(ZH, ZP, ZQ, YS, CS, XS), blk + ("kv",))
    placed = (
        P(blk, "kv", None),
        P(blk, None, "kv", None),
        P(blk, None, "kv", None),
        P(blk, None, "kv", None),
        P(blk, None, "kv", None),
        P("kv", blk),
        P(blk, None),
        P(blk),
        P(),
    )
    return jax.shard_map(
        on_device, mesh=fine, in_specs=placed, out_specs=P(None, blk + ("kv",)), check_vma=False
    )
```

time: 299 us -> 237 us (0.79)
  waiting for transfers between devices: 171 us -> 111 us
  starting transfers between devices: 48.1 us -> 64.5 us
  blocking collectives: 28.2 us -> 18.8 us
  matrix products: 5.63 us -> 1.18 us
  other arithmetic: 5.87 us -> 2.39 us
    all_gather x3 -> x1, waiting for transfers between devices: 125 us -> 0.01 us  [on_device(): near_weight = lax.all_gather(turned, ('y', 'c'), axis=0, tiled=True)]
    all_to_all x2 -> x6, waiting for transfers between devices: 31.5 us -> 94.8 us  [the longest x1 27.8 us: on_device(): lax.all_to_all(partials, quad, split_axis=0, concat_axis=0, tiled=True)]
    all_to_all x2 -> x6, starting transfers between devices: 19.8 us -> 47.4 us  [the longest x1 15.1 us: spread_along(): lax.all_to_all(copies, axis, split_axis=0, concat_axis=0, tiled=True)]
    ppermute x7 -> x2, starting transfers between devices: 28.3 us -> 17 us  [the longest x1 11.2 us: on_device(): rows = jnp.concatenate([rows, lax.ppermute(rows, 'zq', swap)], axis=0)]
    all_to_all x1, blocking collectives: 28.2 us -> 18.8 us  [spread_along(): lax.all_to_all(copies, axis, split_axis=0, concat_axis=0, tiled=True)]
    reshape x2 -> x0, local copies, waits for them, and re-layouts: 4.01 us -> none  [the longest x1 2.62 us: on_device(): terms.reshape(PLANE, XS, 16, ZS, ROWS)]
    reduce_sum x2 -> x1, other arithmetic: 3.51 us -> 0.18 us  [on_device(): logical = jnp.sum(jnp.where(here, lane[None, :], 0), axis=1)]
    ppermute x7 -> x2, waiting for transfers between devices: 14.5 us -> 16.3 us  [the longest x1 11.2 us: on_device(): turned = jnp.concatenate([turned, lax.ppermute(turned, 'zp', swap)], axis=0)]
  transfers between devices with their start and end apart: 12 -> 9, of which waited for: 8 -> 8; matrix products, arithmetic and copies ran while one was open for 2% -> 2% of each run, Pallas kernels for 6% -> 1%
where the time goes in v2:
time: 237 us; the launch traced here: 236 us
  waiting for transfers between devices  111 us (47%)
  starting transfers between devices  64.5 us (27%)
  blocking collectives  18.8 us (8%)
  Pallas kernels  16.6 us (7%)
  between operations  13.6 us (6%)
  local copies, waits for them, and re-layouts  7.76 us (3%)
  other arithmetic  2.39 us (1%)
    all_to_all x1, waiting for transfers between devices, on_device(): lax.all_to_all(partials, quad, split_axis=0, concat_axis=0, tiled=True)  27.8 us
    all_to_all x1, waiting for transfers between devices, on_device(): lax.all_to_all(outgoing, quad, split_axis=0, concat_axis=0, tiled=True)  25.2 us
    all_to_all x1, blocking collectives, spread_along(): lax.all_to_all(copies, axis, split_axis=0, concat_axis=0, tiled=True)  18.8 us
    all_to_all x1, waiting for transfers between devices, spread_along(): lax.all_to_all(copies, axis, split_axis=0, concat_axis=0, tiled=True)  15.2 us
    all_to_all x1, starting transfers between devices, spread_along(): lax.all_to_all(copies, axis, split_axis=0, concat_axis=0, tiled=True)  15.1 us
    all_to_all x1, waiting for transfers between devices, on_device(): far = lax.all_to_all(joined, 'zh', split_axis=0, concat_axis=0, tiled=True)  12.9 us
    ppermute x1, starting transfers between devices, on_device(): rows = jnp.concatenate([rows, lax.ppermute(rows, 'zq', swap)], axis=0)  11.2 us
    ppermute x1, waiting for transfers between devices, on_device(): turned = jnp.concatenate([turned, lax.ppermute(turned, 'zp', swap)], axis=0)  11.2 us
  transfers between devices with their start and end apart: 9, of which 8 were waited for; matrix products, arithmetic and copies ran while one was open for 2% of the time, Pallas kernels for 1%

profile of v2, /device:TPU:1, one launch (start us, length us, event | category | flops | bytes accessed | tf_op | source)
XLA Modules:
  0.0 235.8 jit_solution(13216861072410520607)
XLA Ops:
  6.5 5.9 %collective-permute-start = (bf16[64,2048]{1,0:T(8,128)(2,1)}, bf16[64,2048]{1,0:T(8,128)(2,1)S(1)}, u32[]{:S(2)}, u32[]{:S(2)}) collective-permute-start(bf16[64,2048]{1,0:T(8,128)(2,1)} %bitcast.46), channel_id=1, source_target_pairs={{0,64},{64,0},{1,65},{65,1},{2,66},{66,2},{3,67},{67,3},{4,68},{68... | collective-permute-start | bytes 786440 | tf_op jit(solution)/shard_map/ppermute | solution.py:236
  12.4 11.2 %collective-permute-done = bf16[64,2048]{1,0:T(8,128)(2,1)S(1)} collective-permute-done((bf16[64,2048]{1,0:T(8,128)(2,1)}, bf16[64,2048]{1,0:T(8,128)(2,1)S(1)}, u32[]{:S(2)}, u32[]{:S(2)}) %collective-permute-start) | collective-permute-done | bytes 262176 | tf_op jit(solution)/shard_map/ppermute | solution.py:236
  23.6 1.8 pad_maximum_fusion
  26.3 15.1 %all-to-all-start = ((bf16[4,16,2176]{2,1,0:T(8,128)(2,1)}), bf16[4,16,2176]{2,1,0:T(8,128)(2,1)S(1)}, u32[]{:S(2)}, u32[]{:S(2)}) async-start(bf16[4,16,2176]{2,1,0:T(8,128)(2,1)} %broadcast_in_dim.58), calls=%async_computation | async-start | bytes 557056 | tf_op jit(solution)/shard_map/all_to_all | solution.py:214
  41.7 15.2 %all-to-all-done = bf16[4,16,2176]{2,1,0:T(8,128)(2,1)S(1)} async-done(((bf16[4,16,2176]{2,1,0:T(8,128)(2,1)}), bf16[4,16,2176]{2,1,0:T(8,128)(2,1)S(1)}, u32[]{:S(2)}, u32[]{:S(2)}) %all-to-all-start) | async-done | bytes 278560 | tf_op jit(solution)/shard_map/all_to_all | solution.py:214
  56.9 1.8 dispatch.1
  58.6 10.6 %all-to-all-start.1 = ((bf16[32,8,2048]{2,1,0:T(8,128)(2,1)}), bf16[32,8,2048]{2,1,0:T(8,128)(2,1)S(1)}, u32[]{:S(2)}, u32[]{:S(2)}) async-start(bf16[32,8,2048]{2,1,0:T(8,128)(2,1)} %bitcast.3), calls=%async_computation.1 | async-start | bytes 2097152 | tf_op jit(solution)/shard_map/all_to_all | solution.py:254
  70.6 25.2 %all-to-all-done.1 = bf16[32,8,2048]{2,1,0:T(8,128)(2,1)S(1)} async-done(((bf16[32,8,2048]{2,1,0:T(8,128)(2,1)}), bf16[32,8,2048]{2,1,0:T(8,128)(2,1)S(1)}, u32[]{:S(2)}, u32[]{:S(2)}) %all-to-all-start.1) | async-done | bytes 1048608 | tf_op jit(solution)/shard_map/all_to_all | solution.py:254
  95.8 2.2 copy-done.1
  98.0 9.2 %attend.1 = bf16[256,2176]{1,0:T(8,128)(2,1)} custom-call(bf16[256,2048]{1,0:T(8,128)(2,1)S(1)} %bitcast.36, bf16[1024,256]{1,0:T(8,128)(2,1)S(1)} %get-tuple-element.12.k_ref, bf16[1024,256]{1,0:T(8,128)(2,1)S(1)} %get-tuple-element.11.v_ref, bf16[1024,2048]{1,0:T(8,128)(2,1)S(1)} %copy-done.1), custom_call_target="tpu_custom_call" | custom-call | tf_op jit(solution)/shard_map/attend/pallas_call | solution.py:255
  107.2 5.4 %all-to-all-start.2 = ((bf16[32,8,2176]{2,1,0:T(8,128)(2,1)}), bf16[32,8,2176]{2,1,0:T(8,128)(2,1)S(1)}, u32[]{:S(2)}, u32[]{:S(2)}) async-start(bf16[32,8,2176]{2,1,0:T(8,128)(2,1)} %bitcast.6), calls=%async_computation.2 | async-start | bytes 2228224 | tf_op jit(solution)/shard_map/all_to_all | solution.py:267
  112.7 27.8 %all-to-all-done.2 = bf16[32,8,2176]{2,1,0:T(8,128)(2,1)S(1)} async-done(((bf16[32,8,2176]{2,1,0:T(8,128)(2,1)}), bf16[32,8,2176]{2,1,0:T(8,128)(2,1)S(1)}, u32[]{:S(2)}, u32[]{:S(2)}) %all-to-all-start.2) | async-done | bytes 1114144 | tf_op jit(solution)/shard_map/all_to_all | solution.py:267
  140.5 1.7 gather.1
  142.2 3.7 %all-to-all-start.3 = ((bf16[4,16,2176]{2,1,0:T(8,128)(2,1)}), bf16[4,16,2176]{2,1,0:T(8,128)(2,1)S(1)}, u32[]{:S(2)}, u32[]{:S(2)}) async-start(bf16[4,16,2176]{2,1,0:T(8,128)(2,1)} %bitcast.8), calls=%async_computation.3 | async-start | bytes 557056 | tf_op jit(solution)/shard_map/all_to_all | solution.py:271
  147.6 12.9 %all-to-all-done.3 = bf16[4,16,2176]{2,1,0:T(8,128)(2,1)S(1)} async-done(((bf16[4,16,2176]{2,1,0:T(8,128)(2,1)}), bf16[4,16,2176]{2,1,0:T(8,128)(2,1)S(1)}, u32[]{:S(2)}, u32[]{:S(2)}) %all-to-all-start.3) | async-done | bytes 278560 | tf_op jit(solution)/shard_map/all_to_all | solution.py:271
  160.9 18.8 %all_to_all.53 = bf16[4,16,2048]{2,1,0:T(8,128)(2,1)S(1)} all-to-all(bf16[4,16,2048]{2,1,0:T(8,128)(2,1)S(1)} %broadcast_in_dim.61), channel_id=1, replica_groups=mesh['zh'=4,'zp'=2,'zq'=2,'y'=4,'c'=2,'kv'=4] {'zh'}, dimensions={0} | all-to-all | bytes 524288 | tf_op jit(solution)/shard_map/all_to_all | solution.py:214
  179.7 11.2 %collective-permute-start.1 = (bf16[64,2048]{1,0:T(8,128)(2,1)S(1)}, bf16[64,2048]{1,0:T(8,128)(2,1)S(1)}, u32[]{:S(2)}, u32[]{:S(2)}) collective-permute-start(bf16[64,2048]{1,0:T(8,128)(2,1)S(1)} %bitcast.40), channel_id=1, source_target_pairs={{0,32},{32,0},{1,33},{33,1},{2,34},{34,2},{3,35},{35,3},{4,36},{36... | collective-permute-start | bytes 786440 | tf_op jit(solution)/shard_map/ppermute | solution.py:282
  190.9 5.1 %collective-permute-done.1 = bf16[64,2048]{1,0:T(8,128)(2,1)S(1)} collective-permute-done((bf16[64,2048]{1,0:T(8,128)(2,1)S(1)}, bf16[64,2048]{1,0:T(8,128)(2,1)S(1)}, u32[]{:S(2)}, u32[]{:S(2)}) %collective-permute-start.1) | collective-permute-done | bytes 262176 | tf_op jit(solution)/shard_map/ppermute | solution.py:282
  196.1 2.2 copy-done.2
  198.3 2.6 %project.1 = f32[4,16,16,128]{3,2,1,0:T(8,128)} custom-call(bf16[128,2048]{1,0:T(8,128)(2,1)S(1)} %pad_maximum_fusion.1.rows_ref, bf16[1024,2048]{1,0:T(8,128)(2,1)S(1)} %copy-done.2), custom_call_target="tpu_custom_call" | custom-call | tf_op jit(solution)/shard_map/project/pallas_call | solution.py:284
  200.9 4.0 %all-to-all-start.5 = ((f32[4,16,16,128]{3,2,1,0:T(8,128)}), f32[4,16,16,128]{3,2,1,0:T(8,128)S(1)}, u32[]{:S(2)}, u32[]{:S(2)}) async-start(f32[4,16,16,128]{3,2,1,0:T(8,128)} %project.1), calls=%async_computation.5 | async-start | bytes 1048576 | tf_op jit(solution)/shard_map/all_to_all | solution.py:296
  204.9 7.0 %all-to-all-done.5.terms_ref = f32[4,16,16,128]{3,2,1,0:T(8,128)S(1)} async-done(((f32[4,16,16,128]{3,2,1,0:T(8,128)}), f32[4,16,16,128]{3,2,1,0:T(8,128)S(1)}, u32[]{:S(2)}, u32[]{:S(2)}) %all-to-all-start.5) | async-done | bytes 524320 | tf_op jit(solution)/shard_map/all_to_all | solution.py:296
  212.5 8.6 %all-to-all-start.6 = ((bf16[16,16,128]{2,1,0:T(8,128)(2,1)}), bf16[16,16,128]{2,1,0:T(8,128)(2,1)S(1)}, u32[]{:S(2)}, u32[]{:S(2)}) async-start(bf16[16,16,128]{2,1,0:T(8,128)(2,1)} %sum.1), calls=%async_computation.6 | async-start | bytes 131072 | tf_op jit(solution)/shard_map/all_to_all | solution.py:305
  221.1 6.8 %all-to-all-done.6.parts_ref = bf16[16,16,128]{2,1,0:T(8,128)(2,1)S(1)} async-done(((bf16[16,16,128]{2,1,0:T(8,128)(2,1)}), bf16[16,16,128]{2,1,0:T(8,128)(2,1)S(1)}, u32[]{:S(2)}, u32[]{:S(2)}) %all-to-all-start.6) | async-done | bytes 65568 | tf_op jit(solution)/shard_map/all_to_all | solution.py:305
  (44 shorter events, 6.4 us)
Async XLA Ops:
  6.5 139.3 %copy-start = (bf16[16,128,2,128]{3,2,1,0:T(2,128)(2,1)S(1)}, bf16[16,128,2,128]{3,2,1,0:T(2,128)(2,1)}, u32[]{:S(2)}) copy-start(bf16[16,128,2,128]{3,2,1,0:T(2,128)(2,1)} %param.12) | copy-start | bytes 3145732
  6.5 18.9 %copy-start.3 = (bf16[16,16,128]{2,1,0:T(8,128)(2,1)S(1)}, bf16[16,16,128]{2,1,0:T(8,128)(2,1)}, u32[]{:S(2)}) copy-start(bf16[16,16,128]{2,1,0:T(8,128)(2,1)} %param.9) | copy-start | bytes 196612
  6.5 18.9 %copy-start.4 = (s32[16,8]{0,1:T(8,128)S(1)}, s32[16,8]{0,1:T(8,128)}, u32[]{:S(2)}) copy-start(s32[16,8]{0,1:T(8,128)} %param.15) | copy-start | bytes 1540
  6.5 89.3 %all-gather.2.cloned.1.call-start = ((), (), s32[]{:S(2)}) async-start(), calls=%async_computation.7 | async-start | bytes 4718592 | tf_op jit(solution)/shard_map/all_gather | solution.py:237
  6.5 17.0 %collective-permute-start = (bf16[64,2048]{1,0:T(8,128)(2,1)}, bf16[64,2048]{1,0:T(8,128)(2,1)S(1)}, u32[]{:S(2)}, u32[]{:S(2)}) collective-permute-start(bf16[64,2048]{1,0:T(8,128)(2,1)} %bitcast.46), channel_id=1, source_target_pairs={{0,64},{64,0},{1,65},{65,1},{2,66},{66,2},{3,67},{67,3},{4,68},{68... | collective-permute-start | bytes 786440 | tf_op jit(solution)/shard_map/ppermute | solution.py:236
  25.4 16.1 %copy-start.6 = (s32[128]{0:T(128)S(1)}, s32[128]{0:T(128)}, u32[]{:S(2)}) copy-start(s32[128]{0:T(128)} %param.17) | copy-start | bytes 1540
  26.3 30.5 %all-to-all-start = ((bf16[4,16,2176]{2,1,0:T(8,128)(2,1)}), bf16[4,16,2176]{2,1,0:T(8,128)(2,1)S(1)}, u32[]{:S(2)}, u32[]{:S(2)}) async-start(bf16[4,16,2176]{2,1,0:T(8,128)(2,1)} %broadcast_in_dim.58), calls=%async_computation | async-start | bytes 557056 | tf_op jit(solution)/shard_map/all_to_all | solution.py:214
  58.6 37.2 %all-to-all-start.1 = ((bf16[32,8,2048]{2,1,0:T(8,128)(2,1)}), bf16[32,8,2048]{2,1,0:T(8,128)(2,1)S(1)}, u32[]{:S(2)}, u32[]{:S(2)}) async-start(bf16[32,8,2048]{2,1,0:T(8,128)(2,1)} %bitcast.3), calls=%async_computation.1 | async-start | bytes 2097152 | tf_op jit(solution)/shard_map/all_to_all | solution.py:254
  95.8 2.2 copy-start.1
  107.2 5.4 %copy-start.5 = (s32[16]{0:T(128)S(1)}, s32[16]{0:T(128)}, u32[]{:S(2)}) copy-start(s32[16]{0:T(128)} %param.16) | copy-start | bytes 196
  107.2 33.3 %all-to-all-start.2 = ((bf16[32,8,2176]{2,1,0:T(8,128)(2,1)}), bf16[32,8,2176]{2,1,0:T(8,128)(2,1)S(1)}, u32[]{:S(2)}, u32[]{:S(2)}) async-start(bf16[32,8,2176]{2,1,0:T(8,128)(2,1)} %bitcast.6), calls=%async_computation.2 | async-start | bytes 2228224 | tf_op jit(solution)/shard_map/all_to_all | solution.py:267
  142.2 4.8 %copy-start.7 = (bf16[16,128,2,128]{3,2,1,0:T(2,128)(2,1)S(1)}, bf16[16,128,2,128]{3,2,1,0:T(2,128)(2,1)}, u32[]{:S(2)}) copy-start(bf16[16,128,2,128]{3,2,1,0:T(2,128)(2,1)} %param.13) | copy-start | bytes 3145732
  142.2 18.3 %all-to-all-start.3 = ((bf16[4,16,2176]{2,1,0:T(8,128)(2,1)}), bf16[4,16,2176]{2,1,0:T(8,128)(2,1)S(1)}, u32[]{:S(2)}, u32[]{:S(2)}) async-start(bf16[4,16,2176]{2,1,0:T(8,128)(2,1)} %bitcast.8), calls=%async_computation.3 | async-start | bytes 557056 | tf_op jit(solution)/shard_map/all_to_all | solution.py:271
  179.7 16.3 %collective-permute-start.1 = (bf16[64,2048]{1,0:T(8,128)(2,1)S(1)}, bf16[64,2048]{1,0:T(8,128)(2,1)S(1)}, u32[]{:S(2)}, u32[]{:S(2)}) collective-permute-start(bf16[64,2048]{1,0:T(8,128)(2,1)S(1)} %bitcast.40), channel_id=1, source_target_pairs={{0,32},{32,0},{1,33},{33,1},{2,34},{34,2},{3,35},{35,3},{4,36},{36... | collective-permute-start | bytes 786440 | tf_op jit(solution)/shard_map/ppermute | solution.py:282
  196.1 2.2 copy-start.2
  200.9 11.0 %all-to-all-start.5 = ((f32[4,16,16,128]{3,2,1,0:T(8,128)}), f32[4,16,16,128]{3,2,1,0:T(8,128)S(1)}, u32[]{:S(2)}, u32[]{:S(2)}) async-start(f32[4,16,16,128]{3,2,1,0:T(8,128)} %project.1), calls=%async_computation.5 | async-start | bytes 1048576 | tf_op jit(solution)/shard_map/all_to_all | solution.py:296
  212.5 15.4 %all-to-all-start.6 = ((bf16[16,16,128]{2,1,0:T(8,128)(2,1)}), bf16[16,16,128]{2,1,0:T(8,128)(2,1)S(1)}, u32[]{:S(2)}, u32[]{:S(2)}) async-start(bf16[16,16,128]{2,1,0:T(8,128)(2,1)} %sum.1), calls=%async_computation.6 | async-start | bytes 131072 | tf_op jit(solution)/shard_map/all_to_all | solution.py:305
Sparse Core Ops, SparseCore 0:
  25.6 45.2 all-gather.1

commit v3 on v2

--- a/solution.py
+++ b/solution.py
@@ -40,7 +40,7 @@
     return jnp.where(lanes(whole.shape) < HEADS, whole, 0.0)
 
 
-def dispatch_kernel(logical_ref, pool_ref, out_ref, select_ref):
+def dispatch_kernel(logical_ref, pool_ref, sides_ref, out_ref, select_ref):
     listed = pool_ref[:, WIDE:].astype(jnp.float32)
     logical = logical_ref[0:1, :]
     hot = jnp.zeros((POOL, 128), jnp.float32)
@@ -67,7 +67,7 @@
     ).astype(jnp.bfloat16)
 
 
-def attend_kernel(q_ref, k_ref, v_ref, weight_ref, out_ref):
+def attend_kernel(q_ref, k_ref, v_ref, above_ref, below_ref, out_ref):
     logs = jnp.zeros((SLOTS, 128), jnp.float32)
     lane = lanes((SLOTS, 128))
     for head in range(HEADS):
@@ -87,7 +87,7 @@
     out_ref[:, WIDE:] = split_parts(logs).astype(jnp.bfloat16)
 
 
-def gather_kernel(back_ref, select_ref, joined_ref):
+def gather_kernel(back_ref, select_ref, mine_ref, joined_ref):
     chosen = select_ref[...] > 0.5
     slot_logs = join_parts(back_ref[:, WIDE:].astype(jnp.float32)).T
     lane = lanes((POOL, 128))
@@ -144,42 +144,60 @@
         out_ref[:, head * HD : (head + 1) * HD] = columns[head].astype(jnp.bfloat16)
 
 
-def project_kernel(rows_ref, weight_ref, out_ref):
-    terms = lax.dot_general(
-        weight_ref[...], rows_ref[...], (((1,), (1,)), ((), ())), preferred_element_type=jnp.float32
-    )
-    owners = out_ref.shape[1]
-    for owner in range(owners):
-        for part in range(XS):
-            first = (owner * XS + part) * 16
-            out_ref[part, owner] = terms[first : first + 16, :]
+def project_kernel(rows_ref, mine_ref, other_ref, out_ref, held, sems):
+    pieces = 4
+    length = GROUP * 64 // pieces
+    copies = []
+    for piece in range(pieces):
+        source, first = (mine_ref, piece) if piece < pieces // 2 else (other_ref, piece - pieces // 2)
+        copy = pltpu.make_async_copy(
+            source.at[pl.ds(first * length, length), :], held.at[piece], sems.at[piece]
+        )
+        copy.start()
+        copies.append(copy)
+    for piece in range(pieces):
+        copies[piece].wait()
+        terms = lax.dot_general(
+            held[piece], rows_ref[...], (((1,), (1,)), ((), ())), preferred_element_type=jnp.float32
+        )
+        for owner in range(length // 64):
+            for part in range(XS):
+                first = (owner * XS + part) * 16
+                out_ref[part, piece * (length // 64) + owner] = terms[first : first + 16, :]
 
 
 def sum_kernel(place_ref, terms_ref, out_ref):
-    place = place_ref[0]
-    for owner in range(YS * CS):
-        for half in range(ZP):
-            index = owner * ZP + half
-            term = terms_ref[0, index]
-            for part in range(1, XS):
-                term = term + terms_ref[part, index]
-            side = place if half == 0 else 1 - place
-            out_ref[side * (YS * CS) + owner] = term.astype(jnp.bfloat16)
+    for far_core in range(CS):
+        core = place_ref[2] if far_core == 0 else 1 - place_ref[2]
+        for order, step in enumerate((0, 1, 3, 2)):
+            y = lax.rem(place_ref[1] + step, YS)
+            for far_side in range(ZP):
+                side = place_ref[0] if far_side == 0 else 1 - place_ref[0]
+                index = (far_core * YS + order) * ZP + far_side
+                term = terms_ref[0, index]
+                for part in range(1, XS):
+                    term = term + terms_ref[part, index]
+                out_ref[(side * YS + y) * CS + core] = term.astype(jnp.bfloat16)
 
 
 def settle_kernel(place_ref, parts_ref, out_ref):
     place = place_ref[0]
-    for group in range(GROUP):
-        side, owner = divmod(group, YS * CS)
-        turned = parts_ref[group].astype(jnp.float32).T.astype(jnp.bfloat16)
+    lane = lanes((16, 128))
+    for side in range(ZP):
+        parts = [
+            parts_ref[side * YS * CS + owner].astype(jnp.float32) for owner in range(YS * CS)
+        ]
         for half in range(ZQ):
             near = place if half == 0 else 1 - place
             for far in range(ZH):
-                start = ((far * ZP + side) * ZQ + near) * YS * CS + owner
                 first = (half * ZH + far) * ROWS
-                out_ref[pl.ds(pl.multiple_of(start * ROWS, ROWS), ROWS), :] = turned[
-                    first : first + ROWS, :
-                ]
+                tile = jnp.zeros((16, 128), jnp.float32)
+                for owner in range(YS * CS):
+                    shift = (owner * ROWS - first) % 128
+                    moved = parts[owner] if shift == 0 else pltpu.roll(parts[owner], shift, 1)
+                    tile = jnp.where(lane // ROWS == owner, moved, tile)
+                start = ((far * ZP + side) * ZQ + near) * 128
+                out_ref[:, pl.ds(pl.multiple_of(start, 128), 128)] = tile.astype(jnp.bfloat16)
 
 
 def own_partials(queries, own_keys, own_values, lengths):
@@ -209,6 +227,12 @@
     return jax.ShapeDtypeStruct((rows, PACK), jnp.bfloat16)
 
 
+def inputs(near, far):
+    return [pl.BlockSpec(memory_space=pltpu.VMEM)] * near + [
+        pl.BlockSpec(memory_space=pltpu.HBM)
+    ] * far
+
+
 def spread_along(value, axis, count):
     copies = jnp.broadcast_to(value[None], (count,) + value.shape)
     everyone = lax.all_to_all(copies, axis, split_axis=0, concat_axis=0, tiled=True)
@@ -232,9 +256,14 @@
     listed = jnp.pad(prefix_lists.astype(jnp.bfloat16), ((0, 0), (0, 120)))
     pool = spread_along(jnp.concatenate([flat_queries, listed], axis=1), "zh", ZH)
 
+    up = [(place, (place + 1) % YS) for place in range(YS)]
+    down = [(place, (place - 1) % YS) for place in range(YS)]
     turned = out_weight.T
-    turned = jnp.concatenate([turned, lax.ppermute(turned, "zp", swap)], axis=0)
-    near_weight = lax.all_gather(turned, ("y", "c"), axis=0, tiled=True)
+    sides = jnp.concatenate([turned, lax.ppermute(turned, "zp", swap)], axis=0)
+    above, below = lax.ppermute(sides, "y", down), lax.ppermute(sides, "y", up)
+    across = [lax.ppermute(above[:64], "y", down), lax.ppermute(below[64:], "y", up)]
+    mine = jnp.concatenate([sides, above, below] + across, axis=0)
+    other = lax.ppermute(mine, "c", swap)
 
     lane = jnp.arange(128)
     stored = lax.axis_index("zh") * QUAD + lane
@@ -244,17 +273,18 @@
 
     outgoing, select = pl.pallas_call(
         dispatch_kernel,
+        in_specs=inputs(2, 1),
         out_shape=(
             jax.ShapeDtypeStruct((SLOTS, WIDE), jnp.bfloat16),
             jax.ShapeDtypeStruct((POOL, SLOTS), jnp.float32),
         ),
         compiler_params=PARAMS,
         name="dispatch",
-    )(jnp.broadcast_to(logical[None], (8, 128)), pool)
+    )(jnp.broadcast_to(logical[None], (8, 128)), pool, sides)
     arrived = lax.all_to_all(outgoing, quad, split_axis=0, concat_axis=0, tiled=True)
     partials = pl.pallas_call(
         attend_kernel,
-        in_specs=[pl.BlockSpec(memory_space=pltpu.VMEM)] * 3 + [pl.BlockSpec(memory_space=pl.ANY)],
+        in_specs=inputs(3, 2),
         out_shape=packed(SLOTS),
         compiler_params=PARAMS,
         name="attend",
@@ -262,12 +292,17 @@
         arrived,
         prefix_keys.reshape(TOKENS, 2 * HD),
         prefix_values.reshape(TOKENS, 2 * HD),
-        near_weight,
+        above,
+        below,
     )
     back = lax.all_to_all(partials, quad, split_axis=0, concat_axis=0, tiled=True)
     joined = pl.pallas_call(
-        gather_kernel, out_shape=packed(POOL), compiler_params=PARAMS, name="gather"
-    )(back, select)
+        gather_kernel,
+        in_specs=inputs(2, 1),
+        out_shape=packed(POOL),
+        compiler_params=PARAMS,
+        name="gather",
+    )(back, select, mine)
     far = lax.all_to_all(joined, "zh", split_axis=0, concat_axis=0, tiled=True)
 
     own_out, own_log = own_partials(queries, suffix_keys, suffix_values, suffix_lengths)
@@ -280,36 +315,35 @@
 
     rows = spread_along(attended, "zh", ZH)
     rows = jnp.concatenate([rows, lax.ppermute(rows, "zq", swap)], axis=0)
-    steps = 4
     terms = pl.pallas_call(
         project_kernel,
-        grid=(steps,),
-        in_specs=[
-            pl.BlockSpec((ZQ * POOL, WIDE), lambda step: (0, 0)),
-            pl.BlockSpec((GROUP * 64 // steps, WIDE), lambda step: (step, 0)),
+        in_specs=inputs(1, 2),
+        out_shape=jax.ShapeDtypeStruct((XS, GROUP, 16, ZQ * POOL), jnp.float32),
+        scratch_shapes=[
+            pltpu.VMEM((4, GROUP * 64 // 4, WIDE), jnp.bfloat16),
+            pltpu.SemaphoreType.DMA((4,)),
         ],
-        out_specs=pl.BlockSpec((XS, GROUP // steps, 16, ZQ * POOL), lambda step: (0, step, 0, 0)),
-        out_shape=jax.ShapeDtypeStruct((XS, GROUP, 16, ZQ * POOL), jnp.float32),
         compiler_params=PARAMS,
         name="project",
-    )(rows, near_weight)
+    )(rows, mine, other)
     terms = lax.all_to_all(terms, "kv", split_axis=0, concat_axis=0, tiled=True)
     one = [pl.BlockSpec(memory_space=pltpu.SMEM), pl.BlockSpec(memory_space=pltpu.VMEM)]
+    place = jnp.stack([lax.axis_index(axis) for axis in ("zp", "y", "c")]).astype(jnp.int32)
     parts = pl.pallas_call(
         sum_kernel,
         in_specs=one,
         out_shape=jax.ShapeDtypeStruct((GROUP, 16, ZQ * POOL), jnp.bfloat16),
         compiler_params=PARAMS,
         name="sum",
-    )(lax.axis_index("zp").reshape(1).astype(jnp.int32), terms)
+    )(place, terms)
     parts = lax.all_to_all(parts, ("zp", "y", "c"), split_axis=0, concat_axis=0, tiled=True)
     return pl.pallas_call(
         settle_kernel,
         in_specs=one,
-        out_shape=jax.ShapeDtypeStruct((ZH * QUAD * ROWS, 16), jnp.bfloat16),
+        out_shape=jax.ShapeDtypeStruct((16, ZH * QUAD * ROWS), jnp.bfloat16),
         compiler_params=PARAMS,
         name="settle",
-    )(lax.axis_index("zq").reshape(1).astype(jnp.int32), parts)
+    )(lax.axis_index("zq").reshape(1).astype(jnp.int32), parts).T
 
 
 def solution(mesh):

time: 237 us -> 224 us (0.945)
  waiting for transfers between devices: 111 us -> 76 us
  starting transfers between devices: 64.5 us -> 78.3 us
  between operations: 13.6 us -> 0.28 us
  local copies, waits for them, and re-layouts: 7.76 us -> 16.4 us
  other arithmetic: 2.39 us -> 6.35 us
  blocking collectives: 18.8 us -> 22.1 us
  matrix products: 1.18 us -> 3.88 us
  Pallas kernels: 16.6 us -> 19.3 us
    ppermute x1 -> x6, waiting for transfers between devices: 11.2 us -> 51 us  [the longest x1 21.4 us: on_device(): sides = jnp.concatenate([turned, lax.ppermute(turned, 'zp', swap)], axis=0)]
    all_to_all x1, waiting for transfers between devices: 25.2 us -> 0.01 us  [on_device(): lax.all_to_all(outgoing, quad, split_axis=0, concat_axis=0, tiled=True)]
    all_to_all x1, waiting for transfers between devices: 27.8 us -> 3.36 us  [on_device(): lax.all_to_all(partials, quad, split_axis=0, concat_axis=0, tiled=True)]
    all_to_all x1, waiting for transfers between devices: 15.2 us -> 0.01 us  [spread_along(): lax.all_to_all(copies, axis, split_axis=0, concat_axis=0, tiled=True)]
    ppermute x1 -> x6, starting transfers between devices: 5.86 us -> 19 us  [the longest x1 4.51 us: on_device(): lax.ppermute(above[:64], 'y', down)]
    all_to_all x1, waiting for transfers between devices: 12.9 us -> 3.12 us  [on_device(): far = lax.all_to_all(joined, 'zh', split_axis=0, concat_axis=0, tiled=True)]
    all_to_all x1, starting transfers between devices: 3.7 us -> 10.5 us  [on_device(): far = lax.all_to_all(joined, 'zh', split_axis=0, concat_axis=0, tiled=True)]
    all_to_all x1, starting transfers between devices: 10.6 us -> 6.93 us  [on_device(): lax.all_to_all(outgoing, quad, split_axis=0, concat_axis=0, tiled=True)]
  transfers between devices with their start and end apart: 9 -> 13, of which waited for: 8 -> 10; matrix products, arithmetic and copies ran while one was open for 2% -> 9% of each run, Pallas kernels for 1% -> 1%
where the time goes in v3:
time: 224 us; the launch traced here: 223 us
  starting transfers between devices  78.3 us (35%)
  waiting for transfers between devices  76 us (34%)
  blocking collectives  22.1 us (10%)
  Pallas kernels  19.3 us (9%)
  local copies, waits for them, and re-layouts  16.4 us (7%)
  other arithmetic  6.35 us (3%)
  matrix products  3.88 us (2%)
    all_to_all x1, blocking collectives, spread_along(): lax.all_to_all(copies, axis, split_axis=0, concat_axis=0, tiled=True)  22.1 us
    ppermute x1, waiting for transfers between devices, on_device(): sides = jnp.concatenate([turned, lax.ppermute(turned, 'zp', swap)], axis=0)  21.4 us
    all_to_all x1, starting transfers between devices, spread_along(): lax.all_to_all(copies, axis, split_axis=0, concat_axis=0, tiled=True)  15.6 us
    ppermute x1, waiting for transfers between devices, on_device(): lax.ppermute(sides, 'y', down)  15.5 us
    all_to_all x1, starting transfers between devices, on_device(): far = lax.all_to_all(joined, 'zh', split_axis=0, concat_axis=0, tiled=True)  10.5 us
    ppermute x1, starting transfers between devices, on_device(): rows = jnp.concatenate([rows, lax.ppermute(rows, 'zq', swap)], axis=0)  9.5 us
    pallas_call x1, Pallas kernels, on_device(): pl.pallas_call(attend_kernel, in_specs=inputs(3, 2), out_shape=packed(SLO...  9.2 us
    ppermute x1, waiting for transfers between devices, on_device(): lax.ppermute(above[:64], 'y', down)  7.12 us
  transfers between devices with their start and end apart: 13, of which 10 were waited for; matrix products, arithmetic and copies ran while one was open for 9% of the time, Pallas kernels for 1%

profile of v3, /device:TPU:1, one launch (start us, length us, event | category | flops | bytes accessed | tf_op | source)
XLA Modules:
  0.0 222.7 jit_solution(14852012759077077093)
XLA Ops:
  2.5 15.6 %all-to-all-start = ((bf16[4,16,2176]{2,1,0:T(8,128)(2,1)}), bf16[4,16,2176]{2,1,0:T(8,128)(2,1)S(1)}, u32[]{:S(2)}, u32[]{:S(2)}) async-start(bf16[4,16,2176]{2,1,0:T(8,128)(2,1)} %broadcast_in_dim.58), calls=%async_computation | async-start | bytes 557056 | tf_op jit(solution)/shard_map/all_to_all | solution.py:238
  18.1 3.1 %collective-permute-start = (bf16[64,2048]{1,0:T(8,128)(2,1)}, bf16[64,2048]{1,0:T(8,128)(2,1)S(1)}, u32[]{:S(2)}, u32[]{:S(2)}) collective-permute-start(bf16[64,2048]{1,0:T(8,128)(2,1)} %bitcast.43), channel_id=1, source_target_pairs={{0,64},{64,0},{1,65},{65,1},{2,66},{66,2},{3,67},{67,3},{4,68},{68... | collective-permute-start | bytes 786440 | tf_op jit(solution)/shard_map/ppermute | solution.py:262
  22.1 21.4 %collective-permute-done = bf16[64,2048]{1,0:T(8,128)(2,1)S(1)} collective-permute-done((bf16[64,2048]{1,0:T(8,128)(2,1)}, bf16[64,2048]{1,0:T(8,128)(2,1)S(1)}, u32[]{:S(2)}, u32[]{:S(2)}) %collective-permute-start) | collective-permute-done | bytes 262176 | tf_op jit(solution)/shard_map/ppermute | solution.py:262
  47.2 6.9 %all-to-all-start.1 = ((bf16[32,8,2048]{2,1,0:T(8,128)(2,1)}), bf16[32,8,2048]{2,1,0:T(8,128)(2,1)S(1)}, u32[]{:S(2)}, u32[]{:S(2)}) async-start(bf16[32,8,2048]{2,1,0:T(8,128)(2,1)} %bitcast.6), calls=%async_computation.1 | async-start | bytes 2097152 | tf_op jit(solution)/shard_map/all_to_all | solution.py:284
  54.1 4.5 %collective-permute-start.1 = (bf16[128,2048]{1,0:T(8,128)(2,1)}, bf16[128,2048]{1,0:T(8,128)(2,1)S(1)}, u32[]{:S(2)}, u32[]{:S(2)}) collective-permute-start(bf16[128,2048]{1,0:T(8,128)(2,1)} %pad_maximum_fusion.sides_ref), channel_id=1, source_target_pairs={{0,24},{8,0},{16,8},{24,16},{1,25},{9,1},{17,9},{25,17},{2,26},{10... | collective-permute-start | bytes 1572872 | tf_op jit(solution)/shard_map/ppermute | solution.py:263
  62.9 15.5 %collective-permute-done.1.above_ref = bf16[128,2048]{1,0:T(8,128)(2,1)S(1)} collective-permute-done((bf16[128,2048]{1,0:T(8,128)(2,1)}, bf16[128,2048]{1,0:T(8,128)(2,1)S(1)}, u32[]{:S(2)}, u32[]{:S(2)}) %collective-permute-start.1) | collective-permute-done | bytes 524320 | tf_op jit(solution)/shard_map/ppermute | solution.py:263
  83.5 9.2 %attend.1 = bf16[256,2176]{1,0:T(8,128)(2,1)} custom-call(bf16[256,2048]{1,0:T(8,128)(2,1)S(1)} %bitcast.39, bf16[1024,256]{1,0:T(8,128)(2,1)S(1)} %copy-done.7, bf16[1024,256]{1,0:T(8,128)(2,1)S(1)} %copy-done.6, bf16[128,2048]{1,0:T(8,128)(2,1)S(1)} %collective-permute-done.1.above_ref, bf16[128,2048]{1,0:T(8,128)(2,1)S(1)} %collective-permute-done.2.below_ref), custom_call_target="tpu_custom_call" | custom-call | tf_op jit(solution)/shard_map/attend/pallas_call | solution.py:285
  92.7 5.7 %all-to-all-start.2 = ((bf16[32,8,2176]{2,1,0:T(8,128)(2,1)}), bf16[32,8,2176]{2,1,0:T(8,128)(2,1)}, u32[]{:S(2)}, u32[]{:S(2)}) async-start(bf16[32,8,2176]{2,1,0:T(8,128)(2,1)} %bitcast.8), calls=%async_computation.2 | async-start | bytes 2228224 | tf_op jit(solution)/shard_map/all_to_all | solution.py:298
  101.1 4.5 %collective-permute-start.3 = (bf16[64,2048]{1,0:T(8,128)(2,1)S(1)}, bf16[64,2048]{1,0:T(8,128)(2,1)S(1)}, u32[]{:S(2)}, u32[]{:S(2)}) collective-permute-start(bf16[64,2048]{1,0:T(8,128)(2,1)S(1)} %slice.8), channel_id=1, source_target_pairs={{0,24},{8,0},{16,8},{24,16},{1,25},{9,1},{17,9},{25,17},{2,26},{10... | collective-permute-start | bytes 786440 | tf_op jit(solution)/shard_map/ppermute | solution.py:264
  108.7 7.1 %collective-permute-done.3 = bf16[64,2048]{1,0:T(8,128)(2,1)S(1)} collective-permute-done((bf16[64,2048]{1,0:T(8,128)(2,1)S(1)}, bf16[64,2048]{1,0:T(8,128)(2,1)S(1)}, u32[]{:S(2)}, u32[]{:S(2)}) %collective-permute-start.3) | collective-permute-done | bytes 262176 | tf_op jit(solution)/shard_map/ppermute | solution.py:264
  115.8 4.2 %collective-permute-done.4 = bf16[64,2048]{1,0:T(8,128)(2,1)S(1)} collective-permute-done((bf16[64,2048]{1,0:T(8,128)(2,1)S(1)}, bf16[64,2048]{1,0:T(8,128)(2,1)S(1)}, u32[]{:S(2)}, u32[]{:S(2)}) %collective-permute-start.4) | collective-permute-done | bytes 262176 | tf_op jit(solution)/shard_map/ppermute | solution.py:264
  120.0 3.0 %collective-permute-start.6 = (bf16[512,2048]{1,0:T(8,128)(2,1)S(1)}, bf16[512,2048]{1,0:T(8,128)(2,1)}, u32[]{:S(2)}, u32[]{:S(2)}) collective-permute-start(bf16[512,2048]{1,0:T(8,128)(2,1)S(1)} %constant_dynamic-update-slice_fusion.mine_ref), channel_id=1, source_target_pairs={{0,4},{4,0},{1,5},{5,1},{2,6},{6,2},{3,7},{7,3},{8,12},{12,8},{9,1... | collective-permute-start | bytes 6291464 | tf_op jit(solution)/shard_map/ppermute | solution.py:266
  123.0 3.4 %all-to-all-done.2 = bf16[32,8,2176]{2,1,0:T(8,128)(2,1)} async-done(((bf16[32,8,2176]{2,1,0:T(8,128)(2,1)}), bf16[32,8,2176]{2,1,0:T(8,128)(2,1)}, u32[]{:S(2)}, u32[]{:S(2)}) %all-to-all-start.2) | async-done | bytes 1114144 | tf_op jit(solution)/shard_map/all_to_all | solution.py:298
  126.4 2.9 %gather.1 = bf16[64,2176]{1,0:T(8,128)(2,1)} custom-call(bf16[256,2176]{1,0:T(8,128)(2,1)} %bitcast.9.back_ref, f32[64,256]{1,0:T(8,128)S(1)} %get-tuple-element.8.select_ref, bf16[512,2048]{1,0:T(8,128)(2,1)S(1)} %constant_dynamic-update-slice_fusion.mine_ref), custom_call_target="tpu_custom_call" | custom-call | tf_op jit(solution)/shard_map/gather/pallas_call | solution.py:299
  129.3 10.5 %all-to-all-start.3 = ((bf16[4,16,2176]{2,1,0:T(8,128)(2,1)}), bf16[4,16,2176]{2,1,0:T(8,128)(2,1)S(1)}, u32[]{:S(2)}, u32[]{:S(2)}) async-start(bf16[4,16,2176]{2,1,0:T(8,128)(2,1)} %bitcast.10), calls=%async_computation.3 | async-start | bytes 557056 | tf_op jit(solution)/shard_map/all_to_all | solution.py:306
  151.2 3.1 %all-to-all-done.3 = bf16[4,16,2176]{2,1,0:T(8,128)(2,1)S(1)} async-done(((bf16[4,16,2176]{2,1,0:T(8,128)(2,1)}), bf16[4,16,2176]{2,1,0:T(8,128)(2,1)S(1)}, u32[]{:S(2)}, u32[]{:S(2)}) %all-to-all-start.3) | async-done | bytes 278560 | tf_op jit(solution)/shard_map/all_to_all | solution.py:306
  155.5 22.1 %all_to_all.53 = bf16[4,16,2048]{2,1,0:T(8,128)(2,1)S(1)} all-to-all(bf16[4,16,2048]{2,1,0:T(8,128)(2,1)S(1)} %broadcast_in_dim.61), channel_id=1, replica_groups=mesh['zh'=4,'zp'=2,'zq'=2,'y'=4,'c'=2,'kv'=4] {'zh'}, dimensions={0} | all-to-all | bytes 524288 | tf_op jit(solution)/shard_map/all_to_all | solution.py:238
  177.6 9.5 %collective-permute-start.5 = (bf16[64,2048]{1,0:T(8,128)(2,1)S(1)}, bf16[64,2048]{1,0:T(8,128)(2,1)S(1)}, u32[]{:S(2)}, u32[]{:S(2)}) collective-permute-start(bf16[64,2048]{1,0:T(8,128)(2,1)S(1)} %bitcast.45), channel_id=1, source_target_pairs={{0,32},{32,0},{1,33},{33,1},{2,34},{34,2},{3,35},{35,3},{4,36},{36... | collective-permute-start | bytes 786440 | tf_op jit(solution)/shard_map/ppermute | solution.py:317
  187.1 4.9 %collective-permute-done.5 = bf16[64,2048]{1,0:T(8,128)(2,1)S(1)} collective-permute-done((bf16[64,2048]{1,0:T(8,128)(2,1)S(1)}, bf16[64,2048]{1,0:T(8,128)(2,1)S(1)}, u32[]{:S(2)}, u32[]{:S(2)}) %collective-permute-start.5) | collective-permute-done | bytes 262176 | tf_op jit(solution)/shard_map/ppermute | solution.py:317
  192.1 2.9 %project.1 = f32[4,16,16,128]{3,2,1,0:T(8,128)S(1)} custom-call(bf16[128,2048]{1,0:T(8,128)(2,1)S(1)} %pad_maximum_fusion.1.rows_ref, bf16[512,2048]{1,0:T(8,128)(2,1)S(1)} %constant_dynamic-update-slice_fusion.mine_ref, bf16[512,2048]{1,0:T(8,128)(2,1)} %collective-permute-done.6.other_ref), custom_call_target="tpu_custom_call" | custom-call | tf_op jit(solution)/shard_map/project/pallas_call | solution.py:318
  195.8 4.0 %all-to-all-start.5 = ((f32[4,16,16,128]{3,2,1,0:T(8,128)}), f32[4,16,16,128]{3,2,1,0:T(8,128)S(1)}, u32[]{:S(2)}, u32[]{:S(2)}) async-start(f32[4,16,16,128]{3,2,1,0:T(8,128)} %copy-done.5), calls=%async_computation.5 | async-start | bytes 1048576 | tf_op jit(solution)/shard_map/all_to_all | solution.py:329
  199.9 6.9 %all-to-all-done.5.terms_ref = f32[4,16,16,128]{3,2,1,0:T(8,128)S(1)} async-done(((f32[4,16,16,128]{3,2,1,0:T(8,128)}), f32[4,16,16,128]{3,2,1,0:T(8,128)S(1)}, u32[]{:S(2)}, u32[]{:S(2)}) %all-to-all-start.5) | async-done | bytes 524320 | tf_op jit(solution)/shard_map/all_to_all | solution.py:329
  208.0 7.0 %all-to-all-start.6 = ((bf16[16,16,128]{2,1,0:T(8,128)(2,1)}), bf16[16,16,128]{2,1,0:T(8,128)(2,1)S(1)}, u32[]{:S(2)}, u32[]{:S(2)}) async-start(bf16[16,16,128]{2,1,0:T(8,128)(2,1)} %sum.1), calls=%async_computation.6 | async-start | bytes 131072 | tf_op jit(solution)/shard_map/all_to_all | solution.py:339
  215.0 6.8 %all-to-all-done.6.parts_ref = bf16[16,16,128]{2,1,0:T(8,128)(2,1)S(1)} async-done(((bf16[16,16,128]{2,1,0:T(8,128)(2,1)}), bf16[16,16,128]{2,1,0:T(8,128)(2,1)S(1)}, u32[]{:S(2)}, u32[]{:S(2)}) %all-to-all-start.6) | async-done | bytes 65568 | tf_op jit(solution)/shard_map/all_to_all | solution.py:339
  (71 shorter events, 37.6 us)
Async XLA Ops:
  0.0 139.7 %copy-start = (bf16[16,128,2,128]{3,2,1,0:T(2,128)(2,1)S(1)}, bf16[16,128,2,128]{3,2,1,0:T(2,128)(2,1)}, u32[]{:S(2)}) copy-start(bf16[16,128,2,128]{3,2,1,0:T(2,128)(2,1)} %param.12) | copy-start | bytes 3145732
  2.5 42.9 %all-to-all-start = ((bf16[4,16,2176]{2,1,0:T(8,128)(2,1)}), bf16[4,16,2176]{2,1,0:T(8,128)(2,1)S(1)}, u32[]{:S(2)}, u32[]{:S(2)}) async-start(bf16[4,16,2176]{2,1,0:T(8,128)(2,1)} %broadcast_in_dim.58), calls=%async_computation | async-start | bytes 557056 | tf_op jit(solution)/shard_map/all_to_all | solution.py:238
  18.1 25.3 %collective-permute-start = (bf16[64,2048]{1,0:T(8,128)(2,1)}, bf16[64,2048]{1,0:T(8,128)(2,1)S(1)}, u32[]{:S(2)}, u32[]{:S(2)}) collective-permute-start(bf16[64,2048]{1,0:T(8,128)(2,1)} %bitcast.43), channel_id=1, source_target_pairs={{0,64},{64,0},{1,65},{65,1},{2,66},{66,2},{3,67},{67,3},{4,68},{68... | collective-permute-start | bytes 786440 | tf_op jit(solution)/shard_map/ppermute | solution.py:262
  43.4 1.9 copy-start.10
  47.2 34.1 %all-to-all-start.1 = ((bf16[32,8,2048]{2,1,0:T(8,128)(2,1)}), bf16[32,8,2048]{2,1,0:T(8,128)(2,1)S(1)}, u32[]{:S(2)}, u32[]{:S(2)}) async-start(bf16[32,8,2048]{2,1,0:T(8,128)(2,1)} %bitcast.6), calls=%async_computation.1 | async-start | bytes 2097152 | tf_op jit(solution)/shard_map/all_to_all | solution.py:284
  54.1 24.3 %collective-permute-start.1 = (bf16[128,2048]{1,0:T(8,128)(2,1)}, bf16[128,2048]{1,0:T(8,128)(2,1)S(1)}, u32[]{:S(2)}, u32[]{:S(2)}) collective-permute-start(bf16[128,2048]{1,0:T(8,128)(2,1)} %pad_maximum_fusion.sides_ref), channel_id=1, source_target_pairs={{0,24},{8,0},{16,8},{24,16},{1,25},{9,1},{17,9},{25,17},{2,26},{10... | collective-permute-start | bytes 1572872 | tf_op jit(solution)/shard_map/ppermute | solution.py:263
  58.6 22.6 %collective-permute-start.2 = (bf16[128,2048]{1,0:T(8,128)(2,1)}, bf16[128,2048]{1,0:T(8,128)(2,1)S(1)}, u32[]{:S(2)}, u32[]{:S(2)}) collective-permute-start(bf16[128,2048]{1,0:T(8,128)(2,1)} %pad_maximum_fusion.sides_ref), channel_id=1, source_target_pairs={{0,8},{8,16},{16,24},{24,0},{1,9},{9,17},{17,25},{25,1},{2,10},{10... | collective-permute-start | bytes 1572872 | tf_op jit(solution)/shard_map/ppermute | solution.py:263
  78.4 14.3 %copy-start.1 = (bf16[128,2048]{1,0:T(8,128)(2,1)}, bf16[128,2048]{1,0:T(8,128)(2,1)S(1)}, u32[]{:S(2)}) copy-start(bf16[128,2048]{1,0:T(8,128)(2,1)S(1)} %collective-permute-done.1.above_ref) | copy-start | bytes 1572868
  81.3 11.5 %copy-start.3 = (bf16[128,2048]{1,0:T(8,128)(2,1)}, bf16[128,2048]{1,0:T(8,128)(2,1)S(1)}, u32[]{:S(2)}) copy-start(bf16[128,2048]{1,0:T(8,128)(2,1)S(1)} %collective-permute-done.2.below_ref) | copy-start | bytes 1572868
  81.3 1.2 copy-start.6
  92.7 5.7 %copy-start.13 = (s32[16]{0:T(128)S(1)}, s32[16]{0:T(128)}, u32[]{:S(2)}) copy-start(s32[16]{0:T(128)} %param.16) | copy-start | bytes 196
  92.7 6.4 %copy-start.9 = (bf16[2048,64]{0,1:T(8,128)(2,1)S(1)}, bf16[2048,64]{0,1:T(8,128)(2,1)}, u32[]{:S(2)}) copy-start(bf16[2048,64]{0,1:T(8,128)(2,1)} %param.14) | copy-start | bytes 786436
  92.7 33.6 %all-to-all-start.2 = ((bf16[32,8,2176]{2,1,0:T(8,128)(2,1)}), bf16[32,8,2176]{2,1,0:T(8,128)(2,1)}, u32[]{:S(2)}, u32[]{:S(2)}) async-start(bf16[32,8,2176]{2,1,0:T(8,128)(2,1)} %bitcast.8), calls=%async_computation.2 | async-start | bytes 2228224 | tf_op jit(solution)/shard_map/all_to_all | solution.py:298
  98.5 10.1 %copy-start.2 = (bf16[128,2048]{1,0:T(8,128)(2,1)S(1)}, bf16[128,2048]{1,0:T(8,128)(2,1)}, u32[]{:S(2)}) copy-start(bf16[128,2048]{1,0:T(8,128)(2,1)} %copy-done.1) | copy-start | bytes 1572868
  98.5 10.1 %copy-start.4 = (bf16[128,2048]{1,0:T(8,128)(2,1)S(1)}, bf16[128,2048]{1,0:T(8,128)(2,1)}, u32[]{:S(2)}) copy-start(bf16[128,2048]{1,0:T(8,128)(2,1)} %copy-done.3) | copy-start | bytes 1572868
  101.1 14.6 %collective-permute-start.3 = (bf16[64,2048]{1,0:T(8,128)(2,1)S(1)}, bf16[64,2048]{1,0:T(8,128)(2,1)S(1)}, u32[]{:S(2)}, u32[]{:S(2)}) collective-permute-start(bf16[64,2048]{1,0:T(8,128)(2,1)S(1)} %slice.8), channel_id=1, source_target_pairs={{0,24},{8,0},{16,8},{24,16},{1,25},{9,1},{17,9},{25,17},{2,26},{10... | collective-permute-start | bytes 786440 | tf_op jit(solution)/shard_map/ppermute | solution.py:264
  106.6 13.4 %collective-permute-start.4 = (bf16[64,2048]{1,0:T(8,128)(2,1)S(1)}, bf16[64,2048]{1,0:T(8,128)(2,1)S(1)}, u32[]{:S(2)}, u32[]{:S(2)}) collective-permute-start(bf16[64,2048]{1,0:T(8,128)(2,1)S(1)} %slice.9), channel_id=1, source_target_pairs={{0,8},{8,16},{16,24},{24,0},{1,9},{9,17},{17,25},{25,1},{2,10},{10... | collective-permute-start | bytes 786440 | tf_op jit(solution)/shard_map/ppermute | solution.py:264
  120.0 72.1 %collective-permute-start.6 = (bf16[512,2048]{1,0:T(8,128)(2,1)S(1)}, bf16[512,2048]{1,0:T(8,128)(2,1)}, u32[]{:S(2)}, u32[]{:S(2)}) collective-permute-start(bf16[512,2048]{1,0:T(8,128)(2,1)S(1)} %constant_dynamic-update-slice_fusion.mine_ref), channel_id=1, source_target_pairs={{0,4},{4,0},{1,5},{5,1},{2,6},{6,2},{3,7},{7,3},{8,12},{12,8},{9,1... | collective-permute-start | bytes 6291464 | tf_op jit(solution)/shard_map/ppermute | solution.py:266
  129.3 25.1 %all-to-all-start.3 = ((bf16[4,16,2176]{2,1,0:T(8,128)(2,1)}), bf16[4,16,2176]{2,1,0:T(8,128)(2,1)S(1)}, u32[]{:S(2)}, u32[]{:S(2)}) async-start(bf16[4,16,2176]{2,1,0:T(8,128)(2,1)} %bitcast.10), calls=%async_computation.3 | async-start | bytes 557056 | tf_op jit(solution)/shard_map/all_to_all | solution.py:306
  146.2 1.7 copy-start.11
  146.2 1.8 copy-start.12
  177.6 14.4 %collective-permute-start.5 = (bf16[64,2048]{1,0:T(8,128)(2,1)S(1)}, bf16[64,2048]{1,0:T(8,128)(2,1)S(1)}, u32[]{:S(2)}, u32[]{:S(2)}) collective-permute-start(bf16[64,2048]{1,0:T(8,128)(2,1)S(1)} %bitcast.45), channel_id=1, source_target_pairs={{0,32},{32,0},{1,33},{33,1},{2,34},{34,2},{3,35},{35,3},{4,36},{36... | collective-permute-start | bytes 786440 | tf_op jit(solution)/shard_map/ppermute | solution.py:317
  195.8 11.0 %all-to-all-start.5 = ((f32[4,16,16,128]{3,2,1,0:T(8,128)}), f32[4,16,16,128]{3,2,1,0:T(8,128)S(1)}, u32[]{:S(2)}, u32[]{:S(2)}) async-start(f32[4,16,16,128]{3,2,1,0:T(8,128)} %copy-done.5), calls=%async_computation.5 | async-start | bytes 1048576 | tf_op jit(solution)/shard_map/all_to_all | solution.py:329
  208.0 13.8 %all-to-all-start.6 = ((bf16[16,16,128]{2,1,0:T(8,128)(2,1)}), bf16[16,16,128]{2,1,0:T(8,128)(2,1)S(1)}, u32[]{:S(2)}, u32[]{:S(2)}) async-start(bf16[16,16,128]{2,1,0:T(8,128)(2,1)} %sum.1), calls=%async_computation.6 | async-start | bytes 131072 | tf_op jit(solution)/shard_map/all_to_all | solution.py:339
  (3 other events, 2.6 us)

commit v4 on v3

--- a/solution.py
+++ b/solution.py
@@ -40,7 +40,7 @@
     return jnp.where(lanes(whole.shape) < HEADS, whole, 0.0)
 
 
-def dispatch_kernel(logical_ref, pool_ref, sides_ref, out_ref, select_ref):
+def dispatch_kernel(logical_ref, pool_ref, above_ref, below_ref, out_ref, select_ref):
     listed = pool_ref[:, WIDE:].astype(jnp.float32)
     logical = logical_ref[0:1, :]
     hot = jnp.zeros((POOL, 128), jnp.float32)
@@ -67,15 +67,26 @@
     ).astype(jnp.bfloat16)
 
 
-def attend_kernel(q_ref, k_ref, v_ref, above_ref, below_ref, out_ref):
+def attend_kernel(q_ref, k_ref, v_ref, weight_ref, facing_ref, own_ref, out_ref):
     logs = jnp.zeros((SLOTS, 128), jnp.float32)
     lane = lanes((SLOTS, 128))
+
+    def scores_of(head):
+        group = slice((head // 8) * HD, (head // 8 + 1) * HD)
+        return lax.dot_general(
+            q_ref[:, head * HD : (head + 1) * HD],
+            k_ref[:, group],
+            (((1,), (1,)), ((), ())),
+            preferred_element_type=jnp.float32,
+        )
+
+    coming = scores_of(0)
     for head in range(HEADS):
+        scores = coming
+        if head + 1 < HEADS:
+            coming = scores_of(head + 1)
         group = slice((head // 8) * HD, (head // 8 + 1) * HD)
         at = slice(head * HD, (head + 1) * HD)
-        scores = lax.dot_general(
-            q_ref[:, at], k_ref[:, group], (((1,), (1,)), ((), ())), preferred_element_type=jnp.float32
-        )
         top = jnp.max(scores, axis=1, keepdims=True)
         grown = jnp.exp2((scores - top) * (SCALE * LOG2E))
         total = jnp.sum(grown, axis=1, keepdims=True)
@@ -87,7 +98,7 @@
     out_ref[:, WIDE:] = split_parts(logs).astype(jnp.bfloat16)
 
 
-def gather_kernel(back_ref, select_ref, mine_ref, joined_ref):
+def gather_kernel(back_ref, select_ref, weight_ref, facing_ref, joined_ref):
     chosen = select_ref[...] > 0.5
     slot_logs = join_parts(back_ref[:, WIDE:].astype(jnp.float32)).T
     lane = lanes((POOL, 128))
@@ -136,7 +147,7 @@
     )
 
 
-def final_kernel(far_ref, own_ref, own_log_ref, out_ref):
+def final_kernel(far_ref, own_ref, own_log_ref, weight_ref, out_ref):
     terms = [packed_term(far_ref, index) for index in range(ZH)]
     terms.append((lambda at: own_ref[:, at], own_log_ref[...]))
     columns, _ = merge(terms)
@@ -144,36 +155,32 @@
         out_ref[:, head * HD : (head + 1) * HD] = columns[head].astype(jnp.bfloat16)
 
 
-def project_kernel(rows_ref, mine_ref, other_ref, out_ref, held, sems):
-    pieces = 4
-    length = GROUP * 64 // pieces
+def project_kernel(rows_ref, *refs):
+    sources, out_ref, held, sems = refs[:4], refs[4], refs[5], refs[6]
     copies = []
-    for piece in range(pieces):
-        source, first = (mine_ref, piece) if piece < pieces // 2 else (other_ref, piece - pieces // 2)
-        copy = pltpu.make_async_copy(
-            source.at[pl.ds(first * length, length), :], held.at[piece], sems.at[piece]
-        )
+    for piece, source in enumerate(sources):
+        copy = pltpu.make_async_copy(source, held.at[piece], sems.at[piece])
         copy.start()
         copies.append(copy)
-    for piece in range(pieces):
+    for piece in range(4):
         copies[piece].wait()
         terms = lax.dot_general(
             held[piece], rows_ref[...], (((1,), (1,)), ((), ())), preferred_element_type=jnp.float32
         )
-        for owner in range(length // 64):
+        for owner in range(YS):
             for part in range(XS):
                 first = (owner * XS + part) * 16
-                out_ref[part, piece * (length // 64) + owner] = terms[first : first + 16, :]
+                out_ref[part, piece * YS + owner] = terms[first : first + 16, :]
 
 
 def sum_kernel(place_ref, terms_ref, out_ref):
-    for far_core in range(CS):
-        core = place_ref[2] if far_core == 0 else 1 - place_ref[2]
-        for order, step in enumerate((0, 1, 3, 2)):
-            y = lax.rem(place_ref[1] + step, YS)
-            for far_side in range(ZP):
-                side = place_ref[0] if far_side == 0 else 1 - place_ref[0]
-                index = (far_core * YS + order) * ZP + far_side
+    for far_side in range(ZP):
+        side = place_ref[0] if far_side == 0 else 1 - place_ref[0]
+        for far_core in range(CS):
+            core = place_ref[2] if far_core == 0 else 1 - place_ref[2]
+            for order, step in enumerate((0, 1, 3, 2)):
+                y = lax.rem(place_ref[1] + step, YS)
+                index = (far_side * CS + far_core) * YS + order
                 term = terms_ref[0, index]
                 for part in range(1, XS):
                     term = term + terms_ref[part, index]
@@ -258,12 +265,22 @@
 
     up = [(place, (place + 1) % YS) for place in range(YS)]
     down = [(place, (place - 1) % YS) for place in range(YS)]
+
+    def beside(block):
+        return lax.ppermute(block, "y", down), lax.ppermute(block, "y", up)
+
+    def piece_of(block, above, below):
+        across = [lax.ppermute(above[:32], "y", down), lax.ppermute(below[32:], "y", up)]
+        return jnp.concatenate([block, above, below] + across, axis=0)
+
     turned = out_weight.T
-    sides = jnp.concatenate([turned, lax.ppermute(turned, "zp", swap)], axis=0)
-    above, below = lax.ppermute(sides, "y", down), lax.ppermute(sides, "y", up)
-    across = [lax.ppermute(above[:64], "y", down), lax.ppermute(below[64:], "y", up)]
-    mine = jnp.concatenate([sides, above, below] + across, axis=0)
+    facing = lax.ppermute(turned, "zp", swap)
+    above, below = beside(turned)
+    mine = piece_of(turned, above, below)
+    mine_far = piece_of(facing, *beside(facing))
     other = lax.ppermute(mine, "c", swap)
+    other_far = lax.ppermute(mine_far, "c", swap)
+    own_out, own_log = own_partials(queries, suffix_keys, suffix_values, suffix_lengths)
 
     lane = jnp.arange(128)
     stored = lax.axis_index("zh") * QUAD + lane
@@ -273,18 +290,18 @@
 
     outgoing, select = pl.pallas_call(
         dispatch_kernel,
-        in_specs=inputs(2, 1),
+        in_specs=inputs(2, 2),
         out_shape=(
             jax.ShapeDtypeStruct((SLOTS, WIDE), jnp.bfloat16),
             jax.ShapeDtypeStruct((POOL, SLOTS), jnp.float32),
         ),
         compiler_params=PARAMS,
         name="dispatch",
-    )(jnp.broadcast_to(logical[None], (8, 128)), pool, sides)
+    )(jnp.broadcast_to(logical[None], (8, 128)), pool, above, below)
     arrived = lax.all_to_all(outgoing, quad, split_axis=0, concat_axis=0, tiled=True)
     partials = pl.pallas_call(
         attend_kernel,
-        in_specs=inputs(3, 2),
+        in_specs=inputs(3, 3),
         out_shape=packed(SLOTS),
         compiler_params=PARAMS,
         name="attend",
@@ -292,32 +309,33 @@
         arrived,
         prefix_keys.reshape(TOKENS, 2 * HD),
         prefix_values.reshape(TOKENS, 2 * HD),
-        above,
-        below,
+        mine,
+        facing,
+        own_out,
     )
     back = lax.all_to_all(partials, quad, split_axis=0, concat_axis=0, tiled=True)
     joined = pl.pallas_call(
         gather_kernel,
-        in_specs=inputs(2, 1),
+        in_specs=inputs(2, 2),
         out_shape=packed(POOL),
         compiler_params=PARAMS,
         name="gather",
-    )(back, select, mine)
+    )(back, select, other, mine_far)
     far = lax.all_to_all(joined, "zh", split_axis=0, concat_axis=0, tiled=True)
 
-    own_out, own_log = own_partials(queries, suffix_keys, suffix_values, suffix_lengths)
     attended = pl.pallas_call(
         final_kernel,
+        in_specs=inputs(3, 1),
         out_shape=jax.ShapeDtypeStruct((ROWS, WIDE), jnp.bfloat16),
         compiler_params=PARAMS,
         name="final",
-    )(far, own_out, jnp.pad(own_log, ((0, 0), (0, 112))))
+    )(far, own_out, jnp.pad(own_log, ((0, 0), (0, 112))), other_far)
 
     rows = spread_along(attended, "zh", ZH)
     rows = jnp.concatenate([rows, lax.ppermute(rows, "zq", swap)], axis=0)
     terms = pl.pallas_call(
         project_kernel,
-        in_specs=inputs(1, 2),
+        in_specs=inputs(1, 4),
         out_shape=jax.ShapeDtypeStruct((XS, GROUP, 16, ZQ * POOL), jnp.float32),
         scratch_shapes=[
             pltpu.VMEM((4, GROUP * 64 // 4, WIDE), jnp.bfloat16),
@@ -325,7 +343,7 @@
         ],
         compiler_params=PARAMS,
         name="project",
-    )(rows, mine, other)
+    )(rows, mine, other, mine_far, other_far)
     terms = lax.all_to_all(terms, "kv", split_axis=0, concat_axis=0, tiled=True)
     one = [pl.BlockSpec(memory_space=pltpu.SMEM), pl.BlockSpec(memory_space=pltpu.VMEM)]
     place = jnp.stack([lax.axis_index(axis) for axis in ("zp", "y", "c")]).astype(jnp.int32)

time: 224 us -> 227 us (1.013)
  starting transfers between devices: 78.3 us -> 99.4 us
  waiting for transfers between devices: 76 us -> 68 us
  other arithmetic: 6.35 us -> 2.64 us
  Pallas kernels: 19.3 us -> 15.9 us
  matrix products: 3.88 us -> 1.17 us
  blocking collectives: 22.1 us -> 19.5 us
    ppermute x5 -> x10, starting transfers between devices: 15.9 us -> 32.9 us  [the longest x4 13 us: beside(): return (lax.ppermute(block, 'y', down), lax.ppermute(block, 'y', up))]
    ppermute x5 -> x10, waiting for transfers between devices: 51 us -> 41.8 us  [the longest x1 15.5 us: on_device(): facing = lax.ppermute(turned, 'zp', swap)]
    all_to_all x1, starting transfers between devices: 10.5 us -> 3.62 us  [on_device(): far = lax.all_to_all(joined, 'zh', split_axis=0, concat_axis=0, tiled=True)]
    all_to_all x1, starting transfers between devices: 6.93 us -> 13.7 us  [on_device(): lax.all_to_all(outgoing, quad, split_axis=0, concat_axis=0, tiled=True)]
    unnamed x36 -> x53, local copies, waits for them, and re-layouts: 5.97 us -> 10.6 us
    all_to_all x1, waiting for transfers between devices: 3.12 us -> 7.67 us  [on_device(): far = lax.all_to_all(joined, 'zh', split_axis=0, concat_axis=0, tiled=True)]
    ppermute x1, starting transfers between devices: 9.5 us -> 13.5 us  [on_device(): rows = jnp.concatenate([rows, lax.ppermute(rows, 'zq', swap)], axis=0)]
    all_to_all x1, waiting for transfers between devices: 3.36 us -> 0.01 us  [on_device(): lax.all_to_all(partials, quad, split_axis=0, concat_axis=0, tiled=True)]
  transfers between devices with their start and end apart: 13 -> 18, of which waited for: 10 -> 12; matrix products, arithmetic and copies ran while one was open for 9% -> 5% of each run, Pallas kernels for 1% -> 1%
where the time goes in v4:
time: 227 us; the launch traced here: 225 us
  starting transfers between devices  99.4 us (44%)
  waiting for transfers between devices  68 us (30%)
  blocking collectives  19.5 us (9%)
  local copies, waits for them, and re-layouts  18 us (8%)
  Pallas kernels  15.9 us (7%)
  other arithmetic  2.64 us (1%)
    all_to_all x1, blocking collectives, spread_along(): lax.all_to_all(copies, axis, split_axis=0, concat_axis=0, tiled=True)  19.5 us
    all_to_all x1, starting transfers between devices, spread_along(): lax.all_to_all(copies, axis, split_axis=0, concat_axis=0, tiled=True)  15.6 us
    ppermute x1, waiting for transfers between devices, on_device(): facing = lax.ppermute(turned, 'zp', swap)  15.5 us
    ppermute x4, waiting for transfers between devices, beside(): return (lax.ppermute(block, 'y', down), lax.ppermute(block, 'y', up))  14.9 us
    all_to_all x1, starting transfers between devices, on_device(): lax.all_to_all(outgoing, quad, split_axis=0, concat_axis=0, tiled=True)  13.7 us
    ppermute x1, starting transfers between devices, on_device(): rows = jnp.concatenate([rows, lax.ppermute(rows, 'zq', swap)], axis=0)  13.5 us
    ppermute x4, starting transfers between devices, beside(): return (lax.ppermute(block, 'y', down), lax.ppermute(block, 'y', up))  13 us
    unnamed x53, local copies, waits for them, and re-layouts  10.6 us
  transfers between devices with their start and end apart: 18, of which 12 were waited for; matrix products, arithmetic and copies ran while one was open for 5% of the time, Pallas kernels for 1%

profile of v4, /device:TPU:1, one launch (start us, length us, event | category | flops | bytes accessed | tf_op | source)
XLA Modules:
  0.0 225.1 jit_solution(2424121691161660985)
XLA Ops:
  2.5 15.6 %all-to-all-start = ((bf16[4,16,2176]{2,1,0:T(8,128)(2,1)}), bf16[4,16,2176]{2,1,0:T(8,128)(2,1)S(1)}, u32[]{:S(2)}, u32[]{:S(2)}) async-start(bf16[4,16,2176]{2,1,0:T(8,128)(2,1)} %broadcast_in_dim.58), calls=%async_computation | async-start | bytes 557056 | tf_op jit(solution)/shard_map/all_to_all | solution.py:245
  18.1 4.6 %collective-permute-start = (bf16[64,2048]{1,0:T(8,128)(2,1)}, bf16[64,2048]{1,0:T(8,128)(2,1)S(1)}, u32[]{:S(2)}, u32[]{:S(2)}) collective-permute-start(bf16[64,2048]{1,0:T(8,128)(2,1)} %bitcast.5), channel_id=1, source_target_pairs={{0,24},{8,0},{16,8},{24,16},{1,25},{9,1},{17,9},{25,17},{2,26},{10... | collective-permute-start | bytes 786440 | tf_op jit(solution)/shard_map/ppermute | solution.py:270
  27.7 4.9 %collective-permute-done.1.below_ref = bf16[64,2048]{1,0:T(8,128)(2,1)S(1)} collective-permute-done((bf16[64,2048]{1,0:T(8,128)(2,1)}, bf16[64,2048]{1,0:T(8,128)(2,1)S(1)}, u32[]{:S(2)}, u32[]{:S(2)}) %collective-permute-start.1) | collective-permute-done | bytes 262176 | tf_op jit(solution)/shard_map/ppermute | solution.py:270
  34.5 13.7 %all-to-all-start.1 = ((bf16[32,8,2048]{2,1,0:T(8,128)(2,1)}), bf16[32,8,2048]{2,1,0:T(8,128)(2,1)S(1)}, u32[]{:S(2)}, u32[]{:S(2)}) async-start(bf16[32,8,2048]{2,1,0:T(8,128)(2,1)} %bitcast.44), calls=%async_computation.1 | async-start | bytes 2097152 | tf_op jit(solution)/shard_map/all_to_all | solution.py:301
  48.2 4.3 %collective-permute-start.4 = (bf16[64,2048]{1,0:T(8,128)(2,1)}, bf16[64,2048]{1,0:T(8,128)(2,1)}, u32[]{:S(2)}, u32[]{:S(2)}) collective-permute-start(bf16[64,2048]{1,0:T(8,128)(2,1)} %bitcast.5), channel_id=1, source_target_pairs={{0,64},{64,0},{1,65},{65,1},{2,66},{66,2},{3,67},{67,3},{4,68},{68... | collective-permute-start | bytes 786440 | tf_op jit(solution)/shard_map/ppermute | solution.py:277
  57.0 4.3 %collective-permute-start.2 = (bf16[32,2048]{1,0:T(8,128)(2,1)S(1)}, bf16[32,2048]{1,0:T(8,128)(2,1)S(1)}, u32[]{:S(2)}, u32[]{:S(2)}) collective-permute-start(bf16[32,2048]{1,0:T(8,128)(2,1)S(1)} %slice.16), channel_id=1, source_target_pairs={{0,24},{8,0},{16,8},{24,16},{1,25},{9,1},{17,9},{25,17},{2,26},{10... | collective-permute-start | bytes 393224 | tf_op jit(solution)/shard_map/ppermute | solution.py:273
  64.5 5.2 %collective-permute-done.3 = bf16[32,2048]{1,0:T(8,128)(2,1)S(1)} collective-permute-done((bf16[32,2048]{1,0:T(8,128)(2,1)S(1)}, bf16[32,2048]{1,0:T(8,128)(2,1)S(1)}, u32[]{:S(2)}, u32[]{:S(2)}) %collective-permute-start.3) | collective-permute-done | bytes 131104 | tf_op jit(solution)/shard_map/ppermute | solution.py:273
  69.7 15.5 %collective-permute-done.4.facing_ref = bf16[64,2048]{1,0:T(8,128)(2,1)} collective-permute-done((bf16[64,2048]{1,0:T(8,128)(2,1)}, bf16[64,2048]{1,0:T(8,128)(2,1)}, u32[]{:S(2)}, u32[]{:S(2)}) %collective-permute-start.4) | collective-permute-done | bytes 262176 | tf_op jit(solution)/shard_map/ppermute | solution.py:277
  87.3 6.8 %attend.1 = bf16[256,2176]{1,0:T(8,128)(2,1)} custom-call(bf16[256,2048]{1,0:T(8,128)(2,1)S(1)} %bitcast.39, bf16[1024,256]{1,0:T(8,128)(2,1)S(1)} %copy-done.6, bf16[1024,256]{1,0:T(8,128)(2,1)S(1)} %copy-done.5, bf16[256,2048]{1,0:T(8,128)(2,1)S(1)} %constant_dynamic-update-slice_fusion.weight_ref.refs_0_, ...), custom_call_target="tpu_custom_call" | custom-call | tf_op jit(solution)/shard_map/attend/pallas_call | solution.py:302
  94.0 6.2 %all-to-all-start.2 = ((bf16[32,8,2176]{2,1,0:T(8,128)(2,1)}), bf16[32,8,2176]{2,1,0:T(8,128)(2,1)}, u32[]{:S(2)}, u32[]{:S(2)}) async-start(bf16[32,8,2176]{2,1,0:T(8,128)(2,1)} %bitcast.9), calls=%async_computation.2 | async-start | bytes 2228224 | tf_op jit(solution)/shard_map/all_to_all | solution.py:316
  100.3 4.5 %collective-permute-start.6 = (bf16[64,2048]{1,0:T(8,128)(2,1)}, bf16[64,2048]{1,0:T(8,128)(2,1)S(1)}, u32[]{:S(2)}, u32[]{:S(2)}) collective-permute-start(bf16[64,2048]{1,0:T(8,128)(2,1)} %collective-permute-done.4.facing_ref), channel_id=1, source_target_pairs={{0,24},{8,0},{16,8},{24,16},{1,25},{9,1},{17,9},{25,17},{2,26},{10... | collective-permute-start | bytes 786440 | tf_op jit(solution)/shard_map/ppermute | solution.py:270
  110.4 7.2 %collective-permute-done.6 = bf16[64,2048]{1,0:T(8,128)(2,1)S(1)} collective-permute-done((bf16[64,2048]{1,0:T(8,128)(2,1)}, bf16[64,2048]{1,0:T(8,128)(2,1)S(1)}, u32[]{:S(2)}, u32[]{:S(2)}) %collective-permute-start.6) | collective-permute-done | bytes 262176 | tf_op jit(solution)/shard_map/ppermute | solution.py:270
  117.6 3.1 %collective-permute-start.8 = (bf16[32,2048]{1,0:T(8,128)(2,1)S(1)}, bf16[32,2048]{1,0:T(8,128)(2,1)S(1)}, u32[]{:S(2)}, u32[]{:S(2)}) collective-permute-start(bf16[32,2048]{1,0:T(8,128)(2,1)S(1)} %slice.18), channel_id=1, source_target_pairs={{0,24},{8,0},{16,8},{24,16},{1,25},{9,1},{17,9},{25,17},{2,26},{10... | collective-permute-start | bytes 393224 | tf_op jit(solution)/shard_map/ppermute | solution.py:273
  123.8 4.3 %collective-permute-done.9 = bf16[32,2048]{1,0:T(8,128)(2,1)S(1)} collective-permute-done((bf16[32,2048]{1,0:T(8,128)(2,1)S(1)}, bf16[32,2048]{1,0:T(8,128)(2,1)S(1)}, u32[]{:S(2)}, u32[]{:S(2)}) %collective-permute-start.9) | collective-permute-done | bytes 131104 | tf_op jit(solution)/shard_map/ppermute | solution.py:273
  128.1 4.0 %collective-permute-start.10 = (bf16[256,2048]{1,0:T(8,128)(2,1)S(1)}, bf16[256,2048]{1,0:T(8,128)(2,1)}, u32[]{:S(2)}, u32[]{:S(2)}) collective-permute-start(bf16[256,2048]{1,0:T(8,128)(2,1)S(1)} %constant_dynamic-update-slice_fusion.5.facing_ref.refs_2_), channel_id=1, source_target_pairs={{0,4},{4,0},{1,5},{5,1},{2,6},{6,2},{3,7},{7,3},{8,12},{12,8},{9,1... | collective-permute-start | bytes 3145736 | tf_op jit(solution)/shard_map/ppermute | solution.py:282
  137.2 3.6 %all-to-all-start.3 = ((bf16[4,16,2176]{2,1,0:T(8,128)(2,1)}), bf16[4,16,2176]{2,1,0:T(8,128)(2,1)S(1)}, u32[]{:S(2)}, u32[]{:S(2)}) async-start(bf16[4,16,2176]{2,1,0:T(8,128)(2,1)} %bitcast.11), calls=%async_computation.3 | async-start | bytes 557056 | tf_op jit(solution)/shard_map/all_to_all | solution.py:324
  147.6 7.7 %all-to-all-done.3 = bf16[4,16,2176]{2,1,0:T(8,128)(2,1)S(1)} async-done(((bf16[4,16,2176]{2,1,0:T(8,128)(2,1)}), bf16[4,16,2176]{2,1,0:T(8,128)(2,1)S(1)}, u32[]{:S(2)}, u32[]{:S(2)}) %all-to-all-start.3) | async-done | bytes 278560 | tf_op jit(solution)/shard_map/all_to_all | solution.py:324
  156.4 19.5 %all_to_all.53 = bf16[4,16,2048]{2,1,0:T(8,128)(2,1)S(1)} all-to-all(bf16[4,16,2048]{2,1,0:T(8,128)(2,1)S(1)} %broadcast_in_dim.61), channel_id=1, replica_groups=mesh['zh'=4,'zp'=2,'zq'=2,'y'=4,'c'=2,'kv'=4] {'zh'}, dimensions={0} | all-to-all | bytes 524288 | tf_op jit(solution)/shard_map/all_to_all | solution.py:245
  175.9 13.5 %collective-permute-start.11 = (bf16[64,2048]{1,0:T(8,128)(2,1)S(1)}, bf16[64,2048]{1,0:T(8,128)(2,1)S(1)}, u32[]{:S(2)}, u32[]{:S(2)}) collective-permute-start(bf16[64,2048]{1,0:T(8,128)(2,1)S(1)} %bitcast.45), channel_id=1, source_target_pairs={{0,32},{32,0},{1,33},{33,1},{2,34},{34,2},{3,35},{35,3},{4,36},{36... | collective-permute-start | bytes 786440 | tf_op jit(solution)/shard_map/ppermute | solution.py:335
  189.4 4.9 %collective-permute-done.11 = bf16[64,2048]{1,0:T(8,128)(2,1)S(1)} collective-permute-done((bf16[64,2048]{1,0:T(8,128)(2,1)S(1)}, bf16[64,2048]{1,0:T(8,128)(2,1)S(1)}, u32[]{:S(2)}, u32[]{:S(2)}) %collective-permute-start.11) | collective-permute-done | bytes 262176 | tf_op jit(solution)/shard_map/ppermute | solution.py:335
  198.2 4.0 %all-to-all-start.5 = ((f32[4,16,16,128]{3,2,1,0:T(8,128)}), f32[4,16,16,128]{3,2,1,0:T(8,128)S(1)}, u32[]{:S(2)}, u32[]{:S(2)}) async-start(f32[4,16,16,128]{3,2,1,0:T(8,128)} %copy-done.4), calls=%async_computation.5 | async-start | bytes 1048576 | tf_op jit(solution)/shard_map/all_to_all | solution.py:347
  202.3 6.9 %all-to-all-done.5.terms_ref = f32[4,16,16,128]{3,2,1,0:T(8,128)S(1)} async-done(((f32[4,16,16,128]{3,2,1,0:T(8,128)}), f32[4,16,16,128]{3,2,1,0:T(8,128)S(1)}, u32[]{:S(2)}, u32[]{:S(2)}) %all-to-all-start.5) | async-done | bytes 524320 | tf_op jit(solution)/shard_map/all_to_all | solution.py:347
  210.3 7.2 %all-to-all-start.6 = ((bf16[16,16,128]{2,1,0:T(8,128)(2,1)}), bf16[16,16,128]{2,1,0:T(8,128)(2,1)S(1)}, u32[]{:S(2)}, u32[]{:S(2)}) async-start(bf16[16,16,128]{2,1,0:T(8,128)(2,1)} %sum.1), calls=%async_computation.6 | async-start | bytes 131072 | tf_op jit(solution)/shard_map/all_to_all | solution.py:357
  217.5 6.7 %all-to-all-done.6.parts_ref = bf16[16,16,128]{2,1,0:T(8,128)(2,1)S(1)} async-done(((bf16[16,16,128]{2,1,0:T(8,128)(2,1)}), bf16[16,16,128]{2,1,0:T(8,128)(2,1)S(1)}, u32[]{:S(2)}, u32[]{:S(2)}) %all-to-all-start.6) | async-done | bytes 65568 | tf_op jit(solution)/shard_map/all_to_all | solution.py:357
  (100 shorter events, 46.3 us)
Async XLA Ops:
  0.0 52.6 %copy-start = (bf16[16,128,2,128]{3,2,1,0:T(2,128)(2,1)S(1)}, bf16[16,128,2,128]{3,2,1,0:T(2,128)(2,1)}, u32[]{:S(2)}) copy-start(bf16[16,128,2,128]{3,2,1,0:T(2,128)(2,1)} %param.12) | copy-start | bytes 3145732
  0.0 24.7 %copy-start.19 = (s32[128]{0:T(128)S(1)}, s32[128]{0:T(128)}, u32[]{:S(2)}) copy-start(s32[128]{0:T(128)} %param.17) | copy-start | bytes 1540
  2.5 30.2 %all-to-all-start = ((bf16[4,16,2176]{2,1,0:T(8,128)(2,1)}), bf16[4,16,2176]{2,1,0:T(8,128)(2,1)S(1)}, u32[]{:S(2)}, u32[]{:S(2)}) async-start(bf16[4,16,2176]{2,1,0:T(8,128)(2,1)} %broadcast_in_dim.58), calls=%async_computation | async-start | bytes 557056 | tf_op jit(solution)/shard_map/all_to_all | solution.py:245
  18.1 9.6 %collective-permute-start = (bf16[64,2048]{1,0:T(8,128)(2,1)}, bf16[64,2048]{1,0:T(8,128)(2,1)S(1)}, u32[]{:S(2)}, u32[]{:S(2)}) collective-permute-start(bf16[64,2048]{1,0:T(8,128)(2,1)} %bitcast.5), channel_id=1, source_target_pairs={{0,24},{8,0},{16,8},{24,16},{1,25},{9,1},{17,9},{25,17},{2,26},{10... | collective-permute-start | bytes 786440 | tf_op jit(solution)/shard_map/ppermute | solution.py:270
  22.8 9.9 %collective-permute-start.1 = (bf16[64,2048]{1,0:T(8,128)(2,1)}, bf16[64,2048]{1,0:T(8,128)(2,1)S(1)}, u32[]{:S(2)}, u32[]{:S(2)}) collective-permute-start(bf16[64,2048]{1,0:T(8,128)(2,1)} %bitcast.5), channel_id=1, source_target_pairs={{0,8},{8,16},{16,24},{24,0},{1,9},{9,17},{17,25},{25,1},{2,10},{10... | collective-permute-start | bytes 786440 | tf_op jit(solution)/shard_map/ppermute | solution.py:270
  34.5 18.9 %copy-start.10 = (f32[64,256]{1,0:T(8,128)}, f32[64,256]{1,0:T(8,128)S(1)}, u32[]{:S(2)}) copy-start(f32[64,256]{1,0:T(8,128)S(1)} %get-tuple-element.8.select_ref) | copy-start | bytes 196612
  34.5 18.2 %copy-start.15 = (bf16[16,16,128]{2,1,0:T(8,128)(2,1)S(1)}, bf16[16,16,128]{2,1,0:T(8,128)(2,1)}, u32[]{:S(2)}) copy-start(bf16[16,16,128]{2,1,0:T(8,128)(2,1)} %param.9) | copy-start | bytes 196612
  34.5 50.7 %all-to-all-start.1 = ((bf16[32,8,2048]{2,1,0:T(8,128)(2,1)}), bf16[32,8,2048]{2,1,0:T(8,128)(2,1)S(1)}, u32[]{:S(2)}, u32[]{:S(2)}) async-start(bf16[32,8,2048]{2,1,0:T(8,128)(2,1)} %bitcast.44), calls=%async_computation.1 | async-start | bytes 2097152 | tf_op jit(solution)/shard_map/all_to_all | solution.py:301
  48.2 37.0 %collective-permute-start.4 = (bf16[64,2048]{1,0:T(8,128)(2,1)}, bf16[64,2048]{1,0:T(8,128)(2,1)}, u32[]{:S(2)}, u32[]{:S(2)}) collective-permute-start(bf16[64,2048]{1,0:T(8,128)(2,1)} %bitcast.5), channel_id=1, source_target_pairs={{0,64},{64,0},{1,65},{65,1},{2,66},{66,2},{3,67},{67,3},{4,68},{68... | collective-permute-start | bytes 786440 | tf_op jit(solution)/shard_map/ppermute | solution.py:277
  57.0 7.5 %collective-permute-start.2 = (bf16[32,2048]{1,0:T(8,128)(2,1)S(1)}, bf16[32,2048]{1,0:T(8,128)(2,1)S(1)}, u32[]{:S(2)}, u32[]{:S(2)}) collective-permute-start(bf16[32,2048]{1,0:T(8,128)(2,1)S(1)} %slice.16), channel_id=1, source_target_pairs={{0,24},{8,0},{16,8},{24,16},{1,25},{9,1},{17,9},{25,17},{2,26},{10... | collective-permute-start | bytes 393224 | tf_op jit(solution)/shard_map/ppermute | solution.py:273
  61.3 8.4 %collective-permute-start.3 = (bf16[32,2048]{1,0:T(8,128)(2,1)S(1)}, bf16[32,2048]{1,0:T(8,128)(2,1)S(1)}, u32[]{:S(2)}, u32[]{:S(2)}) collective-permute-start(bf16[32,2048]{1,0:T(8,128)(2,1)S(1)} %slice.17), channel_id=1, source_target_pairs={{0,8},{8,16},{16,24},{24,0},{1,9},{9,17},{17,25},{25,1},{2,10},{10... | collective-permute-start | bytes 393224 | tf_op jit(solution)/shard_map/ppermute | solution.py:273
  94.0 39.1 %all-to-all-start.2 = ((bf16[32,8,2176]{2,1,0:T(8,128)(2,1)}), bf16[32,8,2176]{2,1,0:T(8,128)(2,1)}, u32[]{:S(2)}, u32[]{:S(2)}) async-start(bf16[32,8,2176]{2,1,0:T(8,128)(2,1)} %bitcast.9), calls=%async_computation.2 | async-start | bytes 2228224 | tf_op jit(solution)/shard_map/all_to_all | solution.py:316
  100.3 17.3 %collective-permute-start.6 = (bf16[64,2048]{1,0:T(8,128)(2,1)}, bf16[64,2048]{1,0:T(8,128)(2,1)S(1)}, u32[]{:S(2)}, u32[]{:S(2)}) collective-permute-start(bf16[64,2048]{1,0:T(8,128)(2,1)} %collective-permute-done.4.facing_ref), channel_id=1, source_target_pairs={{0,24},{8,0},{16,8},{24,16},{1,25},{9,1},{17,9},{25,17},{2,26},{10... | collective-permute-start | bytes 786440 | tf_op jit(solution)/shard_map/ppermute | solution.py:270
  104.8 16.0 %collective-permute-start.7 = (bf16[64,2048]{1,0:T(8,128)(2,1)}, bf16[64,2048]{1,0:T(8,128)(2,1)S(1)}, u32[]{:S(2)}, u32[]{:S(2)}) collective-permute-start(bf16[64,2048]{1,0:T(8,128)(2,1)} %collective-permute-done.4.facing_ref), channel_id=1, source_target_pairs={{0,8},{8,16},{16,24},{24,0},{1,9},{9,17},{17,25},{25,1},{2,10},{10... | collective-permute-start | bytes 786440 | tf_op jit(solution)/shard_map/ppermute | solution.py:270
  107.7 25.4 %copy-start.11 = (f32[64,256]{1,0:T(8,128)S(1)}, f32[64,256]{1,0:T(8,128)}, u32[]{:S(2)}) copy-start(f32[64,256]{1,0:T(8,128)} %copy-done.10) | copy-start | bytes 196612
  107.7 24.4 %collective-permute-start.5 = (bf16[256,2048]{1,0:T(8,128)(2,1)S(1)}, bf16[256,2048]{1,0:T(8,128)(2,1)S(1)}, u32[]{:S(2)}, u32[]{:S(2)}) collective-permute-start(bf16[256,2048]{1,0:T(8,128)(2,1)S(1)} %constant_dynamic-update-slice_fusion.weight_ref.refs_0_), channel_id=1, source_target_pairs={{0,4},{4,0},{1,5},{5,1},{2,6},{6,2},{3,7},{7,3},{8,12},{12,8},{9,1... | collective-permute-start | bytes 3145736 | tf_op jit(solution)/shard_map/ppermute | solution.py:281
  117.6 6.2 %collective-permute-start.8 = (bf16[32,2048]{1,0:T(8,128)(2,1)S(1)}, bf16[32,2048]{1,0:T(8,128)(2,1)S(1)}, u32[]{:S(2)}, u32[]{:S(2)}) collective-permute-start(bf16[32,2048]{1,0:T(8,128)(2,1)S(1)} %slice.18), channel_id=1, source_target_pairs={{0,24},{8,0},{16,8},{24,16},{1,25},{9,1},{17,9},{25,17},{2,26},{10... | collective-permute-start | bytes 393224 | tf_op jit(solution)/shard_map/ppermute | solution.py:273
  120.8 7.3 %collective-permute-start.9 = (bf16[32,2048]{1,0:T(8,128)(2,1)S(1)}, bf16[32,2048]{1,0:T(8,128)(2,1)S(1)}, u32[]{:S(2)}, u32[]{:S(2)}) collective-permute-start(bf16[32,2048]{1,0:T(8,128)(2,1)S(1)} %slice.19), channel_id=1, source_target_pairs={{0,8},{8,16},{16,24},{24,0},{1,9},{9,17},{17,25},{25,1},{2,10},{10... | collective-permute-start | bytes 393224 | tf_op jit(solution)/shard_map/ppermute | solution.py:273
  128.1 19.5 %collective-permute-start.10 = (bf16[256,2048]{1,0:T(8,128)(2,1)S(1)}, bf16[256,2048]{1,0:T(8,128)(2,1)}, u32[]{:S(2)}, u32[]{:S(2)}) collective-permute-start(bf16[256,2048]{1,0:T(8,128)(2,1)S(1)} %constant_dynamic-update-slice_fusion.5.facing_ref.refs_2_), channel_id=1, source_target_pairs={{0,4},{4,0},{1,5},{5,1},{2,6},{6,2},{3,7},{7,3},{8,12},{12,8},{9,1... | collective-permute-start | bytes 3145736 | tf_op jit(solution)/shard_map/ppermute | solution.py:282
  137.2 18.0 %all-to-all-start.3 = ((bf16[4,16,2176]{2,1,0:T(8,128)(2,1)}), bf16[4,16,2176]{2,1,0:T(8,128)(2,1)S(1)}, u32[]{:S(2)}, u32[]{:S(2)}) async-start(bf16[4,16,2176]{2,1,0:T(8,128)(2,1)} %bitcast.11), calls=%async_computation.3 | async-start | bytes 557056 | tf_op jit(solution)/shard_map/all_to_all | solution.py:324
  156.4 38.0 %copy-start.3 = (bf16[256,2048]{1,0:T(8,128)(2,1)S(1)}, bf16[256,2048]{1,0:T(8,128)(2,1)}, u32[]{:S(2)}) copy-start(bf16[256,2048]{1,0:T(8,128)(2,1)} %copy-done.1) | copy-start | bytes 3145732
  175.9 18.4 %collective-permute-start.11 = (bf16[64,2048]{1,0:T(8,128)(2,1)S(1)}, bf16[64,2048]{1,0:T(8,128)(2,1)S(1)}, u32[]{:S(2)}, u32[]{:S(2)}) collective-permute-start(bf16[64,2048]{1,0:T(8,128)(2,1)S(1)} %bitcast.45), channel_id=1, source_target_pairs={{0,32},{32,0},{1,33},{33,1},{2,34},{34,2},{3,35},{35,3},{4,36},{36... | collective-permute-start | bytes 786440 | tf_op jit(solution)/shard_map/ppermute | solution.py:335
  198.2 10.9 %all-to-all-start.5 = ((f32[4,16,16,128]{3,2,1,0:T(8,128)}), f32[4,16,16,128]{3,2,1,0:T(8,128)S(1)}, u32[]{:S(2)}, u32[]{:S(2)}) async-start(f32[4,16,16,128]{3,2,1,0:T(8,128)} %copy-done.4), calls=%async_computation.5 | async-start | bytes 1048576 | tf_op jit(solution)/shard_map/all_to_all | solution.py:347
  210.3 13.9 %all-to-all-start.6 = ((bf16[16,16,128]{2,1,0:T(8,128)(2,1)}), bf16[16,16,128]{2,1,0:T(8,128)(2,1)S(1)}, u32[]{:S(2)}, u32[]{:S(2)}) async-start(bf16[16,16,128]{2,1,0:T(8,128)(2,1)} %sum.1), calls=%async_computation.6 | async-start | bytes 131072 | tf_op jit(solution)/shard_map/all_to_all | solution.py:357
  (15 other events, 42.2 us)

commit v5 on v4

--- a/solution.py
+++ b/solution.py
@@ -7,7 +7,7 @@
 
 ZH, ZP, ZQ, YS, CS, XS = 4, 2, 2, 4, 2, 4
 QUAD = ZP * ZQ * YS * CS
-GROUP = ZP * YS * CS
+GROUP = ZQ * YS * CS
 ROWS = 16
 HEADS = 16
 HD = 128
@@ -20,7 +20,7 @@
 FAR = -1e30
 SCALE = HD ** -0.5
 LOG2E = 1.4426950408889634
-PARAMS = pltpu.CompilerParams(vmem_limit_bytes=40 * 1024 * 1024)
+PARAMS = pltpu.CompilerParams(vmem_limit_bytes=20 * 1024 * 1024)
 
 
 def lanes(shape):
@@ -98,7 +98,7 @@
     out_ref[:, WIDE:] = split_parts(logs).astype(jnp.bfloat16)
 
 
-def gather_kernel(back_ref, select_ref, weight_ref, facing_ref, joined_ref):
+def gather_kernel(back_ref, select_ref, weight_ref, above_ref, below_ref, joined_ref):
     chosen = select_ref[...] > 0.5
     slot_logs = join_parts(back_ref[:, WIDE:].astype(jnp.float32)).T
     lane = lanes((POOL, 128))
@@ -174,7 +174,7 @@
 
 
 def sum_kernel(place_ref, terms_ref, out_ref):
-    for far_side in range(ZP):
+    for far_side in range(ZQ):
         side = place_ref[0] if far_side == 0 else 1 - place_ref[0]
         for far_core in range(CS):
             core = place_ref[2] if far_core == 0 else 1 - place_ref[2]
@@ -187,24 +187,20 @@
                 out_ref[(side * YS + y) * CS + core] = term.astype(jnp.bfloat16)
 
 
-def settle_kernel(place_ref, parts_ref, out_ref):
-    place = place_ref[0]
+def settle_kernel(parts_ref, out_ref):
     lane = lanes((16, 128))
-    for side in range(ZP):
+    for side in range(ZQ):
         parts = [
             parts_ref[side * YS * CS + owner].astype(jnp.float32) for owner in range(YS * CS)
         ]
-        for half in range(ZQ):
-            near = place if half == 0 else 1 - place
-            for far in range(ZH):
-                first = (half * ZH + far) * ROWS
-                tile = jnp.zeros((16, 128), jnp.float32)
-                for owner in range(YS * CS):
-                    shift = (owner * ROWS - first) % 128
-                    moved = parts[owner] if shift == 0 else pltpu.roll(parts[owner], shift, 1)
-                    tile = jnp.where(lane // ROWS == owner, moved, tile)
-                start = ((far * ZP + side) * ZQ + near) * 128
-                out_ref[:, pl.ds(pl.multiple_of(start, 128), 128)] = tile.astype(jnp.bfloat16)
+        for far in range(ZH * ZP):
+            tile = jnp.zeros((16, 128), jnp.float32)
+            for owner in range(YS * CS):
+                shift = (owner - far) * ROWS % 128
+                moved = parts[owner] if shift == 0 else pltpu.roll(parts[owner], shift, 1)
+                tile = jnp.where(lane // ROWS == owner, moved, tile)
+            start = (far * ZQ + side) * 128
+            out_ref[:, start : start + 128] = tile.astype(jnp.bfloat16)
 
 
 def own_partials(queries, own_keys, own_values, lengths):
@@ -236,7 +232,7 @@
 
 def inputs(near, far):
     return [pl.BlockSpec(memory_space=pltpu.VMEM)] * near + [
-        pl.BlockSpec(memory_space=pltpu.HBM)
+        pl.BlockSpec(memory_space=pl.ANY)
     ] * far
 
 
@@ -274,10 +270,11 @@
         return jnp.concatenate([block, above, below] + across, axis=0)
 
     turned = out_weight.T
-    facing = lax.ppermute(turned, "zp", swap)
+    facing = lax.ppermute(turned, "zq", swap)
     above, below = beside(turned)
     mine = piece_of(turned, above, below)
-    mine_far = piece_of(facing, *beside(facing))
+    above_far, below_far = beside(facing)
+    mine_far = piece_of(facing, above_far, below_far)
     other = lax.ppermute(mine, "c", swap)
     other_far = lax.ppermute(mine_far, "c", swap)
     own_out, own_log = own_partials(queries, suffix_keys, suffix_values, suffix_lengths)
@@ -316,11 +313,11 @@
     back = lax.all_to_all(partials, quad, split_axis=0, concat_axis=0, tiled=True)
     joined = pl.pallas_call(
         gather_kernel,
-        in_specs=inputs(2, 2),
+        in_specs=inputs(2, 3),
         out_shape=packed(POOL),
         compiler_params=PARAMS,
         name="gather",
-    )(back, select, other, mine_far)
+    )(back, select, other, above_far, below_far)
     far = lax.all_to_all(joined, "zh", split_axis=0, concat_axis=0, tiled=True)
 
     attended = pl.pallas_call(
@@ -329,39 +326,39 @@
         out_shape=jax.ShapeDtypeStruct((ROWS, WIDE), jnp.bfloat16),
         compiler_params=PARAMS,
         name="final",
-    )(far, own_out, jnp.pad(own_log, ((0, 0), (0, 112))), other_far)
-
-    rows = spread_along(attended, "zh", ZH)
-    rows = jnp.concatenate([rows, lax.ppermute(rows, "zq", swap)], axis=0)
+    )(far, own_out, jnp.pad(own_log, ((0, 0), (0, 112))), mine_far)
+
+    rows = spread_along(attended, ("zh", "zp"), ZH * ZP)
     terms = pl.pallas_call(
         project_kernel,
         in_specs=inputs(1, 4),
-        out_shape=jax.ShapeDtypeStruct((XS, GROUP, 16, ZQ * POOL), jnp.float32),
+        out_shape=jax.ShapeDtypeStruct((XS, GROUP, 16, ZP * POOL), jnp.float32),
         scratch_shapes=[
-            pltpu.VMEM((4, GROUP * 64 // 4, WIDE), jnp.bfloat16),
+            pltpu.VMEM((4, YS * 64, WIDE), jnp.bfloat16),
             pltpu.SemaphoreType.DMA((4,)),
         ],
         compiler_params=PARAMS,
         name="project",
     )(rows, mine, other, mine_far, other_far)
     terms = lax.all_to_all(terms, "kv", split_axis=0, concat_axis=0, tiled=True)
-    one = [pl.BlockSpec(memory_space=pltpu.SMEM), pl.BlockSpec(memory_space=pltpu.VMEM)]
-    place = jnp.stack([lax.axis_index(axis) for axis in ("zp", "y", "c")]).astype(jnp.int32)
+    place = jnp.stack([lax.axis_index(axis) for axis in ("zq", "y", "c")]).astype(jnp.int32)
     parts = pl.pallas_call(
         sum_kernel,
-        in_specs=one,
-        out_shape=jax.ShapeDtypeStruct((GROUP, 16, ZQ * POOL), jnp.bfloat16),
+        in_specs=[
+            pl.BlockSpec(memory_space=pltpu.SMEM),
+            pl.BlockSpec(memory_space=pltpu.VMEM),
+        ],
+        out_shape=jax.ShapeDtypeStruct((GROUP, 16, ZP * POOL), jnp.bfloat16),
         compiler_params=PARAMS,
         name="sum",
     )(place, terms)
-    parts = lax.all_to_all(parts, ("zp", "y", "c"), split_axis=0, concat_axis=0, tiled=True)
+    parts = lax.all_to_all(parts, ("zq", "y", "c"), split_axis=0, concat_axis=0, tiled=True)
     return pl.pallas_call(
         settle_kernel,
-        in_specs=one,
         out_shape=jax.ShapeDtypeStruct((16, ZH * QUAD * ROWS), jnp.bfloat16),
         compiler_params=PARAMS,
         name="settle",
-    )(lax.axis_index("zq").reshape(1).astype(jnp.int32), parts).T
+    )(parts).T
 
 
 def solution(mesh):

time: 227 us -> 216 us (0.952)
  starting transfers between devices: 99.4 us -> 87 us
  blocking collectives: 19.5 us -> 24.7 us
  waiting for transfers between devices: 68 us -> 63.6 us
    ppermute x2 -> x1, waiting for transfers between devices: 20.4 us -> 2.78 us  [on_device(): facing = lax.ppermute(turned, 'zq', swap)]
    ppermute x2 -> x1, starting transfers between devices: 17.8 us -> 3.43 us  [on_device(): facing = lax.ppermute(turned, 'zq', swap)]
    all_to_all x1 -> x2, waiting for transfers between devices: 0.01 us -> 13.1 us  [spread_along(): lax.all_to_all(copies, axis, split_axis=0, concat_axis=0, tiled=True)]
    all_to_all x1 -> x2, starting transfers between devices: 15.6 us -> 24.3 us  [spread_along(): lax.all_to_all(copies, axis, split_axis=0, concat_axis=0, tiled=True)]
    all_to_all x1 -> x0, starting transfers between devices: 7.2 us -> none  [on_device(): lax.all_to_all(parts, ('zp', 'y', 'c'), split_axis=0, concat_axis=0, tile...]
    all_to_all x1 -> x0, waiting for transfers between devices: 6.72 us -> none  [on_device(): lax.all_to_all(parts, ('zp', 'y', 'c'), split_axis=0, concat_axis=0, tile...]
    ppermute x2, waiting for transfers between devices: 9.43 us -> 3.9 us  [piece_of(): lax.ppermute(below[32:], 'y', up)]
    all_to_all x1, blocking collectives: 19.5 us -> 24.7 us  [on_device(): lax.all_to_all(parts, ('zq', 'y', 'c'), split_axis=0, concat_axis=0, tile...]
  transfers between devices with their start and end apart: 18 -> 17, of which waited for: 12 -> 12; matrix products, arithmetic and copies ran while one was open for 5% -> 5% of each run, Pallas kernels for 1% -> 1%
where the time goes in v5:
time: 216 us; the launch traced here: 215 us
  starting transfers between devices  87 us (40%)
  waiting for transfers between devices  63.6 us (29%)
  blocking collectives  24.7 us (11%)
  local copies, waits for them, and re-layouts  19.3 us (9%)
  Pallas kernels  16.9 us (8%)
    all_to_all x1, blocking collectives, on_device(): lax.all_to_all(parts, ('zq', 'y', 'c'), split_axis=0, concat_axis=0, tile...  24.7 us
    all_to_all x2, starting transfers between devices, spread_along(): lax.all_to_all(copies, axis, split_axis=0, concat_axis=0, tiled=True)  24.3 us
    ppermute x4, waiting for transfers between devices, beside(): return (lax.ppermute(block, 'y', down), lax.ppermute(block, 'y', up))  15.1 us
    all_to_all x1, starting transfers between devices, on_device(): lax.all_to_all(outgoing, quad, split_axis=0, concat_axis=0, tiled=True)  13.7 us
    unnamed x51, local copies, waits for them, and re-layouts  13.3 us
    all_to_all x2, waiting for transfers between devices, spread_along(): lax.all_to_all(copies, axis, split_axis=0, concat_axis=0, tiled=True)  13.1 us
    ppermute x4, starting transfers between devices, beside(): return (lax.ppermute(block, 'y', down), lax.ppermute(block, 'y', up))  13 us
    all_to_all x1, waiting for transfers between devices, on_device(): far = lax.all_to_all(joined, 'zh', split_axis=0, concat_axis=0, tiled=True)  12 us
  transfers between devices with their start and end apart: 17, of which 12 were waited for; matrix products, arithmetic and copies ran while one was open for 5% of the time, Pallas kernels for 1%

profile of v5, /device:TPU:1, one launch (start us, length us, event | category | flops | bytes accessed | tf_op | source)
XLA Modules:
  0.0 214.5 jit_solution(17784351936090059545)
XLA Ops:
  2.5 15.6 %all-to-all-start = ((bf16[4,16,2176]{2,1,0:T(8,128)(2,1)}), bf16[4,16,2176]{2,1,0:T(8,128)(2,1)S(1)}, u32[]{:S(2)}, u32[]{:S(2)}) async-start(bf16[4,16,2176]{2,1,0:T(8,128)(2,1)} %broadcast_in_dim.58), calls=%async_computation | async-start | bytes 557056 | tf_op jit(solution)/shard_map/all_to_all | solution.py:241
  18.1 4.6 %collective-permute-start = (bf16[64,2048]{1,0:T(8,128)(2,1)}, bf16[64,2048]{1,0:T(8,128)(2,1)S(1)}, u32[]{:S(2)}, u32[]{:S(2)}) collective-permute-start(bf16[64,2048]{1,0:T(8,128)(2,1)} %bitcast.4), channel_id=1, source_target_pairs={{0,24},{8,0},{16,8},{24,16},{1,25},{9,1},{17,9},{25,17},{2,26},{10... | collective-permute-start | bytes 786440 | tf_op jit(solution)/shard_map/ppermute | solution.py:266
  24.9 2.8 %collective-permute-done.above_ref = bf16[64,2048]{1,0:T(8,128)(2,1)S(1)} collective-permute-done((bf16[64,2048]{1,0:T(8,128)(2,1)}, bf16[64,2048]{1,0:T(8,128)(2,1)S(1)}, u32[]{:S(2)}, u32[]{:S(2)}) %collective-permute-start) | collective-permute-done | bytes 262176 | tf_op jit(solution)/shard_map/ppermute | solution.py:266
  27.7 4.9 %collective-permute-done.1.below_ref = bf16[64,2048]{1,0:T(8,128)(2,1)S(1)} collective-permute-done((bf16[64,2048]{1,0:T(8,128)(2,1)}, bf16[64,2048]{1,0:T(8,128)(2,1)S(1)}, u32[]{:S(2)}, u32[]{:S(2)}) %collective-permute-start.1) | collective-permute-done | bytes 262176 | tf_op jit(solution)/shard_map/ppermute | solution.py:266
  34.5 13.7 %all-to-all-start.1 = ((bf16[32,8,2048]{2,1,0:T(8,128)(2,1)}), bf16[32,8,2048]{2,1,0:T(8,128)(2,1)S(1)}, u32[]{:S(2)}, u32[]{:S(2)}) async-start(bf16[32,8,2048]{2,1,0:T(8,128)(2,1)} %bitcast.43), calls=%async_computation.1 | async-start | bytes 2097152 | tf_op jit(solution)/shard_map/all_to_all | solution.py:298
  48.2 3.4 %collective-permute-start.4 = (bf16[64,2048]{1,0:T(8,128)(2,1)}, bf16[64,2048]{1,0:T(8,128)(2,1)}, u32[]{:S(2)}, u32[]{:S(2)}) collective-permute-start(bf16[64,2048]{1,0:T(8,128)(2,1)} %bitcast.4), channel_id=1, source_target_pairs={{0,32},{32,0},{1,33},{33,1},{2,34},{34,2},{3,35},{35,3},{4,36},{36... | collective-permute-start | bytes 786440 | tf_op jit(solution)/shard_map/ppermute | solution.py:273
  56.0 4.3 %collective-permute-start.2 = (bf16[32,2048]{1,0:T(8,128)(2,1)S(1)}, bf16[32,2048]{1,0:T(8,128)(2,1)S(1)}, u32[]{:S(2)}, u32[]{:S(2)}) collective-permute-start(bf16[32,2048]{1,0:T(8,128)(2,1)S(1)} %slice.16), channel_id=1, source_target_pairs={{0,24},{8,0},{16,8},{24,16},{1,25},{9,1},{17,9},{25,17},{2,26},{10... | collective-permute-start | bytes 393224 | tf_op jit(solution)/shard_map/ppermute | solution.py:269
  64.4 3.9 %collective-permute-done.3 = bf16[32,2048]{1,0:T(8,128)(2,1)S(1)} collective-permute-done((bf16[32,2048]{1,0:T(8,128)(2,1)S(1)}, bf16[32,2048]{1,0:T(8,128)(2,1)S(1)}, u32[]{:S(2)}, u32[]{:S(2)}) %collective-permute-start.3) | collective-permute-done | bytes 131104 | tf_op jit(solution)/shard_map/ppermute | solution.py:269
  68.3 2.8 %collective-permute-done.4.facing_ref = bf16[64,2048]{1,0:T(8,128)(2,1)} collective-permute-done((bf16[64,2048]{1,0:T(8,128)(2,1)}, bf16[64,2048]{1,0:T(8,128)(2,1)}, u32[]{:S(2)}, u32[]{:S(2)}) %collective-permute-start.4) | collective-permute-done | bytes 262176 | tf_op jit(solution)/shard_map/ppermute | solution.py:273
  71.1 3.6 %all-to-all-done.1 = bf16[32,8,2048]{2,1,0:T(8,128)(2,1)S(1)} async-done(((bf16[32,8,2048]{2,1,0:T(8,128)(2,1)}), bf16[32,8,2048]{2,1,0:T(8,128)(2,1)S(1)}, u32[]{:S(2)}, u32[]{:S(2)}) %all-to-all-start.1) | async-done | bytes 1048608 | tf_op jit(solution)/shard_map/all_to_all | solution.py:298
  76.8 6.8 %attend.1 = bf16[256,2176]{1,0:T(8,128)(2,1)} custom-call(bf16[256,2048]{1,0:T(8,128)(2,1)S(1)} %bitcast.38, bf16[1024,256]{1,0:T(8,128)(2,1)S(1)} %copy-done.3, bf16[1024,256]{1,0:T(8,128)(2,1)S(1)} %copy-done.2, bf16[256,2048]{1,0:T(8,128)(2,1)S(1)} %constant_dynamic-update-slice_fusion.weight_ref.refs_0_, ...), custom_call_target="tpu_custom_call" | custom-call | tf_op jit(solution)/shard_map/attend/pallas_call | solution.py:299
  83.6 5.6 %all-to-all-start.2 = ((bf16[32,8,2176]{2,1,0:T(8,128)(2,1)}), bf16[32,8,2176]{2,1,0:T(8,128)(2,1)}, u32[]{:S(2)}, u32[]{:S(2)}) async-start(bf16[32,8,2176]{2,1,0:T(8,128)(2,1)} %bitcast.8), calls=%async_computation.2 | async-start | bytes 2228224 | tf_op jit(solution)/shard_map/all_to_all | solution.py:313
  91.6 4.6 %collective-permute-start.6 = (bf16[64,2048]{1,0:T(8,128)(2,1)}, bf16[64,2048]{1,0:T(8,128)(2,1)S(1)}, u32[]{:S(2)}, u32[]{:S(2)}) collective-permute-start(bf16[64,2048]{1,0:T(8,128)(2,1)} %collective-permute-done.4.facing_ref), channel_id=1, source_target_pairs={{0,24},{8,0},{16,8},{24,16},{1,25},{9,1},{17,9},{25,17},{2,26},{10... | collective-permute-start | bytes 786440 | tf_op jit(solution)/shard_map/ppermute | solution.py:266
  99.1 7.4 %collective-permute-done.6.above_ref = bf16[64,2048]{1,0:T(8,128)(2,1)S(1)} collective-permute-done((bf16[64,2048]{1,0:T(8,128)(2,1)}, bf16[64,2048]{1,0:T(8,128)(2,1)S(1)}, u32[]{:S(2)}, u32[]{:S(2)}) %collective-permute-start.6) | collective-permute-done | bytes 262176 | tf_op jit(solution)/shard_map/ppermute | solution.py:266
  107.2 4.5 %collective-permute-start.8 = (bf16[32,2048]{1,0:T(8,128)(2,1)}, bf16[32,2048]{1,0:T(8,128)(2,1)}, u32[]{:S(2)}, u32[]{:S(2)}) collective-permute-start(bf16[32,2048]{1,0:T(8,128)(2,1)} %slice.18), channel_id=1, source_target_pairs={{0,24},{8,0},{16,8},{24,16},{1,25},{9,1},{17,9},{25,17},{2,26},{10... | collective-permute-start | bytes 393224 | tf_op jit(solution)/shard_map/ppermute | solution.py:269
  120.8 4.1 %all-to-all-start.3 = ((bf16[4,16,2176]{2,1,0:T(8,128)(2,1)}), bf16[4,16,2176]{2,1,0:T(8,128)(2,1)}, u32[]{:S(2)}, u32[]{:S(2)}) async-start(bf16[4,16,2176]{2,1,0:T(8,128)(2,1)} %bitcast.41), calls=%async_computation.3 | async-start | bytes 557056 | tf_op jit(solution)/shard_map/all_to_all | solution.py:321
  127.8 12.0 %all-to-all-done.3 = bf16[4,16,2176]{2,1,0:T(8,128)(2,1)} async-done(((bf16[4,16,2176]{2,1,0:T(8,128)(2,1)}), bf16[4,16,2176]{2,1,0:T(8,128)(2,1)}, u32[]{:S(2)}, u32[]{:S(2)}) %all-to-all-start.3) | async-done | bytes 278560 | tf_op jit(solution)/shard_map/all_to_all | solution.py:321
  141.9 8.7 %all-to-all-start.4 = ((bf16[8,16,2048]{2,1,0:T(8,128)(2,1)}), bf16[8,16,2048]{2,1,0:T(8,128)(2,1)}, u32[]{:S(2)}, u32[]{:S(2)}) async-start(bf16[8,16,2048]{2,1,0:T(8,128)(2,1)} %broadcast_in_dim.61), calls=%async_computation.4 | async-start | bytes 1048576 | tf_op jit(solution)/shard_map/all_to_all | solution.py:241
  150.6 4.1 %collective-permute-start.10 = (bf16[256,2048]{1,0:T(8,128)(2,1)S(1)}, bf16[256,2048]{1,0:T(8,128)(2,1)S(1)}, u32[]{:S(2)}, u32[]{:S(2)}) collective-permute-start(bf16[256,2048]{1,0:T(8,128)(2,1)S(1)} %constant_dynamic-update-slice_fusion.5.weight_ref.refs_2_), channel_id=1, source_target_pairs={{0,4},{4,0},{1,5},{5,1},{2,6},{6,2},{3,7},{7,3},{8,12},{12,8},{9,1... | collective-permute-start | bytes 3145736 | tf_op jit(solution)/shard_map/ppermute | solution.py:279
  157.9 13.1 %all-to-all-done.4 = bf16[8,16,2048]{2,1,0:T(8,128)(2,1)} async-done(((bf16[8,16,2048]{2,1,0:T(8,128)(2,1)}), bf16[8,16,2048]{2,1,0:T(8,128)(2,1)}, u32[]{:S(2)}, u32[]{:S(2)}) %all-to-all-start.4) | async-done | bytes 524320 | tf_op jit(solution)/shard_map/all_to_all | solution.py:241
  172.2 4.4 %project.1 = f32[4,16,16,128]{3,2,1,0:T(8,128)S(1)} custom-call(bf16[128,2048]{1,0:T(8,128)(2,1)} %bitcast.13.rows_ref, bf16[256,2048]{1,0:T(8,128)(2,1)S(1)} %constant_dynamic-update-slice_fusion.weight_ref.refs_0_, bf16[256,2048]{1,0:T(8,128)(2,1)} %collective-permute-done.5.weight_ref.refs_1_, ...), custom_call_target="tpu_custom_call" | custom-call | tf_op jit(solution)/shard_map/project/pallas_call | solution.py:332
  177.4 4.0 %all-to-all-start.5 = ((f32[4,16,16,128]{3,2,1,0:T(8,128)}), f32[4,16,16,128]{3,2,1,0:T(8,128)S(1)}, u32[]{:S(2)}, u32[]{:S(2)}) async-start(f32[4,16,16,128]{3,2,1,0:T(8,128)} %copy-done.1), calls=%async_computation.5 | async-start | bytes 1048576 | tf_op jit(solution)/shard_map/all_to_all | solution.py:343
  181.5 6.9 %all-to-all-done.5.terms_ref = f32[4,16,16,128]{3,2,1,0:T(8,128)S(1)} async-done(((f32[4,16,16,128]{3,2,1,0:T(8,128)}), f32[4,16,16,128]{3,2,1,0:T(8,128)S(1)}, u32[]{:S(2)}, u32[]{:S(2)}) %all-to-all-start.5) | async-done | bytes 524320 | tf_op jit(solution)/shard_map/all_to_all | solution.py:343
  189.0 24.7 %all_to_all.53.parts_ref = bf16[16,16,128]{2,1,0:T(8,128)(2,1)S(1)} all-to-all(bf16[16,16,128]{2,1,0:T(8,128)(2,1)S(1)} %sum.1), channel_id=1, replica_groups=mesh['zh'=4,'zp'=2,'zq'=2,'y'=4,'c'=2,'kv'=4] {'zq','y','c'}, dimensions={0} | all-to-all | bytes 131072 | tf_op jit(solution)/shard_map/all_to_all | solution.py:355
  (95 shorter events, 43.7 us)
Async XLA Ops:
  0.0 51.7 %copy-start = (bf16[16,128,2,128]{3,2,1,0:T(2,128)(2,1)S(1)}, bf16[16,128,2,128]{3,2,1,0:T(2,128)(2,1)}, u32[]{:S(2)}) copy-start(bf16[16,128,2,128]{3,2,1,0:T(2,128)(2,1)} %param.12) | copy-start | bytes 3145732
  0.0 24.7 %copy-start.18 = (s32[128]{0:T(128)S(1)}, s32[128]{0:T(128)}, u32[]{:S(2)}) copy-start(s32[128]{0:T(128)} %param.17) | copy-start | bytes 1540
  2.5 30.2 %all-to-all-start = ((bf16[4,16,2176]{2,1,0:T(8,128)(2,1)}), bf16[4,16,2176]{2,1,0:T(8,128)(2,1)S(1)}, u32[]{:S(2)}, u32[]{:S(2)}) async-start(bf16[4,16,2176]{2,1,0:T(8,128)(2,1)} %broadcast_in_dim.58), calls=%async_computation | async-start | bytes 557056 | tf_op jit(solution)/shard_map/all_to_all | solution.py:241
  18.1 9.6 %collective-permute-start = (bf16[64,2048]{1,0:T(8,128)(2,1)}, bf16[64,2048]{1,0:T(8,128)(2,1)S(1)}, u32[]{:S(2)}, u32[]{:S(2)}) collective-permute-start(bf16[64,2048]{1,0:T(8,128)(2,1)} %bitcast.4), channel_id=1, source_target_pairs={{0,24},{8,0},{16,8},{24,16},{1,25},{9,1},{17,9},{25,17},{2,26},{10... | collective-permute-start | bytes 786440 | tf_op jit(solution)/shard_map/ppermute | solution.py:266
  22.8 9.9 %collective-permute-start.1 = (bf16[64,2048]{1,0:T(8,128)(2,1)}, bf16[64,2048]{1,0:T(8,128)(2,1)S(1)}, u32[]{:S(2)}, u32[]{:S(2)}) collective-permute-start(bf16[64,2048]{1,0:T(8,128)(2,1)} %bitcast.4), channel_id=1, source_target_pairs={{0,8},{8,16},{16,24},{24,0},{1,9},{9,17},{17,25},{25,1},{2,10},{10... | collective-permute-start | bytes 786440 | tf_op jit(solution)/shard_map/ppermute | solution.py:266
  34.4 18.0 %copy-start.10 = (f32[64,256]{1,0:T(8,128)}, f32[64,256]{1,0:T(8,128)S(1)}, u32[]{:S(2)}) copy-start(f32[64,256]{1,0:T(8,128)S(1)} %get-tuple-element.8.select_ref) | copy-start | bytes 196612
  34.4 17.2 %copy-start.17 = (s32[16]{0:T(128)S(1)}, s32[16]{0:T(128)}, u32[]{:S(2)}) copy-start(s32[16]{0:T(128)} %param.16) | copy-start | bytes 196
  34.4 17.3 %copy-start.14 = (bf16[16,16,128]{2,1,0:T(8,128)(2,1)S(1)}, bf16[16,16,128]{2,1,0:T(8,128)(2,1)}, u32[]{:S(2)}) copy-start(bf16[16,16,128]{2,1,0:T(8,128)(2,1)} %param.9) | copy-start | bytes 196612
  34.5 40.3 %all-to-all-start.1 = ((bf16[32,8,2048]{2,1,0:T(8,128)(2,1)}), bf16[32,8,2048]{2,1,0:T(8,128)(2,1)S(1)}, u32[]{:S(2)}, u32[]{:S(2)}) async-start(bf16[32,8,2048]{2,1,0:T(8,128)(2,1)} %bitcast.43), calls=%async_computation.1 | async-start | bytes 2097152 | tf_op jit(solution)/shard_map/all_to_all | solution.py:298
  48.2 22.9 %collective-permute-start.4 = (bf16[64,2048]{1,0:T(8,128)(2,1)}, bf16[64,2048]{1,0:T(8,128)(2,1)}, u32[]{:S(2)}, u32[]{:S(2)}) collective-permute-start(bf16[64,2048]{1,0:T(8,128)(2,1)} %bitcast.4), channel_id=1, source_target_pairs={{0,32},{32,0},{1,33},{33,1},{2,34},{34,2},{3,35},{35,3},{4,36},{36... | collective-permute-start | bytes 786440 | tf_op jit(solution)/shard_map/ppermute | solution.py:273
  53.9 6.4 %copy-start.5 = (bf16[64,2048]{1,0:T(8,128)(2,1)S(1)}, bf16[64,2048]{1,0:T(8,128)(2,1)}, u32[]{:S(2)}) copy-start(bf16[64,2048]{1,0:T(8,128)(2,1)} %copy-done.4) | copy-start | bytes 786436
  56.0 8.4 %collective-permute-start.2 = (bf16[32,2048]{1,0:T(8,128)(2,1)S(1)}, bf16[32,2048]{1,0:T(8,128)(2,1)S(1)}, u32[]{:S(2)}, u32[]{:S(2)}) collective-permute-start(bf16[32,2048]{1,0:T(8,128)(2,1)S(1)} %slice.16), channel_id=1, source_target_pairs={{0,24},{8,0},{16,8},{24,16},{1,25},{9,1},{17,9},{25,17},{2,26},{10... | collective-permute-start | bytes 393224 | tf_op jit(solution)/shard_map/ppermute | solution.py:269
  60.4 8.0 %collective-permute-start.3 = (bf16[32,2048]{1,0:T(8,128)(2,1)S(1)}, bf16[32,2048]{1,0:T(8,128)(2,1)S(1)}, u32[]{:S(2)}, u32[]{:S(2)}) collective-permute-start(bf16[32,2048]{1,0:T(8,128)(2,1)S(1)} %slice.17), channel_id=1, source_target_pairs={{0,8},{8,16},{16,24},{24,0},{1,9},{9,17},{17,25},{25,1},{2,10},{10... | collective-permute-start | bytes 393224 | tf_op jit(solution)/shard_map/ppermute | solution.py:269
  83.6 7.8 %copy-start.16 = (f32[16,2,8]{2,1,0:T(2,128)S(1)}, f32[16,2,8]{2,1,0:T(2,128)}, u32[]{:S(2)}) copy-start(f32[16,2,8]{2,1,0:T(2,128)} %copy-done.15) | copy-start | bytes 3076
  83.6 33.5 %all-to-all-start.2 = ((bf16[32,8,2176]{2,1,0:T(8,128)(2,1)}), bf16[32,8,2176]{2,1,0:T(8,128)(2,1)}, u32[]{:S(2)}, u32[]{:S(2)}) async-start(bf16[32,8,2176]{2,1,0:T(8,128)(2,1)} %bitcast.8), calls=%async_computation.2 | async-start | bytes 2228224 | tf_op jit(solution)/shard_map/all_to_all | solution.py:313
  89.2 25.9 %collective-permute-start.5 = (bf16[256,2048]{1,0:T(8,128)(2,1)S(1)}, bf16[256,2048]{1,0:T(8,128)(2,1)}, u32[]{:S(2)}, u32[]{:S(2)}) collective-permute-start(bf16[256,2048]{1,0:T(8,128)(2,1)S(1)} %constant_dynamic-update-slice_fusion.weight_ref.refs_0_), channel_id=1, source_target_pairs={{0,4},{4,0},{1,5},{5,1},{2,6},{6,2},{3,7},{7,3},{8,12},{12,8},{9,1... | collective-permute-start | bytes 3145736 | tf_op jit(solution)/shard_map/ppermute | solution.py:278
  91.6 14.9 %collective-permute-start.6 = (bf16[64,2048]{1,0:T(8,128)(2,1)}, bf16[64,2048]{1,0:T(8,128)(2,1)S(1)}, u32[]{:S(2)}, u32[]{:S(2)}) collective-permute-start(bf16[64,2048]{1,0:T(8,128)(2,1)} %collective-permute-done.4.facing_ref), channel_id=1, source_target_pairs={{0,24},{8,0},{16,8},{24,16},{1,25},{9,1},{17,9},{25,17},{2,26},{10... | collective-permute-start | bytes 786440 | tf_op jit(solution)/shard_map/ppermute | solution.py:266
  96.1 15.5 %collective-permute-start.7 = (bf16[64,2048]{1,0:T(8,128)(2,1)}, bf16[64,2048]{1,0:T(8,128)(2,1)}, u32[]{:S(2)}, u32[]{:S(2)}) collective-permute-start(bf16[64,2048]{1,0:T(8,128)(2,1)} %collective-permute-done.4.facing_ref), channel_id=1, source_target_pairs={{0,8},{8,16},{16,24},{24,0},{1,9},{9,17},{17,25},{25,1},{2,10},{10... | collective-permute-start | bytes 786440 | tf_op jit(solution)/shard_map/ppermute | solution.py:266
  107.2 18.8 %collective-permute-start.8 = (bf16[32,2048]{1,0:T(8,128)(2,1)}, bf16[32,2048]{1,0:T(8,128)(2,1)}, u32[]{:S(2)}, u32[]{:S(2)}) collective-permute-start(bf16[32,2048]{1,0:T(8,128)(2,1)} %slice.18), channel_id=1, source_target_pairs={{0,24},{8,0},{16,8},{24,16},{1,25},{9,1},{17,9},{25,17},{2,26},{10... | collective-permute-start | bytes 393224 | tf_op jit(solution)/shard_map/ppermute | solution.py:269
  113.2 13.6 %collective-permute-start.9 = (bf16[32,2048]{1,0:T(8,128)(2,1)}, bf16[32,2048]{1,0:T(8,128)(2,1)}, u32[]{:S(2)}, u32[]{:S(2)}) collective-permute-start(bf16[32,2048]{1,0:T(8,128)(2,1)} %slice.19), channel_id=1, source_target_pairs={{0,8},{8,16},{16,24},{24,0},{1,9},{9,17},{17,25},{25,1},{2,10},{10... | collective-permute-start | bytes 393224 | tf_op jit(solution)/shard_map/ppermute | solution.py:269
  120.8 18.9 %all-to-all-start.3 = ((bf16[4,16,2176]{2,1,0:T(8,128)(2,1)}), bf16[4,16,2176]{2,1,0:T(8,128)(2,1)}, u32[]{:S(2)}, u32[]{:S(2)}) async-start(bf16[4,16,2176]{2,1,0:T(8,128)(2,1)} %bitcast.41), calls=%async_computation.3 | async-start | bytes 557056 | tf_op jit(solution)/shard_map/all_to_all | solution.py:321
  141.9 29.0 %all-to-all-start.4 = ((bf16[8,16,2048]{2,1,0:T(8,128)(2,1)}), bf16[8,16,2048]{2,1,0:T(8,128)(2,1)}, u32[]{:S(2)}, u32[]{:S(2)}) async-start(bf16[8,16,2048]{2,1,0:T(8,128)(2,1)} %broadcast_in_dim.61), calls=%async_computation.4 | async-start | bytes 1048576 | tf_op jit(solution)/shard_map/all_to_all | solution.py:241
  150.6 6.3 %collective-permute-start.10 = (bf16[256,2048]{1,0:T(8,128)(2,1)S(1)}, bf16[256,2048]{1,0:T(8,128)(2,1)S(1)}, u32[]{:S(2)}, u32[]{:S(2)}) collective-permute-start(bf16[256,2048]{1,0:T(8,128)(2,1)S(1)} %constant_dynamic-update-slice_fusion.5.weight_ref.refs_2_), channel_id=1, source_target_pairs={{0,4},{4,0},{1,5},{5,1},{2,6},{6,2},{3,7},{7,3},{8,12},{12,8},{9,1... | collective-permute-start | bytes 3145736 | tf_op jit(solution)/shard_map/ppermute | solution.py:279
  177.4 11.0 %all-to-all-start.5 = ((f32[4,16,16,128]{3,2,1,0:T(8,128)}), f32[4,16,16,128]{3,2,1,0:T(8,128)S(1)}, u32[]{:S(2)}, u32[]{:S(2)}) async-start(f32[4,16,16,128]{3,2,1,0:T(8,128)} %copy-done.1), calls=%async_computation.5 | async-start | bytes 1048576 | tf_op jit(solution)/shard_map/all_to_all | solution.py:343
  (13 other events, 16.8 us)

commit v6 on v5

--- a/solution.py
+++ b/solution.py
@@ -38,6 +38,22 @@
 def join_parts(packed):
     whole = packed + pltpu.roll(packed, 112, 1) + pltpu.roll(packed, 96, 1)
     return jnp.where(lanes(whole.shape) < HEADS, whole, 0.0)
+
+
+def prepare_kernel(queries_ref, listed_ref, out_ref):
+    place = lax.broadcasted_iota(jnp.int32, (8, 128), 0)
+    spread = jnp.where(lanes((8, 128)) == place, 1.0, 0.0).astype(jnp.bfloat16)
+    listed = lax.dot_general(
+        listed_ref[...].astype(jnp.float32).astype(jnp.bfloat16),
+        spread,
+        (((0,), (0,)), ((), ())),
+        preferred_element_type=jnp.float32,
+    ).astype(jnp.bfloat16)
+    heads = [queries_ref[:, head, :] for head in range(HEADS)]
+    for copy in range(ZH):
+        for head in range(HEADS):
+            out_ref[copy, :, head * HD : (head + 1) * HD] = heads[head]
+        out_ref[copy, :, WIDE:] = listed
 
 
 def dispatch_kernel(logical_ref, pool_ref, above_ref, below_ref, out_ref, select_ref):
@@ -152,21 +168,17 @@
     terms.append((lambda at: own_ref[:, at], own_log_ref[...]))
     columns, _ = merge(terms)
     for head in range(HEADS):
-        out_ref[:, head * HD : (head + 1) * HD] = columns[head].astype(jnp.bfloat16)
+        rows = columns[head].astype(jnp.bfloat16)
+        for copy in range(ZH * ZP):
+            out_ref[copy, :, head * HD : (head + 1) * HD] = rows
 
 
 def project_kernel(rows_ref, *refs):
-    sources, out_ref, held, sems = refs[:4], refs[4], refs[5], refs[6]
-    copies = []
-    for piece, source in enumerate(sources):
-        copy = pltpu.make_async_copy(source, held.at[piece], sems.at[piece])
-        copy.start()
-        copies.append(copy)
+    out_ref = refs[4]
     for piece in range(4):
-        copies[piece].wait()
         terms = lax.dot_general(
-            held[piece], rows_ref[...], (((1,), (1,)), ((), ())), preferred_element_type=jnp.float32
-        )
+            refs[piece][...], rows_ref[...], (((1,), (1,)), ((), ())), preferred_element_type=jnp.float32
+        ).astype(jnp.bfloat16)
         for owner in range(YS):
             for part in range(XS):
                 first = (owner * XS + part) * 16
@@ -181,13 +193,13 @@
             for order, step in enumerate((0, 1, 3, 2)):
                 y = lax.rem(place_ref[1] + step, YS)
                 index = (far_side * CS + far_core) * YS + order
-                term = terms_ref[0, index]
+                term = terms_ref[0, index].astype(jnp.float32)
                 for part in range(1, XS):
-                    term = term + terms_ref[part, index]
+                    term = term + terms_ref[part, index].astype(jnp.float32)
                 out_ref[(side * YS + y) * CS + core] = term.astype(jnp.bfloat16)
 
 
-def settle_kernel(parts_ref, out_ref):
+def settle_kernel(place_ref, parts_ref, out_ref):
     lane = lanes((16, 128))
     for side in range(ZQ):
         parts = [
@@ -236,10 +248,8 @@
     ] * far
 
 
-def spread_along(value, axis, count):
-    copies = jnp.broadcast_to(value[None], (count,) + value.shape)
-    everyone = lax.all_to_all(copies, axis, split_axis=0, concat_axis=0, tiled=True)
-    return everyone.reshape((count * value.shape[0],) + value.shape[1:])
+def exchange(value, axis):
+    return lax.all_to_all(value, axis, split_axis=0, concat_axis=0, tiled=True)
 
 
 def on_device(
@@ -255,9 +265,15 @@
 ):
     quad = ("zp", "zq", "y", "c")
     swap = [(0, 1), (1, 0)]
-    flat_queries = queries.reshape(ROWS, WIDE)
-    listed = jnp.pad(prefix_lists.astype(jnp.bfloat16), ((0, 0), (0, 120)))
-    pool = spread_along(jnp.concatenate([flat_queries, listed], axis=1), "zh", ZH)
+    pool = exchange(
+        pl.pallas_call(
+            prepare_kernel,
+            out_shape=jax.ShapeDtypeStruct((ZH, ROWS, PACK), jnp.bfloat16),
+            compiler_params=PARAMS,
+            name="prepare",
+        )(queries, prefix_lists.T),
+        "zh",
+    ).reshape(POOL, PACK)
 
     up = [(place, (place + 1) % YS) for place in range(YS)]
     down = [(place, (place - 1) % YS) for place in range(YS)]
@@ -295,7 +311,7 @@
         compiler_params=PARAMS,
         name="dispatch",
     )(jnp.broadcast_to(logical[None], (8, 128)), pool, above, below)
-    arrived = lax.all_to_all(outgoing, quad, split_axis=0, concat_axis=0, tiled=True)
+    arrived = exchange(outgoing, quad)
     partials = pl.pallas_call(
         attend_kernel,
         in_specs=inputs(3, 3),
@@ -310,7 +326,7 @@
         facing,
         own_out,
     )
-    back = lax.all_to_all(partials, quad, split_axis=0, concat_axis=0, tiled=True)
+    back = exchange(partials, quad)
     joined = pl.pallas_call(
         gather_kernel,
         in_specs=inputs(2, 3),
@@ -318,29 +334,24 @@
         compiler_params=PARAMS,
         name="gather",
     )(back, select, other, above_far, below_far)
-    far = lax.all_to_all(joined, "zh", split_axis=0, concat_axis=0, tiled=True)
+    far = exchange(joined, "zh")
 
     attended = pl.pallas_call(
         final_kernel,
         in_specs=inputs(3, 1),
-        out_shape=jax.ShapeDtypeStruct((ROWS, WIDE), jnp.bfloat16),
+        out_shape=jax.ShapeDtypeStruct((ZH * ZP, ROWS, WIDE), jnp.bfloat16),
         compiler_params=PARAMS,
         name="final",
     )(far, own_out, jnp.pad(own_log, ((0, 0), (0, 112))), mine_far)
 
-    rows = spread_along(attended, ("zh", "zp"), ZH * ZP)
+    rows = exchange(attended, ("zh", "zp")).reshape(ZP * POOL, WIDE)
     terms = pl.pallas_call(
         project_kernel,
-        in_specs=inputs(1, 4),
-        out_shape=jax.ShapeDtypeStruct((XS, GROUP, 16, ZP * POOL), jnp.float32),
-        scratch_shapes=[
-            pltpu.VMEM((4, YS * 64, WIDE), jnp.bfloat16),
-            pltpu.SemaphoreType.DMA((4,)),
-        ],
+        out_shape=jax.ShapeDtypeStruct((XS, GROUP, 16, ZP * POOL), jnp.bfloat16),
         compiler_params=PARAMS,
         name="project",
     )(rows, mine, other, mine_far, other_far)
-    terms = lax.all_to_all(terms, "kv", split_axis=0, concat_axis=0, tiled=True)
+    terms = exchange(terms, "kv")
     place = jnp.stack([lax.axis_index(axis) for axis in ("zq", "y", "c")]).astype(jnp.int32)
     parts = pl.pallas_call(
         sum_kernel,
@@ -352,13 +363,17 @@
         compiler_params=PARAMS,
         name="sum",
     )(place, terms)
-    parts = lax.all_to_all(parts, ("zq", "y", "c"), split_axis=0, concat_axis=0, tiled=True)
+    parts = exchange(parts, ("zq", "y", "c"))
     return pl.pallas_call(
         settle_kernel,
+        in_specs=[
+            pl.BlockSpec(memory_space=pltpu.SMEM),
+            pl.BlockSpec(memory_space=pltpu.VMEM),
+        ],
         out_shape=jax.ShapeDtypeStruct((16, ZH * QUAD * ROWS), jnp.bfloat16),
         compiler_params=PARAMS,
         name="settle",
-    )(parts).T
+    )(lax.axis_index("zp").reshape(1).astype(jnp.int32), parts).T
 
 
 def solution(mesh):

time: 216 us -> 213 us (0.986)
  blocking collectives: 24.7 us -> 0 us
  starting transfers between devices: 87 us -> 105 us
  waiting for transfers between devices: 63.6 us -> 67.3 us
    all_to_all x1 -> x0, blocking collectives: 24.7 us -> none  [on_device(): lax.all_to_all(parts, ('zq', 'y', 'c'), split_axis=0, concat_axis=0, tile...]
    all_to_all x6 -> x7, starting transfers between devices: 51.7 us -> 69.9 us  [exchange(): return lax.all_to_all(value, axis, split_axis=0, concat_axis=0, tiled=True)]
    all_to_all x6 -> x7, waiting for transfers between devices: 37.5 us -> 41.9 us  [exchange(): return lax.all_to_all(value, axis, split_axis=0, concat_axis=0, tiled=True)]
    pallas_call x2 -> x3, Pallas kernels: 5.25 us -> 5.04 us  [the longest x1 3.33 us: on_device(): pl.pallas_call(project_kernel, out_shape=jax.ShapeDtypeStruct((XS, GROUP,...]
  transfers between devices with their start and end apart: 17 -> 18, of which waited for: 12 -> 13; matrix products, arithmetic and copies ran while one was open for 5% -> 5% of each run, Pallas kernels for 1% -> 1%
where the time goes in v6:
time: 213 us; the launch traced here: 211 us
  starting transfers between devices  105 us (49%)
  waiting for transfers between devices  67.3 us (32%)
  local copies, waits for them, and re-layouts  18.4 us (9%)
  Pallas kernels  17.4 us (8%)
    all_to_all x7, starting transfers between devices, exchange(): return lax.all_to_all(value, axis, split_axis=0, concat_axis=0, tiled=True)  69.9 us
    all_to_all x7, waiting for transfers between devices, exchange(): return lax.all_to_all(value, axis, split_axis=0, concat_axis=0, tiled=True)  41.9 us
    ppermute x4, waiting for transfers between devices, beside(): return (lax.ppermute(block, 'y', down), lax.ppermute(block, 'y', up))  14.4 us
    unnamed x51, local copies, waits for them, and re-layouts  13.9 us
    ppermute x4, starting transfers between devices, beside(): return (lax.ppermute(block, 'y', down), lax.ppermute(block, 'y', up))  13 us
    ppermute x2, starting transfers between devices, piece_of(): lax.ppermute(above[:32], 'y', down)  8.8 us
    pallas_call x1, Pallas kernels, on_device(): pl.pallas_call(attend_kernel, in_specs=inputs(3, 3), out_shape=packed(SLO...  6.8 us
  transfers between devices with their start and end apart: 18, of which 13 were waited for; matrix products, arithmetic and copies ran while one was open for 5% of the time, Pallas kernels for 1%

profile of v6, /device:TPU:1, one launch (start us, length us, event | category | flops | bytes accessed | tf_op | source)
XLA Modules:
  0.0 211.2 jit_solution(14119186495208064522)
XLA Ops:
  2.5 15.6 %all-to-all-start = ((bf16[4,16,2176]{2,1,0:T(8,128)(2,1)}), bf16[4,16,2176]{2,1,0:T(8,128)(2,1)S(1)}, u32[]{:S(2)}, u32[]{:S(2)}) async-start(bf16[4,16,2176]{2,1,0:T(8,128)(2,1)} %prepare.1), calls=%async_computation | async-start | bytes 557056 | tf_op jit(solution)/shard_map/all_to_all | solution.py:252
  18.1 4.6 %collective-permute-start = (bf16[64,2048]{1,0:T(8,128)(2,1)}, bf16[64,2048]{1,0:T(8,128)(2,1)S(1)}, u32[]{:S(2)}, u32[]{:S(2)}) collective-permute-start(bf16[64,2048]{1,0:T(8,128)(2,1)} %bitcast.6), channel_id=1, source_target_pairs={{0,24},{8,0},{16,8},{24,16},{1,25},{9,1},{17,9},{25,17},{2,26},{10... | collective-permute-start | bytes 786440 | tf_op jit(solution)/shard_map/ppermute | solution.py:282
  27.7 4.9 %collective-permute-done.1.below_ref = bf16[64,2048]{1,0:T(8,128)(2,1)S(1)} collective-permute-done((bf16[64,2048]{1,0:T(8,128)(2,1)}, bf16[64,2048]{1,0:T(8,128)(2,1)S(1)}, u32[]{:S(2)}, u32[]{:S(2)}) %collective-permute-start.1) | collective-permute-done | bytes 262176 | tf_op jit(solution)/shard_map/ppermute | solution.py:282
  34.5 13.7 %all-to-all-start.1 = ((bf16[32,8,2048]{2,1,0:T(8,128)(2,1)}), bf16[32,8,2048]{2,1,0:T(8,128)(2,1)S(1)}, u32[]{:S(2)}, u32[]{:S(2)}) async-start(bf16[32,8,2048]{2,1,0:T(8,128)(2,1)} %bitcast.41), calls=%async_computation.1 | async-start | bytes 2097152 | tf_op jit(solution)/shard_map/all_to_all | solution.py:252
  48.2 3.4 %collective-permute-start.4 = (bf16[64,2048]{1,0:T(8,128)(2,1)}, bf16[64,2048]{1,0:T(8,128)(2,1)}, u32[]{:S(2)}, u32[]{:S(2)}) collective-permute-start(bf16[64,2048]{1,0:T(8,128)(2,1)} %bitcast.6), channel_id=1, source_target_pairs={{0,32},{32,0},{1,33},{33,1},{2,34},{34,2},{3,35},{35,3},{4,36},{36... | collective-permute-start | bytes 786440 | tf_op jit(solution)/shard_map/ppermute | solution.py:289
  56.1 4.3 %collective-permute-start.2 = (bf16[32,2048]{1,0:T(8,128)(2,1)S(1)}, bf16[32,2048]{1,0:T(8,128)(2,1)S(1)}, u32[]{:S(2)}, u32[]{:S(2)}) collective-permute-start(bf16[32,2048]{1,0:T(8,128)(2,1)S(1)} %slice.16), channel_id=1, source_target_pairs={{0,24},{8,0},{16,8},{24,16},{1,25},{9,1},{17,9},{25,17},{2,26},{10... | collective-permute-start | bytes 393224 | tf_op jit(solution)/shard_map/ppermute | solution.py:285
  64.5 3.9 %collective-permute-done.3 = bf16[32,2048]{1,0:T(8,128)(2,1)S(1)} collective-permute-done((bf16[32,2048]{1,0:T(8,128)(2,1)S(1)}, bf16[32,2048]{1,0:T(8,128)(2,1)S(1)}, u32[]{:S(2)}, u32[]{:S(2)}) %collective-permute-start.3) | collective-permute-done | bytes 131104 | tf_op jit(solution)/shard_map/ppermute | solution.py:285
  68.4 2.8 %collective-permute-done.4.facing_ref = bf16[64,2048]{1,0:T(8,128)(2,1)} collective-permute-done((bf16[64,2048]{1,0:T(8,128)(2,1)}, bf16[64,2048]{1,0:T(8,128)(2,1)}, u32[]{:S(2)}, u32[]{:S(2)}) %collective-permute-start.4) | collective-permute-done | bytes 262176 | tf_op jit(solution)/shard_map/ppermute | solution.py:289
  71.1 3.6 %all-to-all-done.1 = bf16[32,8,2048]{2,1,0:T(8,128)(2,1)S(1)} async-done(((bf16[32,8,2048]{2,1,0:T(8,128)(2,1)}), bf16[32,8,2048]{2,1,0:T(8,128)(2,1)S(1)}, u32[]{:S(2)}, u32[]{:S(2)}) %all-to-all-start.1) | async-done | bytes 1048608 | tf_op jit(solution)/shard_map/all_to_all | solution.py:252
  76.9 6.8 %attend.1 = bf16[256,2176]{1,0:T(8,128)(2,1)} custom-call(bf16[256,2048]{1,0:T(8,128)(2,1)S(1)} %bitcast.36, bf16[1024,256]{1,0:T(8,128)(2,1)S(1)} %copy-done.2, bf16[1024,256]{1,0:T(8,128)(2,1)S(1)} %copy-done.1, bf16[256,2048]{1,0:T(8,128)(2,1)S(1)} %constant_dynamic-update-slice_fusion.weight_ref.refs_0_, ...), custom_call_target="tpu_custom_call" | custom-call | tf_op jit(solution)/shard_map/attend/pallas_call | solution.py:315
  83.7 5.6 %all-to-all-start.2 = ((bf16[32,8,2176]{2,1,0:T(8,128)(2,1)}), bf16[32,8,2176]{2,1,0:T(8,128)(2,1)}, u32[]{:S(2)}, u32[]{:S(2)}) async-start(bf16[32,8,2176]{2,1,0:T(8,128)(2,1)} %bitcast.10), calls=%async_computation.2 | async-start | bytes 2228224 | tf_op jit(solution)/shard_map/all_to_all | solution.py:252
  91.6 4.6 %collective-permute-start.6 = (bf16[64,2048]{1,0:T(8,128)(2,1)}, bf16[64,2048]{1,0:T(8,128)(2,1)S(1)}, u32[]{:S(2)}, u32[]{:S(2)}) collective-permute-start(bf16[64,2048]{1,0:T(8,128)(2,1)} %collective-permute-done.4.facing_ref), channel_id=1, source_target_pairs={{0,24},{8,0},{16,8},{24,16},{1,25},{9,1},{17,9},{25,17},{2,26},{10... | collective-permute-start | bytes 786440 | tf_op jit(solution)/shard_map/ppermute | solution.py:282
  99.2 7.4 %collective-permute-done.6.above_ref = bf16[64,2048]{1,0:T(8,128)(2,1)S(1)} collective-permute-done((bf16[64,2048]{1,0:T(8,128)(2,1)}, bf16[64,2048]{1,0:T(8,128)(2,1)S(1)}, u32[]{:S(2)}, u32[]{:S(2)}) %collective-permute-start.6) | collective-permute-done | bytes 262176 | tf_op jit(solution)/shard_map/ppermute | solution.py:282
  107.2 4.5 %collective-permute-start.8 = (bf16[32,2048]{1,0:T(8,128)(2,1)}, bf16[32,2048]{1,0:T(8,128)(2,1)}, u32[]{:S(2)}, u32[]{:S(2)}) collective-permute-start(bf16[32,2048]{1,0:T(8,128)(2,1)} %slice.18), channel_id=1, source_target_pairs={{0,24},{8,0},{16,8},{24,16},{1,25},{9,1},{17,9},{25,17},{2,26},{10... | collective-permute-start | bytes 393224 | tf_op jit(solution)/shard_map/ppermute | solution.py:285
  120.9 4.1 %all-to-all-start.3 = ((bf16[4,16,2176]{2,1,0:T(8,128)(2,1)}), bf16[4,16,2176]{2,1,0:T(8,128)(2,1)}, u32[]{:S(2)}, u32[]{:S(2)}) async-start(bf16[4,16,2176]{2,1,0:T(8,128)(2,1)} %bitcast.39), calls=%async_computation.3 | async-start | bytes 557056 | tf_op jit(solution)/shard_map/all_to_all | solution.py:252
  127.9 11.9 %all-to-all-done.3 = bf16[4,16,2176]{2,1,0:T(8,128)(2,1)} async-done(((bf16[4,16,2176]{2,1,0:T(8,128)(2,1)}), bf16[4,16,2176]{2,1,0:T(8,128)(2,1)}, u32[]{:S(2)}, u32[]{:S(2)}) %all-to-all-start.3) | async-done | bytes 278560 | tf_op jit(solution)/shard_map/all_to_all | solution.py:252
  142.0 8.7 %all-to-all-start.4 = ((bf16[8,16,2048]{2,1,0:T(8,128)(2,1)}), bf16[8,16,2048]{2,1,0:T(8,128)(2,1)}, u32[]{:S(2)}, u32[]{:S(2)}) async-start(bf16[8,16,2048]{2,1,0:T(8,128)(2,1)} %copy-done.3), calls=%async_computation.4 | async-start | bytes 1048576 | tf_op jit(solution)/shard_map/all_to_all | solution.py:252
  150.7 4.0 %collective-permute-start.10 = (bf16[256,2048]{1,0:T(8,128)(2,1)S(1)}, bf16[256,2048]{1,0:T(8,128)(2,1)S(1)}, u32[]{:S(2)}, u32[]{:S(2)}) collective-permute-start(bf16[256,2048]{1,0:T(8,128)(2,1)S(1)} %constant_dynamic-update-slice_fusion.5.weight_ref.refs_2_), channel_id=1, source_target_pairs={{0,4},{4,0},{1,5},{5,1},{2,6},{6,2},{3,7},{7,3},{8,12},{12,8},{9,1... | collective-permute-start | bytes 3145736 | tf_op jit(solution)/shard_map/ppermute | solution.py:295
  158.0 13.1 %all-to-all-done.4 = bf16[8,16,2048]{2,1,0:T(8,128)(2,1)} async-done(((bf16[8,16,2048]{2,1,0:T(8,128)(2,1)}), bf16[8,16,2048]{2,1,0:T(8,128)(2,1)}, u32[]{:S(2)}, u32[]{:S(2)}) %all-to-all-start.4) | async-done | bytes 524320 | tf_op jit(solution)/shard_map/all_to_all | solution.py:252
  172.3 3.3 %project.1 = bf16[4,16,16,128]{3,2,1,0:T(8,128)(2,1)} custom-call(bf16[128,2048]{1,0:T(8,128)(2,1)} %bitcast.15.rows_ref, bf16[256,2048]{1,0:T(8,128)(2,1)S(1)} %constant_dynamic-update-slice_fusion.weight_ref.refs_0_, bf16[256,2048]{1,0:T(8,128)(2,1)} %collective-permute-done.5.weight_ref.refs_1_, ...), custom_call_target="tpu_custom_call" | custom-call | tf_op jit(solution)/shard_map/project/pallas_call | solution.py:348
  175.6 4.0 %all-to-all-start.5 = ((bf16[4,16,16,128]{3,2,1,0:T(8,128)(2,1)}), bf16[4,16,16,128]{3,2,1,0:T(8,128)(2,1)S(1)}, u32[]{:S(2)}, u32[]{:S(2)}) async-start(bf16[4,16,16,128]{3,2,1,0:T(8,128)(2,1)} %project.1), calls=%async_computation.5 | async-start | bytes 524288 | tf_op jit(solution)/shard_map/all_to_all | solution.py:252
  179.7 5.5 %all-to-all-done.5.terms_ref = bf16[4,16,16,128]{3,2,1,0:T(8,128)(2,1)S(1)} async-done(((bf16[4,16,16,128]{3,2,1,0:T(8,128)(2,1)}), bf16[4,16,16,128]{3,2,1,0:T(8,128)(2,1)S(1)}, u32[]{:S(2)}, u32[]{:S(2)}) %all-to-all-start.5) | async-done | bytes 262176 | tf_op jit(solution)/shard_map/all_to_all | solution.py:252
  186.4 18.2 %all-to-all-start.6 = ((bf16[16,16,128]{2,1,0:T(8,128)(2,1)}), bf16[16,16,128]{2,1,0:T(8,128)(2,1)S(1)}, u32[]{:S(2)}, u32[]{:S(2)}) async-start(bf16[16,16,128]{2,1,0:T(8,128)(2,1)} %sum.1), calls=%async_computation.6 | async-start | bytes 131072 | tf_op jit(solution)/shard_map/all_to_all | solution.py:252
  204.5 5.8 %all-to-all-done.6.parts_ref = bf16[16,16,128]{2,1,0:T(8,128)(2,1)S(1)} async-done(((bf16[16,16,128]{2,1,0:T(8,128)(2,1)}), bf16[16,16,128]{2,1,0:T(8,128)(2,1)S(1)}, u32[]{:S(2)}, u32[]{:S(2)}) %all-to-all-start.6) | async-done | bytes 65568 | tf_op jit(solution)/shard_map/all_to_all | solution.py:252
  (93 shorter events, 46.4 us)
Async XLA Ops:
  0.0 51.7 %copy-start = (bf16[16,128,2,128]{3,2,1,0:T(2,128)(2,1)S(1)}, bf16[16,128,2,128]{3,2,1,0:T(2,128)(2,1)}, u32[]{:S(2)}) copy-start(bf16[16,128,2,128]{3,2,1,0:T(2,128)(2,1)} %param.12) | copy-start | bytes 3145732
  2.5 30.2 %all-to-all-start = ((bf16[4,16,2176]{2,1,0:T(8,128)(2,1)}), bf16[4,16,2176]{2,1,0:T(8,128)(2,1)S(1)}, u32[]{:S(2)}, u32[]{:S(2)}) async-start(bf16[4,16,2176]{2,1,0:T(8,128)(2,1)} %prepare.1), calls=%async_computation | async-start | bytes 557056 | tf_op jit(solution)/shard_map/all_to_all | solution.py:252
  18.1 9.6 %collective-permute-start = (bf16[64,2048]{1,0:T(8,128)(2,1)}, bf16[64,2048]{1,0:T(8,128)(2,1)S(1)}, u32[]{:S(2)}, u32[]{:S(2)}) collective-permute-start(bf16[64,2048]{1,0:T(8,128)(2,1)} %bitcast.6), channel_id=1, source_target_pairs={{0,24},{8,0},{16,8},{24,16},{1,25},{9,1},{17,9},{25,17},{2,26},{10... | collective-permute-start | bytes 786440 | tf_op jit(solution)/shard_map/ppermute | solution.py:282
  22.8 9.9 %collective-permute-start.1 = (bf16[64,2048]{1,0:T(8,128)(2,1)}, bf16[64,2048]{1,0:T(8,128)(2,1)S(1)}, u32[]{:S(2)}, u32[]{:S(2)}) collective-permute-start(bf16[64,2048]{1,0:T(8,128)(2,1)} %bitcast.6), channel_id=1, source_target_pairs={{0,8},{8,16},{16,24},{24,0},{1,9},{9,17},{17,25},{25,1},{2,10},{10... | collective-permute-start | bytes 786440 | tf_op jit(solution)/shard_map/ppermute | solution.py:282
  34.5 18.0 %copy-start.12 = (f32[64,256]{1,0:T(8,128)}, f32[64,256]{1,0:T(8,128)S(1)}, u32[]{:S(2)}) copy-start(f32[64,256]{1,0:T(8,128)S(1)} %get-tuple-element.8.select_ref) | copy-start | bytes 196612
  34.5 17.2 %copy-start.19 = (s32[16]{0:T(128)S(1)}, s32[16]{0:T(128)}, u32[]{:S(2)}) copy-start(s32[16]{0:T(128)} %param.16) | copy-start | bytes 196
  34.5 17.3 %copy-start.11 = (bf16[16,16,128]{2,1,0:T(8,128)(2,1)S(1)}, bf16[16,16,128]{2,1,0:T(8,128)(2,1)}, u32[]{:S(2)}) copy-start(bf16[16,16,128]{2,1,0:T(8,128)(2,1)} %queries_ref.1) | copy-start | bytes 196612
  34.5 40.3 %all-to-all-start.1 = ((bf16[32,8,2048]{2,1,0:T(8,128)(2,1)}), bf16[32,8,2048]{2,1,0:T(8,128)(2,1)S(1)}, u32[]{:S(2)}, u32[]{:S(2)}) async-start(bf16[32,8,2048]{2,1,0:T(8,128)(2,1)} %bitcast.41), calls=%async_computation.1 | async-start | bytes 2097152 | tf_op jit(solution)/shard_map/all_to_all | solution.py:252
  48.2 22.9 %collective-permute-start.4 = (bf16[64,2048]{1,0:T(8,128)(2,1)}, bf16[64,2048]{1,0:T(8,128)(2,1)}, u32[]{:S(2)}, u32[]{:S(2)}) collective-permute-start(bf16[64,2048]{1,0:T(8,128)(2,1)} %bitcast.6), channel_id=1, source_target_pairs={{0,32},{32,0},{1,33},{33,1},{2,34},{34,2},{3,35},{35,3},{4,36},{36... | collective-permute-start | bytes 786440 | tf_op jit(solution)/shard_map/ppermute | solution.py:289
  53.9 6.4 %copy-start.5 = (bf16[64,2048]{1,0:T(8,128)(2,1)S(1)}, bf16[64,2048]{1,0:T(8,128)(2,1)}, u32[]{:S(2)}) copy-start(bf16[64,2048]{1,0:T(8,128)(2,1)} %copy-done.4) | copy-start | bytes 786436
  56.1 8.4 %collective-permute-start.2 = (bf16[32,2048]{1,0:T(8,128)(2,1)S(1)}, bf16[32,2048]{1,0:T(8,128)(2,1)S(1)}, u32[]{:S(2)}, u32[]{:S(2)}) collective-permute-start(bf16[32,2048]{1,0:T(8,128)(2,1)S(1)} %slice.16), channel_id=1, source_target_pairs={{0,24},{8,0},{16,8},{24,16},{1,25},{9,1},{17,9},{25,17},{2,26},{10... | collective-permute-start | bytes 393224 | tf_op jit(solution)/shard_map/ppermute | solution.py:285
  60.4 8.0 %collective-permute-start.3 = (bf16[32,2048]{1,0:T(8,128)(2,1)S(1)}, bf16[32,2048]{1,0:T(8,128)(2,1)S(1)}, u32[]{:S(2)}, u32[]{:S(2)}) collective-permute-start(bf16[32,2048]{1,0:T(8,128)(2,1)S(1)} %slice.17), channel_id=1, source_target_pairs={{0,8},{8,16},{16,24},{24,0},{1,9},{9,17},{17,25},{25,1},{2,10},{10... | collective-permute-start | bytes 393224 | tf_op jit(solution)/shard_map/ppermute | solution.py:285
  83.7 7.9 %copy-start.18 = (f32[16,2,8]{2,1,0:T(2,128)S(1)}, f32[16,2,8]{2,1,0:T(2,128)}, u32[]{:S(2)}) copy-start(f32[16,2,8]{2,1,0:T(2,128)} %copy-done.17) | copy-start | bytes 3076
  83.7 33.5 %all-to-all-start.2 = ((bf16[32,8,2176]{2,1,0:T(8,128)(2,1)}), bf16[32,8,2176]{2,1,0:T(8,128)(2,1)}, u32[]{:S(2)}, u32[]{:S(2)}) async-start(bf16[32,8,2176]{2,1,0:T(8,128)(2,1)} %bitcast.10), calls=%async_computation.2 | async-start | bytes 2228224 | tf_op jit(solution)/shard_map/all_to_all | solution.py:252
  89.3 26.0 %collective-permute-start.5 = (bf16[256,2048]{1,0:T(8,128)(2,1)S(1)}, bf16[256,2048]{1,0:T(8,128)(2,1)}, u32[]{:S(2)}, u32[]{:S(2)}) collective-permute-start(bf16[256,2048]{1,0:T(8,128)(2,1)S(1)} %constant_dynamic-update-slice_fusion.weight_ref.refs_0_), channel_id=1, source_target_pairs={{0,4},{4,0},{1,5},{5,1},{2,6},{6,2},{3,7},{7,3},{8,12},{12,8},{9,1... | collective-permute-start | bytes 3145736 | tf_op jit(solution)/shard_map/ppermute | solution.py:294
  91.6 14.9 %collective-permute-start.6 = (bf16[64,2048]{1,0:T(8,128)(2,1)}, bf16[64,2048]{1,0:T(8,128)(2,1)S(1)}, u32[]{:S(2)}, u32[]{:S(2)}) collective-permute-start(bf16[64,2048]{1,0:T(8,128)(2,1)} %collective-permute-done.4.facing_ref), channel_id=1, source_target_pairs={{0,24},{8,0},{16,8},{24,16},{1,25},{9,1},{17,9},{25,17},{2,26},{10... | collective-permute-start | bytes 786440 | tf_op jit(solution)/shard_map/ppermute | solution.py:282
  96.2 15.5 %collective-permute-start.7 = (bf16[64,2048]{1,0:T(8,128)(2,1)}, bf16[64,2048]{1,0:T(8,128)(2,1)}, u32[]{:S(2)}, u32[]{:S(2)}) collective-permute-start(bf16[64,2048]{1,0:T(8,128)(2,1)} %collective-permute-done.4.facing_ref), channel_id=1, source_target_pairs={{0,8},{8,16},{16,24},{24,0},{1,9},{9,17},{17,25},{25,1},{2,10},{10... | collective-permute-start | bytes 786440 | tf_op jit(solution)/shard_map/ppermute | solution.py:282
  107.2 18.8 %collective-permute-start.8 = (bf16[32,2048]{1,0:T(8,128)(2,1)}, bf16[32,2048]{1,0:T(8,128)(2,1)}, u32[]{:S(2)}, u32[]{:S(2)}) collective-permute-start(bf16[32,2048]{1,0:T(8,128)(2,1)} %slice.18), channel_id=1, source_target_pairs={{0,24},{8,0},{16,8},{24,16},{1,25},{9,1},{17,9},{25,17},{2,26},{10... | collective-permute-start | bytes 393224 | tf_op jit(solution)/shard_map/ppermute | solution.py:285
  113.3 13.6 %collective-permute-start.9 = (bf16[32,2048]{1,0:T(8,128)(2,1)}, bf16[32,2048]{1,0:T(8,128)(2,1)}, u32[]{:S(2)}, u32[]{:S(2)}) collective-permute-start(bf16[32,2048]{1,0:T(8,128)(2,1)} %slice.19), channel_id=1, source_target_pairs={{0,8},{8,16},{16,24},{24,0},{1,9},{9,17},{17,25},{25,1},{2,10},{10... | collective-permute-start | bytes 393224 | tf_op jit(solution)/shard_map/ppermute | solution.py:285
  120.9 18.9 %all-to-all-start.3 = ((bf16[4,16,2176]{2,1,0:T(8,128)(2,1)}), bf16[4,16,2176]{2,1,0:T(8,128)(2,1)}, u32[]{:S(2)}, u32[]{:S(2)}) async-start(bf16[4,16,2176]{2,1,0:T(8,128)(2,1)} %bitcast.39), calls=%async_computation.3 | async-start | bytes 557056 | tf_op jit(solution)/shard_map/all_to_all | solution.py:252
  142.0 29.1 %all-to-all-start.4 = ((bf16[8,16,2048]{2,1,0:T(8,128)(2,1)}), bf16[8,16,2048]{2,1,0:T(8,128)(2,1)}, u32[]{:S(2)}, u32[]{:S(2)}) async-start(bf16[8,16,2048]{2,1,0:T(8,128)(2,1)} %copy-done.3), calls=%async_computation.4 | async-start | bytes 1048576 | tf_op jit(solution)/shard_map/all_to_all | solution.py:252
  150.7 6.3 %collective-permute-start.10 = (bf16[256,2048]{1,0:T(8,128)(2,1)S(1)}, bf16[256,2048]{1,0:T(8,128)(2,1)S(1)}, u32[]{:S(2)}, u32[]{:S(2)}) collective-permute-start(bf16[256,2048]{1,0:T(8,128)(2,1)S(1)} %constant_dynamic-update-slice_fusion.5.weight_ref.refs_2_), channel_id=1, source_target_pairs={{0,4},{4,0},{1,5},{5,1},{2,6},{6,2},{3,7},{7,3},{8,12},{12,8},{9,1... | collective-permute-start | bytes 3145736 | tf_op jit(solution)/shard_map/ppermute | solution.py:295
  175.6 9.5 %all-to-all-start.5 = ((bf16[4,16,16,128]{3,2,1,0:T(8,128)(2,1)}), bf16[4,16,16,128]{3,2,1,0:T(8,128)(2,1)S(1)}, u32[]{:S(2)}, u32[]{:S(2)}) async-start(bf16[4,16,16,128]{3,2,1,0:T(8,128)(2,1)} %project.1), calls=%async_computation.5 | async-start | bytes 524288 | tf_op jit(solution)/shard_map/all_to_all | solution.py:252
  186.4 24.0 %all-to-all-start.6 = ((bf16[16,16,128]{2,1,0:T(8,128)(2,1)}), bf16[16,16,128]{2,1,0:T(8,128)(2,1)S(1)}, u32[]{:S(2)}, u32[]{:S(2)}) async-start(bf16[16,16,128]{2,1,0:T(8,128)(2,1)} %sum.1), calls=%async_computation.6 | async-start | bytes 131072 | tf_op jit(solution)/shard_map/all_to_all | solution.py:252
  (15 other events, 18.4 us)

commit v7 on v6

--- a/solution.py
+++ b/solution.py
@@ -83,15 +83,25 @@
     ).astype(jnp.bfloat16)
 
 
-def attend_kernel(q_ref, k_ref, v_ref, weight_ref, facing_ref, own_ref, out_ref):
+def attend_kernel(q_ref, keys_ref, values_ref, weight_ref, facing_ref, own_ref, out_ref, k_ref, v_ref, sems):
+    copies = []
+    for index in range(4):
+        source, held = ((keys_ref, k_ref), (values_ref, v_ref))[index % 2]
+        group = index // 2
+        copy = pltpu.make_async_copy(
+            source.at[:, pl.ds(group * HD, HD)], held.at[group], sems.at[index]
+        )
+        copy.start()
+        copies.append(copy)
     logs = jnp.zeros((SLOTS, 128), jnp.float32)
     lane = lanes((SLOTS, 128))
 
     def scores_of(head):
-        group = slice((head // 8) * HD, (head // 8 + 1) * HD)
+        if head % 8 == 0:
+            copies[head // 8 * 2].wait()
         return lax.dot_general(
             q_ref[:, head * HD : (head + 1) * HD],
-            k_ref[:, group],
+            k_ref[head // 8],
             (((1,), (1,)), ((), ())),
             preferred_element_type=jnp.float32,
         )
@@ -101,13 +111,14 @@
         scores = coming
         if head + 1 < HEADS:
             coming = scores_of(head + 1)
-        group = slice((head // 8) * HD, (head // 8 + 1) * HD)
+        if head % 8 == 0:
+            copies[head // 8 * 2 + 1].wait()
         at = slice(head * HD, (head + 1) * HD)
         top = jnp.max(scores, axis=1, keepdims=True)
         grown = jnp.exp2((scores - top) * (SCALE * LOG2E))
         total = jnp.sum(grown, axis=1, keepdims=True)
         mixed = jnp.dot(
-            grown.astype(jnp.bfloat16), v_ref[:, group], preferred_element_type=jnp.float32
+            grown.astype(jnp.bfloat16), v_ref[head // 8], preferred_element_type=jnp.float32
         )
         out_ref[:, at] = (mixed / total).astype(jnp.bfloat16)
         logs = jnp.where(lane == head, top * SCALE + jnp.log(total), logs)
@@ -173,38 +184,47 @@
             out_ref[copy, :, head * HD : (head + 1) * HD] = rows
 
 
-def project_kernel(rows_ref, *refs):
-    out_ref = refs[4]
+def project_kernel(place_ref, rows_ref, *refs):
+    sources, out_ref, held, sems = refs[:4], refs[4], refs[5], refs[6]
+    half_rows = YS * 64 // 2
+    copies = []
+    for piece, source in enumerate(sources):
+        for half in range(2):
+            rows = pl.ds(half * half_rows, half_rows)
+            copy = pltpu.make_async_copy(
+                source.at[rows, :], held.at[piece, rows, :], sems.at[piece * 2 + half]
+            )
+            copy.start()
+            copies.append(copy)
     for piece in range(4):
-        terms = lax.dot_general(
-            refs[piece][...], rows_ref[...], (((1,), (1,)), ((), ())), preferred_element_type=jnp.float32
-        ).astype(jnp.bfloat16)
-        for owner in range(YS):
-            for part in range(XS):
-                first = (owner * XS + part) * 16
-                out_ref[part, piece * YS + owner] = terms[first : first + 16, :]
-
-
-def sum_kernel(place_ref, terms_ref, out_ref):
-    for far_side in range(ZQ):
+        far_side, far_core = divmod(piece, CS)
         side = place_ref[0] if far_side == 0 else 1 - place_ref[0]
-        for far_core in range(CS):
-            core = place_ref[2] if far_core == 0 else 1 - place_ref[2]
-            for order, step in enumerate((0, 1, 3, 2)):
-                y = lax.rem(place_ref[1] + step, YS)
-                index = (far_side * CS + far_core) * YS + order
-                term = terms_ref[0, index].astype(jnp.float32)
-                for part in range(1, XS):
-                    term = term + terms_ref[part, index].astype(jnp.float32)
-                out_ref[(side * YS + y) * CS + core] = term.astype(jnp.bfloat16)
-
-
-def settle_kernel(place_ref, parts_ref, out_ref):
+        core = place_ref[2] if far_core == 0 else 1 - place_ref[2]
+        for half, steps in enumerate(((0, 1), (3, 2))):
+            copies[piece * 2 + half].wait()
+            terms = lax.dot_general(
+                held[piece, half * half_rows : (half + 1) * half_rows, :],
+                rows_ref[...],
+                (((1,), (1,)), ((), ())),
+                preferred_element_type=jnp.float32,
+            ).astype(jnp.bfloat16)
+            for index, step in enumerate(steps):
+                owner = (side * YS + lax.rem(place_ref[1] + step, YS)) * CS + core
+                for part in range(XS):
+                    first = (index * XS + part) * 16
+                    out_ref[owner * XS + part] = terms[first : first + 16, :]
+
+
+def settle_kernel(terms_ref, out_ref):
     lane = lanes((16, 128))
     for side in range(ZQ):
-        parts = [
-            parts_ref[side * YS * CS + owner].astype(jnp.float32) for owner in range(YS * CS)
-        ]
+        parts = []
+        for owner in range(YS * CS):
+            first = (side * YS * CS + owner) * XS
+            term = terms_ref[first].astype(jnp.float32)
+            for part in range(1, XS):
+                term = term + terms_ref[first + part].astype(jnp.float32)
+            parts.append(term)
         for far in range(ZH * ZP):
             tile = jnp.zeros((16, 128), jnp.float32)
             for owner in range(YS * CS):
@@ -314,8 +334,15 @@
     arrived = exchange(outgoing, quad)
     partials = pl.pallas_call(
         attend_kernel,
-        in_specs=inputs(3, 3),
+        in_specs=[pl.BlockSpec(memory_space=pltpu.VMEM)]
+        + [pl.BlockSpec(memory_space=pltpu.HBM)] * 2
+        + [pl.BlockSpec(memory_space=pl.ANY)] * 3,
         out_shape=packed(SLOTS),
+        scratch_shapes=[
+            pltpu.VMEM((2, TOKENS, HD), jnp.bfloat16),
+            pltpu.VMEM((2, TOKENS, HD), jnp.bfloat16),
+            pltpu.SemaphoreType.DMA((4,)),
+        ],
         compiler_params=PARAMS,
         name="attend",
     )(
@@ -345,35 +372,32 @@
     )(far, own_out, jnp.pad(own_log, ((0, 0), (0, 112))), mine_far)
 
     rows = exchange(attended, ("zh", "zp")).reshape(ZP * POOL, WIDE)
+    owners = ("zq", "y", "c")
     terms = pl.pallas_call(
         project_kernel,
-        out_shape=jax.ShapeDtypeStruct((XS, GROUP, 16, ZP * POOL), jnp.bfloat16),
+        in_specs=[pl.BlockSpec(memory_space=pltpu.SMEM), pl.BlockSpec(memory_space=pltpu.VMEM)]
+        + [pl.BlockSpec(memory_space=pltpu.HBM)] * 4,
+        out_shape=jax.ShapeDtypeStruct((GROUP * XS, 16, ZP * POOL), jnp.bfloat16),
+        scratch_shapes=[
+            pltpu.VMEM((4, YS * 64, WIDE), jnp.bfloat16),
+            pltpu.SemaphoreType.DMA((8,)),
+        ],
         compiler_params=PARAMS,
         name="project",
-    )(rows, mine, other, mine_far, other_far)
-    terms = exchange(terms, "kv")
-    place = jnp.stack([lax.axis_index(axis) for axis in ("zq", "y", "c")]).astype(jnp.int32)
-    parts = pl.pallas_call(
-        sum_kernel,
-        in_specs=[
-            pl.BlockSpec(memory_space=pltpu.SMEM),
-            pl.BlockSpec(memory_space=pltpu.VMEM),
-        ],
-        out_shape=jax.ShapeDtypeStruct((GROUP, 16, ZP * POOL), jnp.bfloat16),
-        compiler_params=PARAMS,
-        name="sum",
-    )(place, terms)
-    parts = exchange(parts, ("zq", "y", "c"))
+    )(
+        jnp.stack([lax.axis_index(axis) for axis in owners]).astype(jnp.int32),
+        rows,
+        mine,
+        other,
+        mine_far,
+        other_far,
+    )
     return pl.pallas_call(
         settle_kernel,
-        in_specs=[
-            pl.BlockSpec(memory_space=pltpu.SMEM),
-            pl.BlockSpec(memory_space=pltpu.VMEM),
-        ],
         out_shape=jax.ShapeDtypeStruct((16, ZH * QUAD * ROWS), jnp.bfloat16),
         compiler_params=PARAMS,
         name="settle",
-    )(lax.axis_index("zp").reshape(1).astype(jnp.int32), parts).T
+    )(exchange(terms, owners + ("kv",))).T
 
 
 def solution(mesh):

time: 213 us -> 208 us (0.977)
  blocking collectives: 0 us -> 29.5 us
  starting transfers between devices: 105 us -> 83.1 us
  waiting for transfers between devices: 67.3 us -> 56.8 us
  local copies, waits for them, and re-layouts: 18.4 us -> 16.2 us
    all_to_all x0 -> x1, blocking collectives: none -> 29.5 us  [exchange(): return lax.all_to_all(value, axis, split_axis=0, concat_axis=0, tiled=True)]
    all_to_all x7 -> x5, starting transfers between devices: 69.9 us -> 47.6 us  [exchange(): return lax.all_to_all(value, axis, split_axis=0, concat_axis=0, tiled=True)]
    all_to_all x7 -> x5, waiting for transfers between devices: 41.9 us -> 31.4 us  [exchange(): return lax.all_to_all(value, axis, split_axis=0, concat_axis=0, tiled=True)]
    unnamed x51 -> x47, local copies, waits for them, and re-layouts: 13.9 us -> 11.7 us
    pallas_call x4 -> x3, Pallas kernels: 12.2 us -> 13 us  [the longest x1 7.43 us: on_device(): pl.pallas_call(attend_kernel, in_specs=[pl.BlockSpec(memory_space=pltpu.V...]
  transfers between devices with their start and end apart: 18 -> 16, of which waited for: 13 -> 11; matrix products, arithmetic and copies ran while one was open for 5% -> 5% of each run, Pallas kernels for 1% -> 1%
where the time goes in v7:
time: 208 us; the launch traced here: 207 us
  starting transfers between devices  83.1 us (40%)
  waiting for transfers between devices  56.8 us (27%)
  blocking collectives  29.5 us (14%)
  Pallas kernels  18.2 us (9%)
  local copies, waits for them, and re-layouts  16.2 us (8%)
    all_to_all x5, starting transfers between devices, exchange(): return lax.all_to_all(value, axis, split_axis=0, concat_axis=0, tiled=True)  47.6 us
    all_to_all x5, waiting for transfers between devices, exchange(): return lax.all_to_all(value, axis, split_axis=0, concat_axis=0, tiled=True)  31.4 us
    all_to_all x1, blocking collectives, exchange(): return lax.all_to_all(value, axis, split_axis=0, concat_axis=0, tiled=True)  29.5 us
    ppermute x4, waiting for transfers between devices, beside(): return (lax.ppermute(block, 'y', down), lax.ppermute(block, 'y', up))  14.4 us
    ppermute x4, starting transfers between devices, beside(): return (lax.ppermute(block, 'y', down), lax.ppermute(block, 'y', up))  13 us
    unnamed x47, local copies, waits for them, and re-layouts  11.7 us
    ppermute x2, starting transfers between devices, piece_of(): lax.ppermute(above[:32], 'y', down)  8.8 us
    pallas_call x1, Pallas kernels, on_device(): pl.pallas_call(attend_kernel, in_specs=[pl.BlockSpec(memory_space=pltpu.V...  7.43 us
  transfers between devices with their start and end apart: 16, of which 11 were waited for; matrix products, arithmetic and copies ran while one was open for 5% of the time, Pallas kernels for 1%

profile of v7, /device:TPU:1, one launch (start us, length us, event | category | flops | bytes accessed | tf_op | source)
XLA Modules:
  0.0 206.6 jit_solution(14570080469382923992)
XLA Ops:
  2.5 15.6 %all-to-all-start = ((bf16[4,16,2176]{2,1,0:T(8,128)(2,1)}), bf16[4,16,2176]{2,1,0:T(8,128)(2,1)S(1)}, u32[]{:S(2)}, u32[]{:S(2)}) async-start(bf16[4,16,2176]{2,1,0:T(8,128)(2,1)} %prepare.1), calls=%async_computation | async-start | bytes 557056 | tf_op jit(solution)/shard_map/all_to_all | solution.py:272
  18.1 4.6 %collective-permute-start = (bf16[64,2048]{1,0:T(8,128)(2,1)}, bf16[64,2048]{1,0:T(8,128)(2,1)S(1)}, u32[]{:S(2)}, u32[]{:S(2)}) collective-permute-start(bf16[64,2048]{1,0:T(8,128)(2,1)} %bitcast.5), channel_id=1, source_target_pairs={{0,24},{8,0},{16,8},{24,16},{1,25},{9,1},{17,9},{25,17},{2,26},{10... | collective-permute-start | bytes 786440 | tf_op jit(solution)/shard_map/ppermute | solution.py:302
  25.6 2.1 %collective-permute-done.above_ref = bf16[64,2048]{1,0:T(8,128)(2,1)S(1)} collective-permute-done((bf16[64,2048]{1,0:T(8,128)(2,1)}, bf16[64,2048]{1,0:T(8,128)(2,1)S(1)}, u32[]{:S(2)}, u32[]{:S(2)}) %collective-permute-start) | collective-permute-done | bytes 262176 | tf_op jit(solution)/shard_map/ppermute | solution.py:302
  27.7 4.9 %collective-permute-done.1.below_ref = bf16[64,2048]{1,0:T(8,128)(2,1)S(1)} collective-permute-done((bf16[64,2048]{1,0:T(8,128)(2,1)}, bf16[64,2048]{1,0:T(8,128)(2,1)S(1)}, u32[]{:S(2)}, u32[]{:S(2)}) %collective-permute-start.1) | collective-permute-done | bytes 262176 | tf_op jit(solution)/shard_map/ppermute | solution.py:302
  34.5 13.7 %all-to-all-start.1 = ((bf16[32,8,2048]{2,1,0:T(8,128)(2,1)}), bf16[32,8,2048]{2,1,0:T(8,128)(2,1)S(1)}, u32[]{:S(2)}, u32[]{:S(2)}) async-start(bf16[32,8,2048]{2,1,0:T(8,128)(2,1)} %bitcast.40), calls=%async_computation.1 | async-start | bytes 2097152 | tf_op jit(solution)/shard_map/all_to_all | solution.py:272
  48.2 3.4 %collective-permute-start.4 = (bf16[64,2048]{1,0:T(8,128)(2,1)}, bf16[64,2048]{1,0:T(8,128)(2,1)}, u32[]{:S(2)}, u32[]{:S(2)}) collective-permute-start(bf16[64,2048]{1,0:T(8,128)(2,1)} %bitcast.5), channel_id=1, source_target_pairs={{0,32},{32,0},{1,33},{33,1},{2,34},{34,2},{3,35},{35,3},{4,36},{36... | collective-permute-start | bytes 786440 | tf_op jit(solution)/shard_map/ppermute | solution.py:309
  56.1 4.3 %collective-permute-start.2 = (bf16[32,2048]{1,0:T(8,128)(2,1)S(1)}, bf16[32,2048]{1,0:T(8,128)(2,1)S(1)}, u32[]{:S(2)}, u32[]{:S(2)}) collective-permute-start(bf16[32,2048]{1,0:T(8,128)(2,1)S(1)} %slice.16), channel_id=1, source_target_pairs={{0,24},{8,0},{16,8},{24,16},{1,25},{9,1},{17,9},{25,17},{2,26},{10... | collective-permute-start | bytes 393224 | tf_op jit(solution)/shard_map/ppermute | solution.py:305
  64.5 3.9 %collective-permute-done.3 = bf16[32,2048]{1,0:T(8,128)(2,1)S(1)} collective-permute-done((bf16[32,2048]{1,0:T(8,128)(2,1)S(1)}, bf16[32,2048]{1,0:T(8,128)(2,1)S(1)}, u32[]{:S(2)}, u32[]{:S(2)}) %collective-permute-start.3) | collective-permute-done | bytes 131104 | tf_op jit(solution)/shard_map/ppermute | solution.py:305
  68.4 2.8 %collective-permute-done.4.facing_ref = bf16[64,2048]{1,0:T(8,128)(2,1)} collective-permute-done((bf16[64,2048]{1,0:T(8,128)(2,1)}, bf16[64,2048]{1,0:T(8,128)(2,1)}, u32[]{:S(2)}, u32[]{:S(2)}) %collective-permute-start.4) | collective-permute-done | bytes 262176 | tf_op jit(solution)/shard_map/ppermute | solution.py:309
  71.1 3.6 %all-to-all-done.1 = bf16[32,8,2048]{2,1,0:T(8,128)(2,1)S(1)} async-done(((bf16[32,8,2048]{2,1,0:T(8,128)(2,1)}), bf16[32,8,2048]{2,1,0:T(8,128)(2,1)S(1)}, u32[]{:S(2)}, u32[]{:S(2)}) %all-to-all-start.1) | async-done | bytes 1048608 | tf_op jit(solution)/shard_map/all_to_all | solution.py:272
  76.9 7.4 %attend.1 = bf16[256,2176]{1,0:T(8,128)(2,1)} custom-call(bf16[256,2048]{1,0:T(8,128)(2,1)S(1)} %bitcast.35, bf16[1024,256]{1,0:T(8,128)(2,1)S(1)} %copy-done.2, bf16[1024,256]{1,0:T(8,128)(2,1)S(1)} %copy-done.1, bf16[256,2048]{1,0:T(8,128)(2,1)S(1)} %constant_dynamic-update-slice_fusion.weight_ref.refs_0_, ...), custom_call_target="tpu_custom_call" | custom-call | tf_op jit(solution)/shard_map/attend/pallas_call | solution.py:335
  84.3 5.4 %all-to-all-start.2 = ((bf16[32,8,2176]{2,1,0:T(8,128)(2,1)}), bf16[32,8,2176]{2,1,0:T(8,128)(2,1)}, u32[]{:S(2)}, u32[]{:S(2)}) async-start(bf16[32,8,2176]{2,1,0:T(8,128)(2,1)} %bitcast.9), calls=%async_computation.2 | async-start | bytes 2228224 | tf_op jit(solution)/shard_map/all_to_all | solution.py:272
  89.8 2.2 %collective-permute-start.5 = (bf16[256,2048]{1,0:T(8,128)(2,1)S(1)}, bf16[256,2048]{1,0:T(8,128)(2,1)}, u32[]{:S(2)}, u32[]{:S(2)}) collective-permute-start(bf16[256,2048]{1,0:T(8,128)(2,1)S(1)} %constant_dynamic-update-slice_fusion.weight_ref.refs_0_), channel_id=1, source_target_pairs={{0,4},{4,0},{1,5},{5,1},{2,6},{6,2},{3,7},{7,3},{8,12},{12,8},{9,1... | collective-permute-start | bytes 3145736 | tf_op jit(solution)/shard_map/ppermute | solution.py:314
  92.2 4.6 %collective-permute-start.6 = (bf16[64,2048]{1,0:T(8,128)(2,1)}, bf16[64,2048]{1,0:T(8,128)(2,1)S(1)}, u32[]{:S(2)}, u32[]{:S(2)}) collective-permute-start(bf16[64,2048]{1,0:T(8,128)(2,1)} %collective-permute-done.4.facing_ref), channel_id=1, source_target_pairs={{0,24},{8,0},{16,8},{24,16},{1,25},{9,1},{17,9},{25,17},{2,26},{10... | collective-permute-start | bytes 786440 | tf_op jit(solution)/shard_map/ppermute | solution.py:302
  99.7 7.4 %collective-permute-done.6.above_ref = bf16[64,2048]{1,0:T(8,128)(2,1)S(1)} collective-permute-done((bf16[64,2048]{1,0:T(8,128)(2,1)}, bf16[64,2048]{1,0:T(8,128)(2,1)S(1)}, u32[]{:S(2)}, u32[]{:S(2)}) %collective-permute-start.6) | collective-permute-done | bytes 262176 | tf_op jit(solution)/shard_map/ppermute | solution.py:302
  107.7 4.5 %collective-permute-start.8 = (bf16[32,2048]{1,0:T(8,128)(2,1)}, bf16[32,2048]{1,0:T(8,128)(2,1)}, u32[]{:S(2)}, u32[]{:S(2)}) collective-permute-start(bf16[32,2048]{1,0:T(8,128)(2,1)} %slice.18), channel_id=1, source_target_pairs={{0,24},{8,0},{16,8},{24,16},{1,25},{9,1},{17,9},{25,17},{2,26},{10... | collective-permute-start | bytes 393224 | tf_op jit(solution)/shard_map/ppermute | solution.py:305
  118.5 2.2 %gather.1 = bf16[64,2176]{1,0:T(8,128)(2,1)S(1)} custom-call(bf16[256,2176]{1,0:T(8,128)(2,1)} %bitcast.10.back_ref, f32[64,256]{1,0:T(8,128)S(1)} %copy-done.11, bf16[256,2048]{1,0:T(8,128)(2,1)} %collective-permute-done.5.weight_ref.refs_1_, bf16[64,2048]{1,0:T(8,128)(2,1)S(1)} %collective-permute-done.6.above_ref, ...), custom_call_target="tpu_custom_call" | custom-call | tf_op jit(solution)/shard_map/gather/pallas_call | solution.py:357
  121.4 4.1 %all-to-all-start.3 = ((bf16[4,16,2176]{2,1,0:T(8,128)(2,1)}), bf16[4,16,2176]{2,1,0:T(8,128)(2,1)}, u32[]{:S(2)}, u32[]{:S(2)}) async-start(bf16[4,16,2176]{2,1,0:T(8,128)(2,1)} %bitcast.38), calls=%async_computation.3 | async-start | bytes 557056 | tf_op jit(solution)/shard_map/all_to_all | solution.py:272
  128.4 12.0 %all-to-all-done.3 = bf16[4,16,2176]{2,1,0:T(8,128)(2,1)} async-done(((bf16[4,16,2176]{2,1,0:T(8,128)(2,1)}), bf16[4,16,2176]{2,1,0:T(8,128)(2,1)}, u32[]{:S(2)}, u32[]{:S(2)}) %all-to-all-start.3) | async-done | bytes 278560 | tf_op jit(solution)/shard_map/all_to_all | solution.py:272
  142.5 8.7 %all-to-all-start.4 = ((bf16[8,16,2048]{2,1,0:T(8,128)(2,1)}), bf16[8,16,2048]{2,1,0:T(8,128)(2,1)}, u32[]{:S(2)}, u32[]{:S(2)}) async-start(bf16[8,16,2048]{2,1,0:T(8,128)(2,1)} %copy-done.3), calls=%async_computation.4 | async-start | bytes 1048576 | tf_op jit(solution)/shard_map/all_to_all | solution.py:272
  151.2 4.2 %collective-permute-start.10 = (bf16[256,2048]{1,0:T(8,128)(2,1)S(1)}, bf16[256,2048]{1,0:T(8,128)(2,1)}, u32[]{:S(2)}, u32[]{:S(2)}) collective-permute-start(bf16[256,2048]{1,0:T(8,128)(2,1)S(1)} %constant_dynamic-update-slice_fusion.5.weight_ref.refs_2_), channel_id=1, source_target_pairs={{0,4},{4,0},{1,5},{5,1},{2,6},{6,2},{3,7},{7,3},{8,12},{12,8},{9,1... | collective-permute-start | bytes 3145736 | tf_op jit(solution)/shard_map/ppermute | solution.py:315
  157.6 13.9 %all-to-all-done.4 = bf16[8,16,2048]{2,1,0:T(8,128)(2,1)} async-done(((bf16[8,16,2048]{2,1,0:T(8,128)(2,1)}), bf16[8,16,2048]{2,1,0:T(8,128)(2,1)}, u32[]{:S(2)}, u32[]{:S(2)}) %all-to-all-start.4) | async-done | bytes 524320 | tf_op jit(solution)/shard_map/all_to_all | solution.py:272
  171.5 4.8 %project.1 = bf16[64,16,128]{2,1,0:T(8,128)(2,1)S(1)} custom-call(s32[3]{0:T(128)S(1)} %pad_add_fusion.place_ref, bf16[128,2048]{1,0:T(8,128)(2,1)} %bitcast.14.rows_ref, bf16[256,2048]{1,0:T(8,128)(2,1)S(1)} %constant_dynamic-update-slice_fusion.weight_ref.refs_0_, bf16[256,2048]{1,0:T(8,128)(2,1)} %collective-permute-done.5.weight_ref.refs_1_, ...), custom_call_target="tpu_custom_call" | custom-call | tf_op jit(solution)/shard_map/project/pallas_call | solution.py:376
  176.3 29.5 %all_to_all.48.terms_ref = bf16[64,16,128]{2,1,0:T(8,128)(2,1)S(1)} all-to-all(bf16[64,16,128]{2,1,0:T(8,128)(2,1)S(1)} %project.1), channel_id=1, replica_groups=mesh['zh'=4,'zp'=2,'zq'=2,'y'=4,'c'=2,'kv'=4] {'zq','y','c','kv'}, dimensions={0} | all-to-all | bytes 524288 | tf_op jit(solution)/shard_map/all_to_all | solution.py:272
  (85 shorter events, 36.3 us)
Async XLA Ops:
  0.0 51.7 %copy-start = (bf16[16,128,2,128]{3,2,1,0:T(2,128)(2,1)S(1)}, bf16[16,128,2,128]{3,2,1,0:T(2,128)(2,1)}, u32[]{:S(2)}) copy-start(bf16[16,128,2,128]{3,2,1,0:T(2,128)(2,1)} %param.12) | copy-start | bytes 3145732
  2.5 30.2 %all-to-all-start = ((bf16[4,16,2176]{2,1,0:T(8,128)(2,1)}), bf16[4,16,2176]{2,1,0:T(8,128)(2,1)S(1)}, u32[]{:S(2)}, u32[]{:S(2)}) async-start(bf16[4,16,2176]{2,1,0:T(8,128)(2,1)} %prepare.1), calls=%async_computation | async-start | bytes 557056 | tf_op jit(solution)/shard_map/all_to_all | solution.py:272
  18.1 9.6 %collective-permute-start = (bf16[64,2048]{1,0:T(8,128)(2,1)}, bf16[64,2048]{1,0:T(8,128)(2,1)S(1)}, u32[]{:S(2)}, u32[]{:S(2)}) collective-permute-start(bf16[64,2048]{1,0:T(8,128)(2,1)} %bitcast.5), channel_id=1, source_target_pairs={{0,24},{8,0},{16,8},{24,16},{1,25},{9,1},{17,9},{25,17},{2,26},{10... | collective-permute-start | bytes 786440 | tf_op jit(solution)/shard_map/ppermute | solution.py:302
  22.8 9.9 %collective-permute-start.1 = (bf16[64,2048]{1,0:T(8,128)(2,1)}, bf16[64,2048]{1,0:T(8,128)(2,1)S(1)}, u32[]{:S(2)}, u32[]{:S(2)}) collective-permute-start(bf16[64,2048]{1,0:T(8,128)(2,1)} %bitcast.5), channel_id=1, source_target_pairs={{0,8},{8,16},{16,24},{24,0},{1,9},{9,17},{17,25},{25,1},{2,10},{10... | collective-permute-start | bytes 786440 | tf_op jit(solution)/shard_map/ppermute | solution.py:302
  32.6 1.8 copy-start.4
  34.5 18.0 %copy-start.10 = (f32[64,256]{1,0:T(8,128)}, f32[64,256]{1,0:T(8,128)S(1)}, u32[]{:S(2)}) copy-start(f32[64,256]{1,0:T(8,128)S(1)} %get-tuple-element.8.select_ref) | copy-start | bytes 196612
  34.5 17.2 %copy-start.17 = (s32[16]{0:T(128)S(1)}, s32[16]{0:T(128)}, u32[]{:S(2)}) copy-start(s32[16]{0:T(128)} %param.16) | copy-start | bytes 196
  34.5 17.3 %copy-start.9 = (bf16[16,16,128]{2,1,0:T(8,128)(2,1)S(1)}, bf16[16,16,128]{2,1,0:T(8,128)(2,1)}, u32[]{:S(2)}) copy-start(bf16[16,16,128]{2,1,0:T(8,128)(2,1)} %queries_ref.1) | copy-start | bytes 196612
  34.5 40.3 %all-to-all-start.1 = ((bf16[32,8,2048]{2,1,0:T(8,128)(2,1)}), bf16[32,8,2048]{2,1,0:T(8,128)(2,1)S(1)}, u32[]{:S(2)}, u32[]{:S(2)}) async-start(bf16[32,8,2048]{2,1,0:T(8,128)(2,1)} %bitcast.40), calls=%async_computation.1 | async-start | bytes 2097152 | tf_op jit(solution)/shard_map/all_to_all | solution.py:272
  48.2 4.5 %copy-start.18 = (bf16[16,128,2,128]{3,2,1,0:T(2,128)(2,1)S(1)}, bf16[16,128,2,128]{3,2,1,0:T(2,128)(2,1)}, u32[]{:S(2)}) copy-start(bf16[16,128,2,128]{3,2,1,0:T(2,128)(2,1)} %param.13) | copy-start | bytes 3145732
  48.2 22.9 %collective-permute-start.4 = (bf16[64,2048]{1,0:T(8,128)(2,1)}, bf16[64,2048]{1,0:T(8,128)(2,1)}, u32[]{:S(2)}, u32[]{:S(2)}) collective-permute-start(bf16[64,2048]{1,0:T(8,128)(2,1)} %bitcast.5), channel_id=1, source_target_pairs={{0,32},{32,0},{1,33},{33,1},{2,34},{34,2},{3,35},{35,3},{4,36},{36... | collective-permute-start | bytes 786440 | tf_op jit(solution)/shard_map/ppermute | solution.py:309
  53.9 6.4 %copy-start.5 = (bf16[64,2048]{1,0:T(8,128)(2,1)S(1)}, bf16[64,2048]{1,0:T(8,128)(2,1)}, u32[]{:S(2)}) copy-start(bf16[64,2048]{1,0:T(8,128)(2,1)} %copy-done.4) | copy-start | bytes 786436
  56.1 8.4 %collective-permute-start.2 = (bf16[32,2048]{1,0:T(8,128)(2,1)S(1)}, bf16[32,2048]{1,0:T(8,128)(2,1)S(1)}, u32[]{:S(2)}, u32[]{:S(2)}) collective-permute-start(bf16[32,2048]{1,0:T(8,128)(2,1)S(1)} %slice.16), channel_id=1, source_target_pairs={{0,24},{8,0},{16,8},{24,16},{1,25},{9,1},{17,9},{25,17},{2,26},{10... | collective-permute-start | bytes 393224 | tf_op jit(solution)/shard_map/ppermute | solution.py:305
  60.4 8.0 %collective-permute-start.3 = (bf16[32,2048]{1,0:T(8,128)(2,1)S(1)}, bf16[32,2048]{1,0:T(8,128)(2,1)S(1)}, u32[]{:S(2)}, u32[]{:S(2)}) collective-permute-start(bf16[32,2048]{1,0:T(8,128)(2,1)S(1)} %slice.17), channel_id=1, source_target_pairs={{0,8},{8,16},{16,24},{24,0},{1,9},{9,17},{17,25},{25,1},{2,10},{10... | collective-permute-start | bytes 393224 | tf_op jit(solution)/shard_map/ppermute | solution.py:305
  84.3 7.8 %copy-start.16 = (f32[16,2,8]{2,1,0:T(2,128)S(1)}, f32[16,2,8]{2,1,0:T(2,128)}, u32[]{:S(2)}) copy-start(f32[16,2,8]{2,1,0:T(2,128)} %copy-done.15) | copy-start | bytes 3076
  84.3 33.4 %all-to-all-start.2 = ((bf16[32,8,2176]{2,1,0:T(8,128)(2,1)}), bf16[32,8,2176]{2,1,0:T(8,128)(2,1)}, u32[]{:S(2)}, u32[]{:S(2)}) async-start(bf16[32,8,2176]{2,1,0:T(8,128)(2,1)} %bitcast.9), calls=%async_computation.2 | async-start | bytes 2228224 | tf_op jit(solution)/shard_map/all_to_all | solution.py:272
  89.8 26.0 %collective-permute-start.5 = (bf16[256,2048]{1,0:T(8,128)(2,1)S(1)}, bf16[256,2048]{1,0:T(8,128)(2,1)}, u32[]{:S(2)}, u32[]{:S(2)}) collective-permute-start(bf16[256,2048]{1,0:T(8,128)(2,1)S(1)} %constant_dynamic-update-slice_fusion.weight_ref.refs_0_), channel_id=1, source_target_pairs={{0,4},{4,0},{1,5},{5,1},{2,6},{6,2},{3,7},{7,3},{8,12},{12,8},{9,1... | collective-permute-start | bytes 3145736 | tf_op jit(solution)/shard_map/ppermute | solution.py:314
  92.2 14.9 %collective-permute-start.6 = (bf16[64,2048]{1,0:T(8,128)(2,1)}, bf16[64,2048]{1,0:T(8,128)(2,1)S(1)}, u32[]{:S(2)}, u32[]{:S(2)}) collective-permute-start(bf16[64,2048]{1,0:T(8,128)(2,1)} %collective-permute-done.4.facing_ref), channel_id=1, source_target_pairs={{0,24},{8,0},{16,8},{24,16},{1,25},{9,1},{17,9},{25,17},{2,26},{10... | collective-permute-start | bytes 786440 | tf_op jit(solution)/shard_map/ppermute | solution.py:302
  96.7 15.5 %collective-permute-start.7 = (bf16[64,2048]{1,0:T(8,128)(2,1)}, bf16[64,2048]{1,0:T(8,128)(2,1)}, u32[]{:S(2)}, u32[]{:S(2)}) collective-permute-start(bf16[64,2048]{1,0:T(8,128)(2,1)} %collective-permute-done.4.facing_ref), channel_id=1, source_target_pairs={{0,8},{8,16},{16,24},{24,0},{1,9},{9,17},{17,25},{25,1},{2,10},{10... | collective-permute-start | bytes 786440 | tf_op jit(solution)/shard_map/ppermute | solution.py:302
  107.7 18.8 %collective-permute-start.8 = (bf16[32,2048]{1,0:T(8,128)(2,1)}, bf16[32,2048]{1,0:T(8,128)(2,1)}, u32[]{:S(2)}, u32[]{:S(2)}) collective-permute-start(bf16[32,2048]{1,0:T(8,128)(2,1)} %slice.18), channel_id=1, source_target_pairs={{0,24},{8,0},{16,8},{24,16},{1,25},{9,1},{17,9},{25,17},{2,26},{10... | collective-permute-start | bytes 393224 | tf_op jit(solution)/shard_map/ppermute | solution.py:305
  113.8 13.6 %collective-permute-start.9 = (bf16[32,2048]{1,0:T(8,128)(2,1)}, bf16[32,2048]{1,0:T(8,128)(2,1)}, u32[]{:S(2)}, u32[]{:S(2)}) collective-permute-start(bf16[32,2048]{1,0:T(8,128)(2,1)} %slice.19), channel_id=1, source_target_pairs={{0,8},{8,16},{16,24},{24,0},{1,9},{9,17},{17,25},{25,1},{2,10},{10... | collective-permute-start | bytes 393224 | tf_op jit(solution)/shard_map/ppermute | solution.py:305
  121.4 18.9 %all-to-all-start.3 = ((bf16[4,16,2176]{2,1,0:T(8,128)(2,1)}), bf16[4,16,2176]{2,1,0:T(8,128)(2,1)}, u32[]{:S(2)}, u32[]{:S(2)}) async-start(bf16[4,16,2176]{2,1,0:T(8,128)(2,1)} %bitcast.38), calls=%async_computation.3 | async-start | bytes 557056 | tf_op jit(solution)/shard_map/all_to_all | solution.py:272
  142.5 29.0 %all-to-all-start.4 = ((bf16[8,16,2048]{2,1,0:T(8,128)(2,1)}), bf16[8,16,2048]{2,1,0:T(8,128)(2,1)}, u32[]{:S(2)}, u32[]{:S(2)}) async-start(bf16[8,16,2048]{2,1,0:T(8,128)(2,1)} %copy-done.3), calls=%async_computation.4 | async-start | bytes 1048576 | tf_op jit(solution)/shard_map/all_to_all | solution.py:272
  151.2 6.5 %collective-permute-start.10 = (bf16[256,2048]{1,0:T(8,128)(2,1)S(1)}, bf16[256,2048]{1,0:T(8,128)(2,1)}, u32[]{:S(2)}, u32[]{:S(2)}) collective-permute-start(bf16[256,2048]{1,0:T(8,128)(2,1)S(1)} %constant_dynamic-update-slice_fusion.5.weight_ref.refs_2_), channel_id=1, source_target_pairs={{0,4},{4,0},{1,5},{5,1},{2,6},{6,2},{3,7},{7,3},{8,12},{12,8},{9,1... | collective-permute-start | bytes 3145736 | tf_op jit(solution)/shard_map/ppermute | solution.py:315
  (11 other events, 9.9 us)

commit v8 on v7

--- a/solution.py
+++ b/solution.py
@@ -83,25 +83,15 @@
     ).astype(jnp.bfloat16)
 
 
-def attend_kernel(q_ref, keys_ref, values_ref, weight_ref, facing_ref, own_ref, out_ref, k_ref, v_ref, sems):
-    copies = []
-    for index in range(4):
-        source, held = ((keys_ref, k_ref), (values_ref, v_ref))[index % 2]
-        group = index // 2
-        copy = pltpu.make_async_copy(
-            source.at[:, pl.ds(group * HD, HD)], held.at[group], sems.at[index]
-        )
-        copy.start()
-        copies.append(copy)
+def attend_kernel(q_ref, k_ref, v_ref, weight_ref, facing_ref, own_ref, out_ref):
     logs = jnp.zeros((SLOTS, 128), jnp.float32)
     lane = lanes((SLOTS, 128))
 
     def scores_of(head):
-        if head % 8 == 0:
-            copies[head // 8 * 2].wait()
+        group = slice((head // 8) * HD, (head // 8 + 1) * HD)
         return lax.dot_general(
             q_ref[:, head * HD : (head + 1) * HD],
-            k_ref[head // 8],
+            k_ref[:, group],
             (((1,), (1,)), ((), ())),
             preferred_element_type=jnp.float32,
         )
@@ -111,14 +101,13 @@
         scores = coming
         if head + 1 < HEADS:
             coming = scores_of(head + 1)
-        if head % 8 == 0:
-            copies[head // 8 * 2 + 1].wait()
+        group = slice((head // 8) * HD, (head // 8 + 1) * HD)
         at = slice(head * HD, (head + 1) * HD)
         top = jnp.max(scores, axis=1, keepdims=True)
         grown = jnp.exp2((scores - top) * (SCALE * LOG2E))
         total = jnp.sum(grown, axis=1, keepdims=True)
         mixed = jnp.dot(
-            grown.astype(jnp.bfloat16), v_ref[head // 8], preferred_element_type=jnp.float32
+            grown.astype(jnp.bfloat16), v_ref[:, group], preferred_element_type=jnp.float32
         )
         out_ref[:, at] = (mixed / total).astype(jnp.bfloat16)
         logs = jnp.where(lane == head, top * SCALE + jnp.log(total), logs)
@@ -186,33 +175,24 @@
 
 def project_kernel(place_ref, rows_ref, *refs):
     sources, out_ref, held, sems = refs[:4], refs[4], refs[5], refs[6]
-    half_rows = YS * 64 // 2
     copies = []
     for piece, source in enumerate(sources):
-        for half in range(2):
-            rows = pl.ds(half * half_rows, half_rows)
-            copy = pltpu.make_async_copy(
-                source.at[rows, :], held.at[piece, rows, :], sems.at[piece * 2 + half]
-            )
-            copy.start()
-            copies.append(copy)
+        copy = pltpu.make_async_copy(source, held.at[piece], sems.at[piece])
+        copy.start()
+        copies.append(copy)
     for piece in range(4):
         far_side, far_core = divmod(piece, CS)
         side = place_ref[0] if far_side == 0 else 1 - place_ref[0]
         core = place_ref[2] if far_core == 0 else 1 - place_ref[2]
-        for half, steps in enumerate(((0, 1), (3, 2))):
-            copies[piece * 2 + half].wait()
-            terms = lax.dot_general(
-                held[piece, half * half_rows : (half + 1) * half_rows, :],
-                rows_ref[...],
-                (((1,), (1,)), ((), ())),
-                preferred_element_type=jnp.float32,
-            ).astype(jnp.bfloat16)
-            for index, step in enumerate(steps):
-                owner = (side * YS + lax.rem(place_ref[1] + step, YS)) * CS + core
-                for part in range(XS):
-                    first = (index * XS + part) * 16
-                    out_ref[owner * XS + part] = terms[first : first + 16, :]
+        copies[piece].wait()
+        terms = lax.dot_general(
+            held[piece], rows_ref[...], (((1,), (1,)), ((), ())), preferred_element_type=jnp.float32
+        ).astype(jnp.bfloat16)
+        for order, step in enumerate((0, 1, 3, 2)):
+            owner = (side * YS + lax.rem(place_ref[1] + step, YS)) * CS + core
+            for part in range(XS):
+                first = (order * XS + part) * 16
+                out_ref[owner * XS + part] = terms[first : first + 16, :]
 
 
 def settle_kernel(terms_ref, out_ref):
@@ -334,15 +314,8 @@
     arrived = exchange(outgoing, quad)
     partials = pl.pallas_call(
         attend_kernel,
-        in_specs=[pl.BlockSpec(memory_space=pltpu.VMEM)]
-        + [pl.BlockSpec(memory_space=pltpu.HBM)] * 2
-        + [pl.BlockSpec(memory_space=pl.ANY)] * 3,
+        in_specs=inputs(3, 3),
         out_shape=packed(SLOTS),
-        scratch_shapes=[
-            pltpu.VMEM((2, TOKENS, HD), jnp.bfloat16),
-            pltpu.VMEM((2, TOKENS, HD), jnp.bfloat16),
-            pltpu.SemaphoreType.DMA((4,)),
-        ],
         compiler_params=PARAMS,
         name="attend",
     )(
@@ -380,7 +353,7 @@
         out_shape=jax.ShapeDtypeStruct((GROUP * XS, 16, ZP * POOL), jnp.bfloat16),
         scratch_shapes=[
             pltpu.VMEM((4, YS * 64, WIDE), jnp.bfloat16),
-            pltpu.SemaphoreType.DMA((8,)),
+            pltpu.SemaphoreType.DMA((4,)),
         ],
         compiler_params=PARAMS,
         name="project",

time: 208 us -> 207 us (level)
  no operation moved by 1% of the time
where the time goes in v8:
time: 207 us; the launch traced here: 206 us
  starting transfers between devices  83.2 us (40%)
  waiting for transfers between devices  56.8 us (27%)
  blocking collectives  29.4 us (14%)
  Pallas kernels  17.3 us (8%)
  local copies, waits for them, and re-layouts  16.2 us (8%)
    all_to_all x5, starting transfers between devices, exchange(): return lax.all_to_all(value, axis, split_axis=0, concat_axis=0, tiled=True)  47.7 us
    all_to_all x5, waiting for transfers between devices, exchange(): return lax.all_to_all(value, axis, split_axis=0, concat_axis=0, tiled=True)  31.4 us
    all_to_all x1, blocking collectives, exchange(): return lax.all_to_all(value, axis, split_axis=0, concat_axis=0, tiled=True)  29.4 us
    ppermute x4, waiting for transfers between devices, beside(): return (lax.ppermute(block, 'y', down), lax.ppermute(block, 'y', up))  14.4 us
    ppermute x4, starting transfers between devices, beside(): return (lax.ppermute(block, 'y', down), lax.ppermute(block, 'y', up))  13 us
    unnamed x47, local copies, waits for them, and re-layouts  11.7 us
    ppermute x2, starting transfers between devices, piece_of(): lax.ppermute(above[:32], 'y', down)  8.8 us
    pallas_call x1, Pallas kernels, on_device(): pl.pallas_call(attend_kernel, in_specs=inputs(3, 3), out_shape=packed(SLO...  6.78 us
  transfers between devices with their start and end apart: 16, of which 11 were waited for; matrix products, arithmetic and copies ran while one was open for 5% of the time, Pallas kernels for 1%

profile of v8, /device:TPU:1, one launch (start us, length us, event | category | flops | bytes accessed | tf_op | source)
XLA Modules:
  0.0 205.6 jit_solution(6610683496411472358)
XLA Ops:
  2.5 15.6 %all-to-all-start = ((bf16[4,16,2176]{2,1,0:T(8,128)(2,1)}), bf16[4,16,2176]{2,1,0:T(8,128)(2,1)S(1)}, u32[]{:S(2)}, u32[]{:S(2)}) async-start(bf16[4,16,2176]{2,1,0:T(8,128)(2,1)} %prepare.1), calls=%async_computation | async-start | bytes 557056 | tf_op jit(solution)/shard_map/all_to_all | solution.py:252
  18.1 4.6 %collective-permute-start = (bf16[64,2048]{1,0:T(8,128)(2,1)}, bf16[64,2048]{1,0:T(8,128)(2,1)S(1)}, u32[]{:S(2)}, u32[]{:S(2)}) collective-permute-start(bf16[64,2048]{1,0:T(8,128)(2,1)} %bitcast.5), channel_id=1, source_target_pairs={{0,24},{8,0},{16,8},{24,16},{1,25},{9,1},{17,9},{25,17},{2,26},{10... | collective-permute-start | bytes 786440 | tf_op jit(solution)/shard_map/ppermute | solution.py:282
  25.6 2.1 %collective-permute-done.above_ref = bf16[64,2048]{1,0:T(8,128)(2,1)S(1)} collective-permute-done((bf16[64,2048]{1,0:T(8,128)(2,1)}, bf16[64,2048]{1,0:T(8,128)(2,1)S(1)}, u32[]{:S(2)}, u32[]{:S(2)}) %collective-permute-start) | collective-permute-done | bytes 262176 | tf_op jit(solution)/shard_map/ppermute | solution.py:282
  27.7 4.9 %collective-permute-done.1.below_ref = bf16[64,2048]{1,0:T(8,128)(2,1)S(1)} collective-permute-done((bf16[64,2048]{1,0:T(8,128)(2,1)}, bf16[64,2048]{1,0:T(8,128)(2,1)S(1)}, u32[]{:S(2)}, u32[]{:S(2)}) %collective-permute-start.1) | collective-permute-done | bytes 262176 | tf_op jit(solution)/shard_map/ppermute | solution.py:282
  34.5 13.7 %all-to-all-start.1 = ((bf16[32,8,2048]{2,1,0:T(8,128)(2,1)}), bf16[32,8,2048]{2,1,0:T(8,128)(2,1)S(1)}, u32[]{:S(2)}, u32[]{:S(2)}) async-start(bf16[32,8,2048]{2,1,0:T(8,128)(2,1)} %bitcast.40), calls=%async_computation.1 | async-start | bytes 2097152 | tf_op jit(solution)/shard_map/all_to_all | solution.py:252
  48.2 3.4 %collective-permute-start.4 = (bf16[64,2048]{1,0:T(8,128)(2,1)}, bf16[64,2048]{1,0:T(8,128)(2,1)}, u32[]{:S(2)}, u32[]{:S(2)}) collective-permute-start(bf16[64,2048]{1,0:T(8,128)(2,1)} %bitcast.5), channel_id=1, source_target_pairs={{0,32},{32,0},{1,33},{33,1},{2,34},{34,2},{3,35},{35,3},{4,36},{36... | collective-permute-start | bytes 786440 | tf_op jit(solution)/shard_map/ppermute | solution.py:289
  56.1 4.3 %collective-permute-start.2 = (bf16[32,2048]{1,0:T(8,128)(2,1)S(1)}, bf16[32,2048]{1,0:T(8,128)(2,1)S(1)}, u32[]{:S(2)}, u32[]{:S(2)}) collective-permute-start(bf16[32,2048]{1,0:T(8,128)(2,1)S(1)} %slice.16), channel_id=1, source_target_pairs={{0,24},{8,0},{16,8},{24,16},{1,25},{9,1},{17,9},{25,17},{2,26},{10... | collective-permute-start | bytes 393224 | tf_op jit(solution)/shard_map/ppermute | solution.py:285
  64.5 3.9 %collective-permute-done.3 = bf16[32,2048]{1,0:T(8,128)(2,1)S(1)} collective-permute-done((bf16[32,2048]{1,0:T(8,128)(2,1)S(1)}, bf16[32,2048]{1,0:T(8,128)(2,1)S(1)}, u32[]{:S(2)}, u32[]{:S(2)}) %collective-permute-start.3) | collective-permute-done | bytes 131104 | tf_op jit(solution)/shard_map/ppermute | solution.py:285
  68.4 2.8 %collective-permute-done.4.facing_ref = bf16[64,2048]{1,0:T(8,128)(2,1)} collective-permute-done((bf16[64,2048]{1,0:T(8,128)(2,1)}, bf16[64,2048]{1,0:T(8,128)(2,1)}, u32[]{:S(2)}, u32[]{:S(2)}) %collective-permute-start.4) | collective-permute-done | bytes 262176 | tf_op jit(solution)/shard_map/ppermute | solution.py:289
  71.1 3.6 %all-to-all-done.1 = bf16[32,8,2048]{2,1,0:T(8,128)(2,1)S(1)} async-done(((bf16[32,8,2048]{2,1,0:T(8,128)(2,1)}), bf16[32,8,2048]{2,1,0:T(8,128)(2,1)S(1)}, u32[]{:S(2)}, u32[]{:S(2)}) %all-to-all-start.1) | async-done | bytes 1048608 | tf_op jit(solution)/shard_map/all_to_all | solution.py:252
  76.9 6.8 %attend.1 = bf16[256,2176]{1,0:T(8,128)(2,1)} custom-call(bf16[256,2048]{1,0:T(8,128)(2,1)S(1)} %bitcast.35, bf16[1024,256]{1,0:T(8,128)(2,1)S(1)} %copy-done.2, bf16[1024,256]{1,0:T(8,128)(2,1)S(1)} %copy-done.1, bf16[256,2048]{1,0:T(8,128)(2,1)S(1)} %constant_dynamic-update-slice_fusion.weight_ref.refs_0_, ...), custom_call_target="tpu_custom_call" | custom-call | tf_op jit(solution)/shard_map/attend/pallas_call | solution.py:315
  83.7 5.6 %all-to-all-start.2 = ((bf16[32,8,2176]{2,1,0:T(8,128)(2,1)}), bf16[32,8,2176]{2,1,0:T(8,128)(2,1)}, u32[]{:S(2)}, u32[]{:S(2)}) async-start(bf16[32,8,2176]{2,1,0:T(8,128)(2,1)} %bitcast.9), calls=%async_computation.2 | async-start | bytes 2228224 | tf_op jit(solution)/shard_map/all_to_all | solution.py:252
  89.2 2.2 %collective-permute-start.5 = (bf16[256,2048]{1,0:T(8,128)(2,1)S(1)}, bf16[256,2048]{1,0:T(8,128)(2,1)}, u32[]{:S(2)}, u32[]{:S(2)}) collective-permute-start(bf16[256,2048]{1,0:T(8,128)(2,1)S(1)} %constant_dynamic-update-slice_fusion.weight_ref.refs_0_), channel_id=1, source_target_pairs={{0,4},{4,0},{1,5},{5,1},{2,6},{6,2},{3,7},{7,3},{8,12},{12,8},{9,1... | collective-permute-start | bytes 3145736 | tf_op jit(solution)/shard_map/ppermute | solution.py:294
  91.6 4.6 %collective-permute-start.6 = (bf16[64,2048]{1,0:T(8,128)(2,1)}, bf16[64,2048]{1,0:T(8,128)(2,1)S(1)}, u32[]{:S(2)}, u32[]{:S(2)}) collective-permute-start(bf16[64,2048]{1,0:T(8,128)(2,1)} %collective-permute-done.4.facing_ref), channel_id=1, source_target_pairs={{0,24},{8,0},{16,8},{24,16},{1,25},{9,1},{17,9},{25,17},{2,26},{10... | collective-permute-start | bytes 786440 | tf_op jit(solution)/shard_map/ppermute | solution.py:282
  99.2 7.4 %collective-permute-done.6.above_ref = bf16[64,2048]{1,0:T(8,128)(2,1)S(1)} collective-permute-done((bf16[64,2048]{1,0:T(8,128)(2,1)}, bf16[64,2048]{1,0:T(8,128)(2,1)S(1)}, u32[]{:S(2)}, u32[]{:S(2)}) %collective-permute-start.6) | collective-permute-done | bytes 262176 | tf_op jit(solution)/shard_map/ppermute | solution.py:282
  107.2 4.5 %collective-permute-start.8 = (bf16[32,2048]{1,0:T(8,128)(2,1)}, bf16[32,2048]{1,0:T(8,128)(2,1)}, u32[]{:S(2)}, u32[]{:S(2)}) collective-permute-start(bf16[32,2048]{1,0:T(8,128)(2,1)} %slice.18), channel_id=1, source_target_pairs={{0,24},{8,0},{16,8},{24,16},{1,25},{9,1},{17,9},{25,17},{2,26},{10... | collective-permute-start | bytes 393224 | tf_op jit(solution)/shard_map/ppermute | solution.py:285
  118.0 2.2 %gather.1 = bf16[64,2176]{1,0:T(8,128)(2,1)S(1)} custom-call(bf16[256,2176]{1,0:T(8,128)(2,1)} %bitcast.10.back_ref, f32[64,256]{1,0:T(8,128)S(1)} %copy-done.11, bf16[256,2048]{1,0:T(8,128)(2,1)} %collective-permute-done.5.weight_ref.refs_1_, bf16[64,2048]{1,0:T(8,128)(2,1)S(1)} %collective-permute-done.6.above_ref, ...), custom_call_target="tpu_custom_call" | custom-call | tf_op jit(solution)/shard_map/gather/pallas_call | solution.py:330
  120.9 4.1 %all-to-all-start.3 = ((bf16[4,16,2176]{2,1,0:T(8,128)(2,1)}), bf16[4,16,2176]{2,1,0:T(8,128)(2,1)}, u32[]{:S(2)}, u32[]{:S(2)}) async-start(bf16[4,16,2176]{2,1,0:T(8,128)(2,1)} %bitcast.38), calls=%async_computation.3 | async-start | bytes 557056 | tf_op jit(solution)/shard_map/all_to_all | solution.py:252
  127.8 12.0 %all-to-all-done.3 = bf16[4,16,2176]{2,1,0:T(8,128)(2,1)} async-done(((bf16[4,16,2176]{2,1,0:T(8,128)(2,1)}), bf16[4,16,2176]{2,1,0:T(8,128)(2,1)}, u32[]{:S(2)}, u32[]{:S(2)}) %all-to-all-start.3) | async-done | bytes 278560 | tf_op jit(solution)/shard_map/all_to_all | solution.py:252
  141.9 8.7 %all-to-all-start.4 = ((bf16[8,16,2048]{2,1,0:T(8,128)(2,1)}), bf16[8,16,2048]{2,1,0:T(8,128)(2,1)}, u32[]{:S(2)}, u32[]{:S(2)}) async-start(bf16[8,16,2048]{2,1,0:T(8,128)(2,1)} %copy-done.3), calls=%async_computation.4 | async-start | bytes 1048576 | tf_op jit(solution)/shard_map/all_to_all | solution.py:252
  150.6 4.2 %collective-permute-start.10 = (bf16[256,2048]{1,0:T(8,128)(2,1)S(1)}, bf16[256,2048]{1,0:T(8,128)(2,1)}, u32[]{:S(2)}, u32[]{:S(2)}) collective-permute-start(bf16[256,2048]{1,0:T(8,128)(2,1)S(1)} %constant_dynamic-update-slice_fusion.5.weight_ref.refs_2_), channel_id=1, source_target_pairs={{0,4},{4,0},{1,5},{5,1},{2,6},{6,2},{3,7},{7,3},{8,12},{12,8},{9,1... | collective-permute-start | bytes 3145736 | tf_op jit(solution)/shard_map/ppermute | solution.py:295
  157.1 13.9 %all-to-all-done.4 = bf16[8,16,2048]{2,1,0:T(8,128)(2,1)} async-done(((bf16[8,16,2048]{2,1,0:T(8,128)(2,1)}), bf16[8,16,2048]{2,1,0:T(8,128)(2,1)}, u32[]{:S(2)}, u32[]{:S(2)}) %all-to-all-start.4) | async-done | bytes 524320 | tf_op jit(solution)/shard_map/all_to_all | solution.py:252
  171.0 4.4 %project.1 = bf16[64,16,128]{2,1,0:T(8,128)(2,1)S(1)} custom-call(s32[3]{0:T(128)S(1)} %pad_add_fusion.place_ref, bf16[128,2048]{1,0:T(8,128)(2,1)} %bitcast.14.rows_ref, bf16[256,2048]{1,0:T(8,128)(2,1)S(1)} %constant_dynamic-update-slice_fusion.weight_ref.refs_0_, bf16[256,2048]{1,0:T(8,128)(2,1)} %collective-permute-done.5.weight_ref.refs_1_, ...), custom_call_target="tpu_custom_call" | custom-call | tf_op jit(solution)/shard_map/project/pallas_call | solution.py:349
  175.4 29.4 %all_to_all.48.terms_ref = bf16[64,16,128]{2,1,0:T(8,128)(2,1)S(1)} all-to-all(bf16[64,16,128]{2,1,0:T(8,128)(2,1)S(1)} %project.1), channel_id=1, replica_groups=mesh['zh'=4,'zp'=2,'zq'=2,'y'=4,'c'=2,'kv'=4] {'zq','y','c','kv'}, dimensions={0} | all-to-all | bytes 524288 | tf_op jit(solution)/shard_map/all_to_all | solution.py:252
  (85 shorter events, 36.3 us)
Async XLA Ops:
  0.0 51.7 %copy-start = (bf16[16,128,2,128]{3,2,1,0:T(2,128)(2,1)S(1)}, bf16[16,128,2,128]{3,2,1,0:T(2,128)(2,1)}, u32[]{:S(2)}) copy-start(bf16[16,128,2,128]{3,2,1,0:T(2,128)(2,1)} %param.12) | copy-start | bytes 3145732
  2.5 30.2 %all-to-all-start = ((bf16[4,16,2176]{2,1,0:T(8,128)(2,1)}), bf16[4,16,2176]{2,1,0:T(8,128)(2,1)S(1)}, u32[]{:S(2)}, u32[]{:S(2)}) async-start(bf16[4,16,2176]{2,1,0:T(8,128)(2,1)} %prepare.1), calls=%async_computation | async-start | bytes 557056 | tf_op jit(solution)/shard_map/all_to_all | solution.py:252
  18.1 9.6 %collective-permute-start = (bf16[64,2048]{1,0:T(8,128)(2,1)}, bf16[64,2048]{1,0:T(8,128)(2,1)S(1)}, u32[]{:S(2)}, u32[]{:S(2)}) collective-permute-start(bf16[64,2048]{1,0:T(8,128)(2,1)} %bitcast.5), channel_id=1, source_target_pairs={{0,24},{8,0},{16,8},{24,16},{1,25},{9,1},{17,9},{25,17},{2,26},{10... | collective-permute-start | bytes 786440 | tf_op jit(solution)/shard_map/ppermute | solution.py:282
  22.8 9.9 %collective-permute-start.1 = (bf16[64,2048]{1,0:T(8,128)(2,1)}, bf16[64,2048]{1,0:T(8,128)(2,1)S(1)}, u32[]{:S(2)}, u32[]{:S(2)}) collective-permute-start(bf16[64,2048]{1,0:T(8,128)(2,1)} %bitcast.5), channel_id=1, source_target_pairs={{0,8},{8,16},{16,24},{24,0},{1,9},{9,17},{17,25},{25,1},{2,10},{10... | collective-permute-start | bytes 786440 | tf_op jit(solution)/shard_map/ppermute | solution.py:282
  32.6 1.8 copy-start.4
  34.5 18.0 %copy-start.10 = (f32[64,256]{1,0:T(8,128)}, f32[64,256]{1,0:T(8,128)S(1)}, u32[]{:S(2)}) copy-start(f32[64,256]{1,0:T(8,128)S(1)} %get-tuple-element.8.select_ref) | copy-start | bytes 196612
  34.5 17.2 %copy-start.17 = (s32[16]{0:T(128)S(1)}, s32[16]{0:T(128)}, u32[]{:S(2)}) copy-start(s32[16]{0:T(128)} %param.16) | copy-start | bytes 196
  34.5 17.3 %copy-start.9 = (bf16[16,16,128]{2,1,0:T(8,128)(2,1)S(1)}, bf16[16,16,128]{2,1,0:T(8,128)(2,1)}, u32[]{:S(2)}) copy-start(bf16[16,16,128]{2,1,0:T(8,128)(2,1)} %queries_ref.1) | copy-start | bytes 196612
  34.5 40.3 %all-to-all-start.1 = ((bf16[32,8,2048]{2,1,0:T(8,128)(2,1)}), bf16[32,8,2048]{2,1,0:T(8,128)(2,1)S(1)}, u32[]{:S(2)}, u32[]{:S(2)}) async-start(bf16[32,8,2048]{2,1,0:T(8,128)(2,1)} %bitcast.40), calls=%async_computation.1 | async-start | bytes 2097152 | tf_op jit(solution)/shard_map/all_to_all | solution.py:252
  48.2 4.5 %copy-start.18 = (bf16[16,128,2,128]{3,2,1,0:T(2,128)(2,1)S(1)}, bf16[16,128,2,128]{3,2,1,0:T(2,128)(2,1)}, u32[]{:S(2)}) copy-start(bf16[16,128,2,128]{3,2,1,0:T(2,128)(2,1)} %param.13) | copy-start | bytes 3145732
  48.2 22.9 %collective-permute-start.4 = (bf16[64,2048]{1,0:T(8,128)(2,1)}, bf16[64,2048]{1,0:T(8,128)(2,1)}, u32[]{:S(2)}, u32[]{:S(2)}) collective-permute-start(bf16[64,2048]{1,0:T(8,128)(2,1)} %bitcast.5), channel_id=1, source_target_pairs={{0,32},{32,0},{1,33},{33,1},{2,34},{34,2},{3,35},{35,3},{4,36},{36... | collective-permute-start | bytes 786440 | tf_op jit(solution)/shard_map/ppermute | solution.py:289
  53.9 6.4 %copy-start.5 = (bf16[64,2048]{1,0:T(8,128)(2,1)S(1)}, bf16[64,2048]{1,0:T(8,128)(2,1)}, u32[]{:S(2)}) copy-start(bf16[64,2048]{1,0:T(8,128)(2,1)} %copy-done.4) | copy-start | bytes 786436
  56.1 8.4 %collective-permute-start.2 = (bf16[32,2048]{1,0:T(8,128)(2,1)S(1)}, bf16[32,2048]{1,0:T(8,128)(2,1)S(1)}, u32[]{:S(2)}, u32[]{:S(2)}) collective-permute-start(bf16[32,2048]{1,0:T(8,128)(2,1)S(1)} %slice.16), channel_id=1, source_target_pairs={{0,24},{8,0},{16,8},{24,16},{1,25},{9,1},{17,9},{25,17},{2,26},{10... | collective-permute-start | bytes 393224 | tf_op jit(solution)/shard_map/ppermute | solution.py:285
  60.4 8.0 %collective-permute-start.3 = (bf16[32,2048]{1,0:T(8,128)(2,1)S(1)}, bf16[32,2048]{1,0:T(8,128)(2,1)S(1)}, u32[]{:S(2)}, u32[]{:S(2)}) collective-permute-start(bf16[32,2048]{1,0:T(8,128)(2,1)S(1)} %slice.17), channel_id=1, source_target_pairs={{0,8},{8,16},{16,24},{24,0},{1,9},{9,17},{17,25},{25,1},{2,10},{10... | collective-permute-start | bytes 393224 | tf_op jit(solution)/shard_map/ppermute | solution.py:285
  83.7 7.9 %copy-start.16 = (f32[16,2,8]{2,1,0:T(2,128)S(1)}, f32[16,2,8]{2,1,0:T(2,128)}, u32[]{:S(2)}) copy-start(f32[16,2,8]{2,1,0:T(2,128)} %copy-done.15) | copy-start | bytes 3076
  83.7 33.5 %all-to-all-start.2 = ((bf16[32,8,2176]{2,1,0:T(8,128)(2,1)}), bf16[32,8,2176]{2,1,0:T(8,128)(2,1)}, u32[]{:S(2)}, u32[]{:S(2)}) async-start(bf16[32,8,2176]{2,1,0:T(8,128)(2,1)} %bitcast.9), calls=%async_computation.2 | async-start | bytes 2228224 | tf_op jit(solution)/shard_map/all_to_all | solution.py:252
  89.2 26.0 %collective-permute-start.5 = (bf16[256,2048]{1,0:T(8,128)(2,1)S(1)}, bf16[256,2048]{1,0:T(8,128)(2,1)}, u32[]{:S(2)}, u32[]{:S(2)}) collective-permute-start(bf16[256,2048]{1,0:T(8,128)(2,1)S(1)} %constant_dynamic-update-slice_fusion.weight_ref.refs_0_), channel_id=1, source_target_pairs={{0,4},{4,0},{1,5},{5,1},{2,6},{6,2},{3,7},{7,3},{8,12},{12,8},{9,1... | collective-permute-start | bytes 3145736 | tf_op jit(solution)/shard_map/ppermute | solution.py:294
  91.6 14.9 %collective-permute-start.6 = (bf16[64,2048]{1,0:T(8,128)(2,1)}, bf16[64,2048]{1,0:T(8,128)(2,1)S(1)}, u32[]{:S(2)}, u32[]{:S(2)}) collective-permute-start(bf16[64,2048]{1,0:T(8,128)(2,1)} %collective-permute-done.4.facing_ref), channel_id=1, source_target_pairs={{0,24},{8,0},{16,8},{24,16},{1,25},{9,1},{17,9},{25,17},{2,26},{10... | collective-permute-start | bytes 786440 | tf_op jit(solution)/shard_map/ppermute | solution.py:282
  96.2 15.5 %collective-permute-start.7 = (bf16[64,2048]{1,0:T(8,128)(2,1)}, bf16[64,2048]{1,0:T(8,128)(2,1)}, u32[]{:S(2)}, u32[]{:S(2)}) collective-permute-start(bf16[64,2048]{1,0:T(8,128)(2,1)} %collective-permute-done.4.facing_ref), channel_id=1, source_target_pairs={{0,8},{8,16},{16,24},{24,0},{1,9},{9,17},{17,25},{25,1},{2,10},{10... | collective-permute-start | bytes 786440 | tf_op jit(solution)/shard_map/ppermute | solution.py:282
  107.2 18.8 %collective-permute-start.8 = (bf16[32,2048]{1,0:T(8,128)(2,1)}, bf16[32,2048]{1,0:T(8,128)(2,1)}, u32[]{:S(2)}, u32[]{:S(2)}) collective-permute-start(bf16[32,2048]{1,0:T(8,128)(2,1)} %slice.18), channel_id=1, source_target_pairs={{0,24},{8,0},{16,8},{24,16},{1,25},{9,1},{17,9},{25,17},{2,26},{10... | collective-permute-start | bytes 393224 | tf_op jit(solution)/shard_map/ppermute | solution.py:285
  113.3 13.6 %collective-permute-start.9 = (bf16[32,2048]{1,0:T(8,128)(2,1)}, bf16[32,2048]{1,0:T(8,128)(2,1)}, u32[]{:S(2)}, u32[]{:S(2)}) collective-permute-start(bf16[32,2048]{1,0:T(8,128)(2,1)} %slice.19), channel_id=1, source_target_pairs={{0,8},{8,16},{16,24},{24,0},{1,9},{9,17},{17,25},{25,1},{2,10},{10... | collective-permute-start | bytes 393224 | tf_op jit(solution)/shard_map/ppermute | solution.py:285
  120.9 18.9 %all-to-all-start.3 = ((bf16[4,16,2176]{2,1,0:T(8,128)(2,1)}), bf16[4,16,2176]{2,1,0:T(8,128)(2,1)}, u32[]{:S(2)}, u32[]{:S(2)}) async-start(bf16[4,16,2176]{2,1,0:T(8,128)(2,1)} %bitcast.38), calls=%async_computation.3 | async-start | bytes 557056 | tf_op jit(solution)/shard_map/all_to_all | solution.py:252
  141.9 29.0 %all-to-all-start.4 = ((bf16[8,16,2048]{2,1,0:T(8,128)(2,1)}), bf16[8,16,2048]{2,1,0:T(8,128)(2,1)}, u32[]{:S(2)}, u32[]{:S(2)}) async-start(bf16[8,16,2048]{2,1,0:T(8,128)(2,1)} %copy-done.3), calls=%async_computation.4 | async-start | bytes 1048576 | tf_op jit(solution)/shard_map/all_to_all | solution.py:252
  150.6 6.5 %collective-permute-start.10 = (bf16[256,2048]{1,0:T(8,128)(2,1)S(1)}, bf16[256,2048]{1,0:T(8,128)(2,1)}, u32[]{:S(2)}, u32[]{:S(2)}) collective-permute-start(bf16[256,2048]{1,0:T(8,128)(2,1)S(1)} %constant_dynamic-update-slice_fusion.5.weight_ref.refs_2_), channel_id=1, source_target_pairs={{0,4},{4,0},{1,5},{5,1},{2,6},{6,2},{3,7},{7,3},{8,12},{12,8},{9,1... | collective-permute-start | bytes 3145736 | tf_op jit(solution)/shard_map/ppermute | solution.py:295
  (11 other events, 9.9 us)
